TPU v7x, 32 devices: a whole 2x2x4 slice. The times are simulated.
32 devices in a mesh: dom: 16 (over z, y, x), feat: 2 (over core).
Axes of the slice: x: 2, y: 2, z: 4, core: 2. Of those that a mesh axis runs over, the one named last changes fastest.
Arguments:
- history: bfloat16 [16384, 256], P('dom', 'feat'), may hold values from -6 to 6
- pull_list: int32 [16, 16, 2], P('dom'), may hold values from -1 to 7, as said below
- remote_tiles: bfloat16 [16, 16, 2, 128, 128], P('dom'), may hold values from -0.1875 to 0.1875
- remote_dst: int32 [16, 16, 2], P('dom'), may hold values from 0 to 15
- local_tiles: bfloat16 [1024, 128, 128], P('dom'), may hold values from -0.1875 to 0.1875
- local_src: int32 [16, 64], P('dom'), may hold values from 0 to 7
- local_dst: int32 [16, 64], P('dom'), may hold values from 0 to 15
- weight: bfloat16 [256, 256], P(None, 'feat'), may hold values from -0.375 to 0.375
- bias: float32 [256], P('feat'), may hold values from -3 to 3
- cotangent: bfloat16 [16384, 256], P('dom', 'feat'), may hold values from -0.046875 to 0.046875
Outputs:
- new_rows: bfloat16 [16384, 256], P('dom', 'feat')
- grad_weight: float32 [256, 256], P(None, 'feat')
- grad_bias: float32 [256], P('feat')
Inputs may be any that keep to these rules, and one draw needn't show every extreme that they name: pull_list[r, o, c] is -1 or a block index local to owner o; in each (r, o) the used entries come first and are distinct; pull_list[r, r] is all -1; every other (r, o) asks 2 or 1 blocks; every partition asks 2 blocks of the next partition, and some owner is asked for 2 blocks by every other partition.
All inputs are finite; a program needn't handle non-finite values.
Results may differ from a plain program's by a relative error of at most 0.0065.
Values may be sent and summed in bfloat16 or wider, within the bound.
No kernel may reach another device: no remote copies, remote signals or barrier semaphores. Data moves between devices by JAX's collectives and lax.ppermute only.
A program may use at most 128 MiB of HBM per device.

v0:
```python
import jax
import jax.numpy as jnp
from jax import lax
from jax.sharding import PartitionSpec as P


def passed_along(block, axis, distance):
    devices = range(lax.axis_size(axis))
    route = [((i - distance) % len(devices), i) for i in devices]
    return lax.ppermute(block, axis, route)


def activate(value):
    return jax.nn.gelu(value, approximate=True)


def select_rows(targets, row_count, values):
    one_hot = (
        targets.reshape(-1)[None, :] == jnp.arange(row_count, dtype=jnp.int32)[:, None]
    ).astype(jnp.float32)
    return jnp.dot(one_hot, values, precision=lax.Precision.HIGHEST)


def per_device(
    history,
    pull_list,
    remote_tiles,
    remote_dst,
    local_tiles,
    local_src,
    local_dst,
    weight,
    bias,
    cotangent,
):
    half_width = history.shape[1]
    block_size = local_tiles.shape[1]
    own_blocks = history.shape[0] // block_size
    row_count = 2 * own_blocks
    blocks = history.reshape(own_blocks, block_size, half_width)
    requested = pull_list[0]
    asked = lax.all_to_all(requested, "dom", split_axis=0, concat_axis=0, tiled=True)
    clamped = jnp.clip(asked, 0, own_blocks - 1)
    picked = blocks[clamped]
    pulled = lax.all_to_all(
        jnp.where((asked >= 0)[:, :, None, None], picked, jnp.zeros((), history.dtype)),
        "dom",
        split_axis=0,
        concat_axis=0,
        tiled=True,
    )
    sources = blocks[local_src[0]]
    local_prod = jnp.einsum(
        "kij,kjf->kif", local_tiles, sources, preferred_element_type=jnp.float32
    )
    partial_value = select_rows(
        local_dst[0], row_count, local_prod.reshape(-1, block_size * half_width)
    )
    products = jnp.einsum(
        "ockj,ocjf->ockf", remote_tiles[0], pulled, preferred_element_type=jnp.float32
    )
    partial_value = partial_value + select_rows(
        remote_dst[0], row_count, products.reshape(-1, block_size * half_width)
    )
    incoming = passed_along(partial_value[own_blocks:], "dom", 1)
    aggregate = (
        (partial_value[:own_blocks] + incoming)
        .reshape(own_blocks * block_size, half_width)
        .astype(jnp.bfloat16)
    )
    aggregate_full = lax.all_gather(aggregate, "feat", axis=1, tiled=True)
    preact = jnp.dot(aggregate_full, weight, preferred_element_type=jnp.float32) + bias
    new_rows, backward_fn = jax.vjp(activate, preact)
    grad_pre = backward_fn(cotangent.astype(jnp.float32))[0].astype(jnp.bfloat16)
    weight_term = lax.dot_general(
        aggregate_full, grad_pre, (((0,), (0,)), ((), ())), preferred_element_type=jnp.float32
    )
    bias_term = jnp.sum(grad_pre.astype(jnp.float32), axis=0)
    grad_weight, grad_bias = lax.psum((weight_term, bias_term), "dom")
    return (new_rows.astype(jnp.bfloat16), grad_weight, grad_bias)


def solution(mesh):
    placed = (
        P("dom", "feat"),
        P("dom", None, None),
        P("dom", None, None, None, None),
        P("dom", None, None),
        P("dom", None, None),
        P("dom", None),
        P("dom", None),
        P(None, "feat"),
        P("feat"),
        P("dom", "feat"),
    )
    return jax.shard_map(
        per_device,
        mesh=mesh,
        in_specs=placed,
        out_specs=(P("dom", "feat"), P(None, "feat"), P("feat")),
        check_vma=False,
    )
```

profile of v0, /device:TPU:0, one launch (start us, length us, event | category | flops | bytes accessed | tf_op | source)
XLA Modules:
  0.0 197.8 jit_solution(7915041659661262824)
XLA Ops:
  7.2 0.9 copy.36
  8.1 15.4 %all_to_all.14 = s32[16,1,2]{2,1,0:T(1,128)S(1)} all-to-all(s32[16,1,2]{2,1,0:T(1,128)S(1)} %copy.36), channel_id=1, replica_groups=mesh['dom'=16,'feat'=2] {'dom'}, dimensions={0} | all-to-all | bytes 256 | tf_op jit(solution)/shard_map/all_to_all | solution.py:42
  23.7 2.6 %gather_fusion.1 = bf16[32,128,128]{2,1,0:T(8,128)(2,1)} fusion(bf16[8,128,128]{2,1,0:T(8,128)(2,1)} %bitcast.37, s32[1024]{0:T(1024)S(1)} %pad_clamp_fusion), kind=kCustom, calls=%fused_computation.1 | custom fusion | bytes 2097280 | tf_op jit(solution)/shard_map/gather | solution.py:44
  26.3 1.6 copy.41
  28.0 0.1 copy.38
  28.1 1.1 broadcast_select_fusion
  29.2 4.3 %all-to-all-start.1 = ((bf16[16,2,128,128]{2,3,1,0:T(8,128)(2,1)}), bf16[16,2,128,128]{2,3,1,0:T(8,128)(2,1)}, u32[]{:S(2)}, u32[]{:S(2)}) async-start(bf16[16,2,128,128]{2,3,1,0:T(8,128)(2,1)} %broadcast_select_fusion), calls=%async_computation.1 | async-start | bytes 2097152 | tf_op jit(solution)/shard_map/all_to_all | solution.py:45
  33.6 2.1 %gather_fusion = bf16[64,128,128]{2,1,0:T(8,128)(2,1)} fusion(bf16[8,128,128]{2,1,0:T(8,128)(2,1)S(1)} %bitcast.38, s32[1024]{0:T(1024)S(1)} %pad_clamp_fusion.1), kind=kCustom, calls=%fused_computation | custom fusion | bytes 4194560 | tf_op jit(solution)/shard_map/gather | solution.py:52
  35.8 5.1 %convolution_bitcast_fusion = f32[64,128,128]{1,2,0:T(8,128)} fusion(bf16[64,128,128]{2,1,0:T(8,128)(2,1)} %gather_fusion, bf16[64,128,128]{2,1,0:T(8,128)(2,1)S(1)} %copy-done), kind=kOutput, calls=%fused_computation.6 | convolution fusion | flops 268435456 | bytes 8388608 | tf_op jit(solution)/shard_map/kij,kjf->kif/dot_general | solution.py:53
  40.9 5.7 %copy.34 = f32[64,128,128]{2,1,0:T(8,128)} copy(f32[64,128,128]{1,2,0:T(8,128)} %convolution_bitcast_fusion) | data formatting | bytes 8388608 | tf_op jit(solution)/shard_map/kij,kjf->kif/dot_general | solution.py:53
  46.8 5.8 %fusion = f32[16,16384]{1,0:T(8,128)S(1)} fusion(f32[8,8,128,128]{3,2,1,0:T(8,128)} %bitcast.39, s32[64]{0:T(128)S(1)} %bitcast.43), kind=kOutput, calls=%fused_computation.3 | convolution fusion | flops 201327616 | bytes 5243136 | tf_op jit(solution)/shard_map/dot_general | solution.py:21
  52.5 4.3 %all-to-all-done.1 = bf16[16,2,128,128]{2,3,1,0:T(8,128)(2,1)} async-done(((bf16[16,2,128,128]{2,3,1,0:T(8,128)(2,1)}), bf16[16,2,128,128]{2,3,1,0:T(8,128)(2,1)}, u32[]{:S(2)}, u32[]{:S(2)}) %all-to-all-start.1) | async-done | bytes 1048608 | tf_op jit(solution)/shard_map/all_to_all | solution.py:45
  56.8 3.7 %convolution_bitcast_fusion.1 = f32[16,2,128,128]{2,3,1,0:T(8,128)} fusion(bf16[16,2,128,128]{2,3,1,0:T(8,128)(2,1)} %all-to-all-done.1, bf16[1,16,2,128,128]{4,3,2,1,0:T(8,128)(2,1)} %param.12), kind=kOutput, calls=%fused_computation.9 | convolution fusion | flops 134217728 | bytes 4194304 | tf_op jit(solution)/shard_map/ockj,ocjf->ockf/dot_general | solution.py:59
  60.6 2.9 %copy.42 = f32[16,2,128,128]{3,2,1,0:T(8,128)} copy(f32[16,2,128,128]{2,3,1,0:T(8,128)} %convolution_bitcast_fusion.1) | data formatting | bytes 4194304 | tf_op jit(solution)/shard_map/ockj,ocjf->ockf/dot_general | solution.py:59
  63.5 3.5 %convolution_add_fusion = f32[16,16384]{1,0:T(8,128)S(1)} fusion(f32[16,16384]{1,0:T(8,128)S(1)} %fusion, f32[4,8,128,128]{3,2,1,0:T(8,128)} %bitcast.40, s32[32]{0:T(128)S(1)} %eq.34), kind=kOutput, calls=%fused_computation.2 | convolution fusion | flops 100925952 | bytes 4194432 | tf_op jit(solution)/shard_map/dot_general | solution.py:21
  67.0 0.6 collective-permute-start
  67.6 14.2 %collective-permute-done = f32[8,16384]{1,0:T(8,128)S(1)} collective-permute-done((f32[8,16384]{1,0:T(8,128)S(1)}, f32[8,16384]{1,0:T(8,128)S(1)}, u32[]{:S(2)}, u32[]{:S(2)}) %collective-permute-start) | collective-permute-done | bytes 524320 | tf_op jit(solution)/shard_map/ppermute | solution.py:10
  82.0 0.1 convert_element_type.21
  82.1 2.2 %all_gather.3 = bf16[1024,256]{1,0:T(8,128)(2,1)S(1)} all-gather(bf16[1024,128]{1,0:T(8,128)(2,1)S(1)} %convert_element_type.21), channel_id=1, replica_groups=mesh['dom'=16,'feat'=2] {'feat'}, dimensions={1}, use_global_device_ids=true | all-gather | bytes 786432 | tf_op jit(solution)/shard_map/all_gather | solution.py:71
  84.3 1.3 convert_reduce_fusion
  85.6 1.0 fusion.21
  86.6 38.9 %psum.15 = f32[128]{0:T(128)} all-reduce(f32[128]{0:T(128)S(1)} %get-tuple-element.3), channel_id=1, replica_groups=mesh['dom'=16,'feat'=2] {'dom'}, use_global_device_ids=true, to_apply=%region_2.3 | all-reduce | flops 128 | bytes 1024 | tf_op jit(solution)/shard_map/psum | solution.py:79
  125.5 63.9 %all-reduce.2.cloned.1.call-done = f32[256,128]{1,0:T(8,128)} async-done(((f32[256,128]{1,0:T(8,128)}), f32[256,128]{1,0:T(8,128)}) %all-reduce.2.cloned.1.call-update) | async-done | bytes 131088 | tf_op jit(solution)/shard_map/psum | solution.py:79
  189.4 1.6 copy.55
  (30 shorter events, 0.7 us)
Async XLA Ops:
  7.2 28.6 %copy-start = (bf16[64,128,128]{2,1,0:T(8,128)(2,1)S(1)}, bf16[64,128,128]{2,1,0:T(8,128)(2,1)}, u32[]{:S(2)}) copy-start(bf16[64,128,128]{2,1,0:T(8,128)(2,1)} %param.14) | copy-start | bytes 6291460
  28.1 5.5 %copy-start.6 = (s32[1,64]{1,0:T(1,128)S(1)}, s32[1,64]{1,0:T(1,128)}, u32[]{:S(2)}) copy-start(s32[1,64]{1,0:T(1,128)} %param.15) | copy-start | bytes 772
  28.1 5.6 %copy-start.1 = (bf16[1024,128]{1,0:T(8,128)(2,1)S(1)}, bf16[1024,128]{1,0:T(8,128)(2,1)}, u32[]{:S(2)}) copy-start(bf16[1024,128]{1,0:T(8,128)(2,1)} %param.10) | copy-start | bytes 786436
  29.2 27.7 %all-to-all-start.1 = ((bf16[16,2,128,128]{2,3,1,0:T(8,128)(2,1)}), bf16[16,2,128,128]{2,3,1,0:T(8,128)(2,1)}, u32[]{:S(2)}, u32[]{:S(2)}) async-start(bf16[16,2,128,128]{2,3,1,0:T(8,128)(2,1)} %broadcast_select_fusion), calls=%async_computation.1 | async-start | bytes 2097152 | tf_op jit(solution)/shard_map/all_to_all | solution.py:45
  33.5 155.9 %all-reduce.2.cloned.1.call-start = ((), (), s32[]{:S(2)}) async-start(), calls=%async_computation.2 | async-start | bytes 262144 | tf_op jit(solution)/shard_map/psum | solution.py:79
  40.9 5.7 %copy-start.2 = (s32[1,16,2]{1,2,0:T(2,128)S(1)}, s32[1,16,2]{1,2,0:T(2,128)}, u32[]{:S(2)}) copy-start(s32[1,16,2]{1,2,0:T(2,128)} %param.13) | copy-start | bytes 388
  40.9 5.8 %copy-start.3 = (s32[1,64]{1,0:T(1,128)S(1)}, s32[1,64]{1,0:T(1,128)}, u32[]{:S(2)}) copy-start(s32[1,64]{1,0:T(1,128)} %param.16) | copy-start | bytes 772
  67.0 17.3 %copy-start.4 = (bf16[1024,128]{1,0:T(8,128)(2,1)S(1)}, bf16[1024,128]{1,0:T(8,128)(2,1)}, u32[]{:S(2)}) copy-start(bf16[1024,128]{1,0:T(8,128)(2,1)} %param.19) | copy-start | bytes 786436
  67.0 17.3 %copy-start.5 = (bf16[256,128]{1,0:T(8,128)(2,1)S(1)}, bf16[256,128]{1,0:T(8,128)(2,1)}, u32[]{:S(2)}) copy-start(bf16[256,128]{1,0:T(8,128)(2,1)} %param.17) | copy-start | bytes 196612
  67.0 17.3 %copy-start.7 = (f32[128]{0:T(128)S(1)}, f32[128]{0:T(128)}, u32[]{:S(2)}) copy-start(f32[128]{0:T(128)} %param.18) | copy-start | bytes 1540
  67.0 14.8 %collective-permute-start = (f32[8,16384]{1,0:T(8,128)S(1)}, f32[8,16384]{1,0:T(8,128)S(1)}, u32[]{:S(2)}, u32[]{:S(2)}) collective-permute-start(f32[8,16384]{1,0:T(8,128)S(1)} %slice.13), channel_id=1, source_target_pairs={{30,0},{0,2},{2,4},{4,6},{6,8},{8,10},{10,12},{12,14},{14,16},{16,... | collective-permute-start | bytes 1572872 | tf_op jit(solution)/shard_map/ppermute | solution.py:10
Sparse Core Ops, SparseCore 0:
  86.8 102.6 all-reduce.1
where the time goes:
time: 198 us
  waiting for transfers between devices  82.5 us (42%)
  blocking collectives  56.4 us (28%)
  matrix products  20.5 us (10%)
  local copies, waits for them, and re-layouts  18.1 us (9%)
  between operations  14.2 us (7%)
  starting transfers between devices  4.98 us (3%)
    psum x1, waiting for transfers between devices, per_device(): grad_weight, grad_bias = lax.psum((weight_term, bias_term), 'dom')  63.9 us
    psum x1, blocking collectives, per_device(): grad_weight, grad_bias = lax.psum((weight_term, bias_term), 'dom')  38.9 us
    all_to_all x1, blocking collectives, per_device(): lax.all_to_all(requested, 'dom', split_axis=0, concat_axis=0, tiled=True)  15.4 us
    ppermute x1, waiting for transfers between devices, passed_along(): return lax.ppermute(block, axis, route)  14.2 us
    dot_general x2, matrix products, select_rows(): return jnp.dot(one_hot, values, precision=lax.Precision.HIGHEST)  9.25 us
    dot_general x1, local copies, waits for them, and re-layouts, per_device(): jnp.einsum('kij,kjf->kif', local_tiles, sources, preferred_element_type=j...  5.65 us
    dot_general x1, matrix products, per_device(): jnp.einsum('kij,kjf->kif', local_tiles, sources, preferred_element_type=j...  5.15 us
    all_to_all x1, starting transfers between devices, per_device(): lax.all_to_all(jnp.where((asked >= 0)[:, :, None, None], picked, jnp.zero...  4.35 us
  transfers between devices with their start and end apart: 3, of which 3 were waited for; matrix products, arithmetic and copies ran while one was open for 10% of the time, Pallas kernels for 0%

commit v1 on v0

v1 whole, which is shorter than its diff:
```python
import functools

import jax
import jax.numpy as jnp
from jax import lax
from jax.experimental import pallas as pl
from jax.experimental.pallas import tpu as pltpu
from jax.sharding import PartitionSpec as P

PEERS = 4
VMEM = pl.BlockSpec(memory_space=pltpu.VMEM)
SMEM = pl.BlockSpec(memory_space=pltpu.SMEM)
PARAMS = pltpu.CompilerParams(vmem_limit_bytes=48 * 1024 * 1024)


def partner(block, bits):
    count = lax.axis_size("dom")
    return lax.ppermute(block, "dom", [(i, i ^ bits) for i in range(count)])


def passed_along(block, axis, distance):
    count = lax.axis_size(axis)
    return lax.ppermute(block, axis, [((i - distance) % count, i) for i in range(count)])


def local_kernel(count, src_ref, dst_ref, tiles_ref, blocks_ref, acc_ref):
    acc_ref[...] = jnp.zeros_like(acc_ref)

    def body(k, carry):
        product = jnp.dot(
            tiles_ref[k], blocks_ref[src_ref[k]], preferred_element_type=jnp.float32
        )
        dst = dst_ref[k]
        acc_ref[dst] = acc_ref[dst] + product
        return carry

    lax.fori_loop(0, count, body, 0, unroll=8)


def local_sum(src, dst, tiles, blocks, row_count):
    count, size, _ = tiles.shape
    return pl.pallas_call(
        functools.partial(local_kernel, count),
        out_shape=jax.ShapeDtypeStruct((row_count, size, blocks.shape[-1]), jnp.float32),
        in_specs=[SMEM, SMEM, VMEM, VMEM],
        out_specs=VMEM,
        compiler_params=PARAMS,
    )(src, dst, tiles, blocks)


def select_kernel(members, cap, me_ref, *refs):
    asked, held, out = refs[: PEERS - 1], refs[PEERS - 1 : -(PEERS - 1)], refs[-(PEERS - 1) :]
    for at, member in enumerate(members):
        owner = me_ref[0] ^ (member * PEERS)
        for j in range(PEERS - 1):
            for c in range(cap):
                wanted = jnp.maximum(asked[j][owner * cap + c], 0)
                out[j][at * cap + c] = held[at][wanted]


def select_blocks(me, asked, members, held, cap):
    size = held[0].shape[1:]
    shape = jax.ShapeDtypeStruct((len(members) * cap, *size), held[0].dtype)
    return pl.pallas_call(
        functools.partial(select_kernel, members, cap),
        out_shape=[shape] * (PEERS - 1),
        in_specs=[SMEM] * PEERS + [VMEM] * len(members),
        out_specs=[VMEM] * (PEERS - 1),
        compiler_params=PARAMS,
    )(me, *asked, *held)


def remote_kernel(members, cap, last, me_ref, wanted_ref, dst_ref, tiles_ref, acc_in, *refs):
    held = refs[: len(members)]
    pulled = refs[len(members) : len(members) + PEERS - 1]
    outs = refs[len(members) + PEERS - 1 :]
    acc = outs[0] if not last else outs[-1]
    acc[...] = acc_in[...]
    for at, member in enumerate(members):
        for j in range(PEERS):
            owner = me_ref[0] ^ (member * PEERS + j)
            for c in range(cap):
                slot = owner * cap + c
                wanted = wanted_ref[slot]
                if j == 0:
                    block = held[at][jnp.maximum(wanted, 0)]
                else:
                    block = pulled[j - 1][at * cap + c]
                block = jnp.where(wanted >= 0, block, jnp.zeros_like(block))
                product = jnp.dot(tiles_ref[slot], block, preferred_element_type=jnp.float32)
                dst = dst_ref[slot]
                acc[dst] = acc[dst] + product
    if last:
        own_ref, next_ref = outs[:2]
        half = own_ref.shape[0]
        own_ref[...] = acc[:half]
        next_ref[...] = acc[half:].astype(next_ref.dtype)


def remote_sum(me, wanted, dst, tiles, acc, members, held, pulled, cap, last):
    row_count, size, width = acc.shape
    shape = (row_count // 2, size, width)
    if last:
        out_shape = [
            jax.ShapeDtypeStruct(shape, jnp.float32),
            jax.ShapeDtypeStruct(shape, jnp.bfloat16),
        ]
        scratch = [pltpu.VMEM(acc.shape, jnp.float32)]
    else:
        out_shape = [jax.ShapeDtypeStruct(acc.shape, jnp.float32)]
        scratch = []
    return pl.pallas_call(
        functools.partial(remote_kernel, members, cap, last),
        out_shape=out_shape,
        in_specs=[SMEM] * 3 + [VMEM] * (2 + len(held) + len(pulled)),
        out_specs=[VMEM] * len(out_shape),
        scratch_shapes=scratch,
        compiler_params=PARAMS,
    )(me, wanted, dst, tiles, acc, *held, *pulled)


def activate(value):
    return jax.nn.gelu(value, approximate=True)


def per_device(
    history,
    pull_list,
    remote_tiles,
    remote_dst,
    local_tiles,
    local_src,
    local_dst,
    weight,
    bias,
    cotangent,
):
    count = lax.axis_size("dom")
    columns = count // PEERS
    cap = pull_list.shape[2]
    half_width = history.shape[1]
    block_size = local_tiles.shape[1]
    own_blocks = history.shape[0] // block_size
    row_count = 2 * own_blocks
    blocks = history.reshape(own_blocks, block_size, half_width)
    me = lax.axis_index("dom").astype(jnp.int32).reshape(1)
    wanted = pull_list.reshape(-1)
    targets = remote_dst.reshape(-1)
    tiles = remote_tiles.reshape(-1, block_size, block_size)

    held = {0: blocks}
    for member in sorted(range(1, columns), key=lambda k: (bin(k).count("1"), -k)):
        low = member & -member
        held[member] = partner(held[member ^ low], low * PEERS)
    asked = [partner(wanted, j) for j in range(1, PEERS)]

    acc = local_sum(local_src.reshape(-1), local_dst.reshape(-1), local_tiles, blocks, row_count)

    first, last = list(range(columns - 1)), [columns - 1]
    for members in (first, last):
        mine = [held[k] for k in members]
        picked = select_blocks(me, asked, members, mine, cap)
        pulled = [partner(picked[j - 1], j) for j in range(1, PEERS)]
        outs = remote_sum(
            me, wanted, targets, tiles, acc, members, mine, pulled, cap, members is last
        )
        acc = outs[0]
    own, following = outs

    incoming = passed_along(following, "dom", 1)
    aggregate = (
        (own + incoming.astype(jnp.float32))
        .reshape(own_blocks * block_size, half_width)
        .astype(jnp.bfloat16)
    )
    aggregate_full = lax.all_gather(aggregate, "feat", axis=1, tiled=True)
    preact = jnp.dot(aggregate_full, weight, preferred_element_type=jnp.float32) + bias
    new_rows, backward_fn = jax.vjp(activate, preact)
    grad_pre = backward_fn(cotangent.astype(jnp.float32))[0].astype(jnp.bfloat16)
    weight_term = lax.dot_general(
        aggregate_full, grad_pre, (((0,), (0,)), ((), ())), preferred_element_type=jnp.float32
    )
    bias_term = jnp.sum(grad_pre.astype(jnp.float32), axis=0)
    total = jnp.concatenate([weight_term, jnp.broadcast_to(bias_term, (8, half_width))])
    bits = 1
    while bits < count:
        total = total + partner(total, bits)
        bits *= 2
    grad_weight, grad_bias = total[: weight.shape[0]], total[weight.shape[0]]
    return (new_rows.astype(jnp.bfloat16), grad_weight, grad_bias)


def solution(mesh):
    placed = (
        P("dom", "feat"),
        P("dom", None, None),
        P("dom", None, None, None, None),
        P("dom", None, None),
        P("dom", None, None),
        P("dom", None),
        P("dom", None),
        P(None, "feat"),
        P("feat"),
        P("dom", "feat"),
    )
    return jax.shard_map(
        per_device,
        mesh=mesh,
        in_specs=placed,
        out_specs=(P("dom", "feat"), P(None, "feat"), P("feat")),
        check_vma=False,
    )
```

time: 198 us -> 83.3 us (0.42)
  blocking collectives: 56.4 us -> 2.18 us
  waiting for transfers between devices: 82.5 us -> 44.9 us
  matrix products: 20.5 us -> 1.68 us
  starting transfers between devices: 4.98 us -> 20.1 us
  between operations: 14.2 us -> 0.83 us
  local copies, waits for them, and re-layouts: 18.1 us -> 7.68 us
  Pallas kernels: 0 us -> 5.52 us
    psum x1 -> x0, waiting for transfers between devices: 63.9 us -> none  [per_device(): grad_weight, grad_bias = lax.psum((weight_term, bias_term), 'dom')]
    psum x1 -> x0, blocking collectives: 38.9 us -> none  [per_device(): grad_weight, grad_bias = lax.psum((weight_term, bias_term), 'dom')]
    ppermute x1 -> x17, waiting for transfers between devices: 14.2 us -> 44.9 us  [the longest x16 36.6 us: partner(): return lax.ppermute(block, 'dom', [(i, i ^ bits) for i in range(count)])]
    ppermute x1 -> x17, starting transfers between devices: 0.59 us -> 20.1 us  [the longest x16 18.4 us: partner(): return lax.ppermute(block, 'dom', [(i, i ^ bits) for i in range(count)])]
    dot_general x4 -> x0, matrix products: 18.1 us -> none  [the longest x2 9.25 us: select_rows(): return jnp.dot(one_hot, values, precision=lax.Precision.HIGHEST)]
    all_to_all x1 -> x0, blocking collectives: 15.4 us -> none  [per_device(): lax.all_to_all(requested, 'dom', split_axis=0, concat_axis=0, tiled=True)]
    dot_general x2 -> x0, local copies, waits for them, and re-layouts: 8.55 us -> none  [the longest x1 5.65 us: per_device(): jnp.einsum('kij,kjf->kif', local_tiles, sources, preferred_element_type=j...]
    gather x3 -> x0, local copies, waits for them, and re-layouts: 6.35 us -> none  [the longest x2 4.22 us: per_device(): picked = blocks[clamped]]
  transfers between devices with their start and end apart: 3 -> 17, of which waited for: 3 -> 10; matrix products, arithmetic and copies ran while one was open for 10% -> 2% of each run, Pallas kernels for 0% -> 6%
where the time goes in v1:
time: 83.3 us; the launch traced here: 83.1 us
  waiting for transfers between devices  44.9 us (54%)
  starting transfers between devices  20.1 us (24%)
  local copies, waits for them, and re-layouts  7.68 us (9%)
  Pallas kernels  5.52 us (7%)
  blocking collectives  2.18 us (3%)
  matrix products  1.68 us (2%)
    ppermute x16, waiting for transfers between devices, partner(): return lax.ppermute(block, 'dom', [(i, i ^ bits) for i in range(count)])  36.6 us
    ppermute x16, starting transfers between devices, partner(): return lax.ppermute(block, 'dom', [(i, i ^ bits) for i in range(count)])  18.4 us
    ppermute x1, waiting for transfers between devices, passed_along(): lax.ppermute(block, axis, [((i - distance) % count, i) for i in range(cou...  8.33 us
    unnamed x20, local copies, waits for them, and re-layouts  6.33 us
    pallas_call x1, Pallas kernels, local_sum(): pl.pallas_call(functools.partial(local_kernel, count), out_shape=jax.Shap...  2.49 us
    all_gather x1, blocking collectives, per_device(): aggregate_full = lax.all_gather(aggregate, 'feat', axis=1, tiled=True)  2.18 us
    pallas_call x2, Pallas kernels, remote_sum(): pl.pallas_call(functools.partial(remote_kernel, members, cap, last), out_...  1.86 us
    ppermute x1, starting transfers between devices, passed_along(): lax.ppermute(block, axis, [((i - distance) % count, i) for i in range(cou...  1.69 us
  transfers between devices with their start and end apart: 17, of which 10 were waited for; matrix products, arithmetic and copies ran while one was open for 2% of the time, Pallas kernels for 6%

profile of v1, /device:TPU:0, one launch (start us, length us, event | category | flops | bytes accessed | tf_op | source)
XLA Modules:
  0.0 83.1 jit_solution(13890214279557693100)
XLA Ops:
  0.6 4.1 %collective-permute-start.1 = (bf16[8,128,128]{2,1,0:T(8,128)(2,1)}, bf16[8,128,128]{2,1,0:T(8,128)(2,1)S(1)}, u32[]{:S(2)}, u32[]{:S(2)}) collective-permute-start(bf16[8,128,128]{2,1,0:T(8,128)(2,1)} %bitcast.14), channel_id=1, source_target_pairs={{0,16},{2,18},{4,20},{6,22},{8,24},{10,26},{12,28},{14,30},{16,0},... | collective-permute-start | bytes 786440 | tf_op jit(solution)/shard_map/ppermute | solution.py:18
  4.7 1.6 %collective-permute-start = (bf16[8,128,128]{2,1,0:T(8,128)(2,1)}, bf16[8,128,128]{2,1,0:T(8,128)(2,1)S(1)}, u32[]{:S(2)}, u32[]{:S(2)}) collective-permute-start(bf16[8,128,128]{2,1,0:T(8,128)(2,1)} %bitcast.15), channel_id=1, source_target_pairs={{0,8},{2,10},{4,12},{6,14},{8,0},{10,2},{12,4},{14,6},{16,24},{18,... | collective-permute-start | bytes 786440 | tf_op jit(solution)/shard_map/ppermute | solution.py:18
  6.3 10.7 %collective-permute-done.1.refs_5_.refs_2_ = bf16[8,128,128]{2,1,0:T(8,128)(2,1)S(1)} collective-permute-done((bf16[8,128,128]{2,1,0:T(8,128)(2,1)}, bf16[8,128,128]{2,1,0:T(8,128)(2,1)S(1)}, u32[]{:S(2)}, u32[]{:S(2)}) %collective-permute-start.1) | collective-permute-done | bytes 262176 | tf_op jit(solution)/shard_map/ppermute | solution.py:18
  18.6 1.6 %collective-permute-start.2 = (s32[32]{0:T(128)S(1)}, s32[32]{0:T(128)S(1)}, u32[]{:S(2)}, u32[]{:S(2)}) collective-permute-start(s32[32]{0:T(128)S(1)} %reshape.31.wanted_ref), channel_id=1, source_target_pairs={{0,2},{2,0},{4,6},{6,4},{8,10},{10,8},{12,14},{14,12},{16,18},{18,... | collective-permute-start | bytes 392 | tf_op jit(solution)/shard_map/ppermute | solution.py:18
  20.1 1.5 %collective-permute-start.3 = (s32[32]{0:T(128)S(1)}, s32[32]{0:T(128)S(1)}, u32[]{:S(2)}, u32[]{:S(2)}) collective-permute-start(s32[32]{0:T(128)S(1)} %reshape.31.wanted_ref), channel_id=1, source_target_pairs={{0,4},{2,6},{4,0},{6,2},{8,12},{10,14},{12,8},{14,10},{16,20},{18,... | collective-permute-start | bytes 392 | tf_op jit(solution)/shard_map/ppermute | solution.py:18
  22.2 1.5 %collective-permute-done.3.refs_1_ = s32[32]{0:T(128)S(1)} collective-permute-done((s32[32]{0:T(128)S(1)}, s32[32]{0:T(128)S(1)}, u32[]{:S(2)}, u32[]{:S(2)}) %collective-permute-start.3) | collective-permute-done | bytes 160 | tf_op jit(solution)/shard_map/ppermute | solution.py:18
  23.7 2.4 %collective-permute-done.4.refs_2_ = s32[32]{0:T(128)S(1)} collective-permute-done((s32[32]{0:T(128)S(1)}, s32[32]{0:T(128)S(1)}, u32[]{:S(2)}, u32[]{:S(2)}) %collective-permute-start.4) | collective-permute-done | bytes 160 | tf_op jit(solution)/shard_map/ppermute | solution.py:18
  26.1 0.9 %copy-done.2 = bf16[1024,128]{1,0:T(8,128)(2,1)S(1)} copy-done((bf16[1024,128]{1,0:T(8,128)(2,1)S(1)}, bf16[1024,128]{1,0:T(8,128)(2,1)}, u32[]{:S(2)}) %copy-start.2) | copy-done | bytes 262168
  28.7 2.4 %collective-permute-start.7 = (bf16[6,128,128]{2,1,0:T(8,128)(2,1)S(1)}, bf16[6,128,128]{2,1,0:T(8,128)(2,1)S(1)}, u32[]{:S(2)}, u32[]{:S(2)}) collective-permute-start(bf16[6,128,128]{2,1,0:T(8,128)(2,1)S(1)} %get-tuple-element.13), channel_id=1, source_target_pairs={{0,6},{2,4},{4,2},{6,0},{8,14},{10,12},{12,10},{14,8},{16,22},{18,... | collective-permute-start | bytes 589832 | tf_op jit(solution)/shard_map/ppermute | solution.py:18
  32.3 1.5 %collective-permute-start.11 = (bf16[2,128,128]{2,1,0:T(8,128)(2,1)S(1)}, bf16[2,128,128]{2,1,0:T(8,128)(2,1)S(1)}, u32[]{:S(2)}, u32[]{:S(2)}) collective-permute-start(bf16[2,128,128]{2,1,0:T(8,128)(2,1)S(1)} %get-tuple-element.16), channel_id=1, source_target_pairs={{0,6},{2,4},{4,2},{6,0},{8,14},{10,12},{12,10},{14,8},{16,22},{18,... | collective-permute-start | bytes 196616 | tf_op jit(solution)/shard_map/ppermute | solution.py:18
  33.8 1.7 %collective-permute-done.5.refs_3_ = bf16[6,128,128]{2,1,0:T(8,128)(2,1)S(1)} collective-permute-done((bf16[6,128,128]{2,1,0:T(8,128)(2,1)S(1)}, bf16[6,128,128]{2,1,0:T(8,128)(2,1)S(1)}, u32[]{:S(2)}, u32[]{:S(2)}) %collective-permute-start.5) | collective-permute-done | bytes 196640 | tf_op jit(solution)/shard_map/ppermute | solution.py:18
  36.8 0.9 %copy-done.3 = bf16[1024,128]{1,0:T(8,128)(2,1)S(1)} copy-done((bf16[1024,128]{1,0:T(8,128)(2,1)S(1)}, bf16[1024,128]{1,0:T(8,128)(2,1)}, u32[]{:S(2)}) %copy-start.3) | copy-done | bytes 262168
  37.7 1.6 %copy-done.4 = bf16[64,128,128]{2,1,0:T(8,128)(2,1)S(1)} copy-done((bf16[64,128,128]{2,1,0:T(8,128)(2,1)S(1)}, bf16[64,128,128]{2,1,0:T(8,128)(2,1)}, u32[]{:S(2)}) %copy-start.4) | copy-done | bytes 2097176
  40.6 2.5 %shard_map.121.acc_in = f32[16,128,128]{2,1,0:T(8,128)S(1)} custom-call(s32[64]{0:T(128)S(1)} %bitcast.19, s32[64]{0:T(128)S(1)} %bitcast.20, bf16[64,128,128]{2,1,0:T(8,128)(2,1)S(1)} %copy-done.4, bf16[8,128,128]{2,1,0:T(8,128)(2,1)S(1)} %bitcast.17), custom_call_target="tpu_custom_call" | custom-call | tf_op jit(solution)/shard_map/pallas_call | solution.py:42
  43.2 1.0 %shard_map.123.acc_in = f32[16,128,128]{2,1,0:T(8,128)S(1)} custom-call(s32[1]{0:T(128)} %bitcast.me_ref, s32[32]{0:T(128)S(1)} %reshape.31.wanted_ref, s32[32]{0:T(128)S(1)} %reshape.32.dst_ref, bf16[32,128,128]{2,1,0:T(8,128)(2,1)S(1)} %bitcast.12, f32[16,128,128]{2,1,0:T(8,128)S(1)} %shard_map.121.acc_in, bf16[8,128,128]{2,1,0:T(8,128)(2,1)S(1)} %bitcast.18, ...), custom_call_target="tpu_custom_call" | custom-call | tf_op jit(solution)/shard_map/pallas_call | solution.py:112
  45.1 1.7 %collective-permute-start.12 = (bf16[8,128,128]{2,1,0:T(8,128)(2,1)S(1)}, bf16[8,128,128]{2,1,0:T(8,128)(2,1)S(1)}, u32[]{:S(2)}, u32[]{:S(2)}) collective-permute-start(bf16[8,128,128]{2,1,0:T(8,128)(2,1)S(1)} %get-tuple-element.18), channel_id=1, source_target_pairs={{30,0},{0,2},{2,4},{4,6},{6,8},{8,10},{10,12},{12,14},{14,16},{16,... | collective-permute-start | bytes 786440 | tf_op jit(solution)/shard_map/ppermute | solution.py:23
  46.8 8.3 %collective-permute-done.12 = bf16[8,128,128]{2,1,0:T(8,128)(2,1)S(1)} collective-permute-done((bf16[8,128,128]{2,1,0:T(8,128)(2,1)S(1)}, bf16[8,128,128]{2,1,0:T(8,128)(2,1)S(1)}, u32[]{:S(2)}, u32[]{:S(2)}) %collective-permute-start.12) | collective-permute-done | bytes 262176 | tf_op jit(solution)/shard_map/ppermute | solution.py:23
  55.2 2.2 %all_gather.3 = bf16[1024,256]{1,0:T(8,128)(2,1)S(1)} all-gather(bf16[1024,128]{1,0:T(8,128)(2,1)S(1)} %bitcast.21), channel_id=1, replica_groups=mesh['dom'=16,'feat'=2] {'feat'}, dimensions={1}, use_global_device_ids=true | all-gather | bytes 786432 | tf_op jit(solution)/shard_map/all_gather | solution.py:176
  57.4 1.3 %convert_reduce_fusion = (f32[128]{0:T(128)S(1)}, bf16[1024,128]{1,0:T(8,128)(2,1)S(1)}, bf16[1024,128]{1,0:T(8,128)(2,1)}) fusion(bf16[1024,128]{1,0:T(8,128)(2,1)S(1)} %copy-done.7, f32[128]{0:T(128)S(1)} %copy-done.8, bf16[1024,256]{1,0:T(8,128)(2,1)S(1)} %all_gather.3, bf16[256,128]{1,0:T(8,128)(2,1)S(1)} %copy-done), kind=kOutput, calls=%fused_computation.15 | convolution fusion | flops 70516608 | bytes 1377280 | tf_op jit(solution)/shard_map/dot_general | solution.py:177
  59.2 5.6 %collective-permute-done.13 = f32[264,128]{1,0:T(8,128)S(1)} collective-permute-done((f32[264,128]{1,0:T(8,128)S(1)}, f32[264,128]{1,0:T(8,128)S(1)}, u32[]{:S(2)}, u32[]{:S(2)}) %collective-permute-start.13) | collective-permute-done | bytes 135200 | tf_op jit(solution)/shard_map/ppermute | solution.py:18
  64.9 5.0 %collective-permute-done.14 = f32[264,128]{1,0:T(8,128)S(1)} collective-permute-done((f32[264,128]{1,0:T(8,128)S(1)}, f32[264,128]{1,0:T(8,128)S(1)}, u32[]{:S(2)}, u32[]{:S(2)}) %collective-permute-start.14) | collective-permute-done | bytes 135200 | tf_op jit(solution)/shard_map/ppermute | solution.py:18
  70.0 5.0 %collective-permute-done.15 = f32[264,128]{1,0:T(8,128)S(1)} collective-permute-done((f32[264,128]{1,0:T(8,128)S(1)}, f32[264,128]{1,0:T(8,128)S(1)}, u32[]{:S(2)}, u32[]{:S(2)}) %collective-permute-start.15) | collective-permute-done | bytes 135200 | tf_op jit(solution)/shard_map/ppermute | solution.py:18
  75.0 2.2 %collective-permute-start.16 = (f32[264,128]{1,0:T(8,128)S(1)}, f32[264,128]{1,0:T(8,128)S(1)}, u32[]{:S(2)}, u32[]{:S(2)}) collective-permute-start(f32[264,128]{1,0:T(8,128)S(1)} %add.37), channel_id=1, source_target_pairs={{0,16},{2,18},{4,20},{6,22},{8,24},{10,26},{12,28},{14,30},{16,0},... | collective-permute-start | bytes 405512 | tf_op jit(solution)/shard_map/ppermute | solution.py:18
  77.2 4.7 %collective-permute-done.16 = f32[264,128]{1,0:T(8,128)S(1)} collective-permute-done((f32[264,128]{1,0:T(8,128)S(1)}, f32[264,128]{1,0:T(8,128)S(1)}, u32[]{:S(2)}, u32[]{:S(2)}) %collective-permute-start.16) | collective-permute-done | bytes 135200 | tf_op jit(solution)/shard_map/ppermute | solution.py:18
  (49 shorter events, 10.2 us)
Async XLA Ops:
  0.6 56.7 %copy-start = (bf16[256,128]{1,0:T(8,128)(2,1)S(1)}, bf16[256,128]{1,0:T(8,128)(2,1)}, u32[]{:S(2)}) copy-start(bf16[256,128]{1,0:T(8,128)(2,1)} %param.17) | copy-start | bytes 196612
  0.6 16.3 %collective-permute-start.1 = (bf16[8,128,128]{2,1,0:T(8,128)(2,1)}, bf16[8,128,128]{2,1,0:T(8,128)(2,1)S(1)}, u32[]{:S(2)}, u32[]{:S(2)}) collective-permute-start(bf16[8,128,128]{2,1,0:T(8,128)(2,1)} %bitcast.14), channel_id=1, source_target_pairs={{0,16},{2,18},{4,20},{6,22},{8,24},{10,26},{12,28},{14,30},{16,0},... | collective-permute-start | bytes 786440 | tf_op jit(solution)/shard_map/ppermute | solution.py:18
  4.7 21.3 %collective-permute-start = (bf16[8,128,128]{2,1,0:T(8,128)(2,1)}, bf16[8,128,128]{2,1,0:T(8,128)(2,1)S(1)}, u32[]{:S(2)}, u32[]{:S(2)}) collective-permute-start(bf16[8,128,128]{2,1,0:T(8,128)(2,1)} %bitcast.15), channel_id=1, source_target_pairs={{0,8},{2,10},{4,12},{6,14},{8,0},{10,2},{12,4},{14,6},{16,24},{18,... | collective-permute-start | bytes 786440 | tf_op jit(solution)/shard_map/ppermute | solution.py:18
  17.0 14.2 %collective-permute-start.8 = (bf16[8,128,128]{2,1,0:T(8,128)(2,1)S(1)}, bf16[8,128,128]{2,1,0:T(8,128)(2,1)S(1)}, u32[]{:S(2)}, u32[]{:S(2)}) collective-permute-start(bf16[8,128,128]{2,1,0:T(8,128)(2,1)S(1)} %collective-permute-done.1.refs_5_.refs_2_), channel_id=1, source_target_pairs={{0,8},{2,10},{4,12},{6,14},{8,0},{10,2},{12,4},{14,6},{16,24},{18,... | collective-permute-start | bytes 786440 | tf_op jit(solution)/shard_map/ppermute | solution.py:18
  18.6 3.6 %collective-permute-start.2 = (s32[32]{0:T(128)S(1)}, s32[32]{0:T(128)S(1)}, u32[]{:S(2)}, u32[]{:S(2)}) collective-permute-start(s32[32]{0:T(128)S(1)} %reshape.31.wanted_ref), channel_id=1, source_target_pairs={{0,2},{2,0},{4,6},{6,4},{8,10},{10,8},{12,14},{14,12},{16,18},{18,... | collective-permute-start | bytes 392 | tf_op jit(solution)/shard_map/ppermute | solution.py:18
  20.1 3.5 %collective-permute-start.3 = (s32[32]{0:T(128)S(1)}, s32[32]{0:T(128)S(1)}, u32[]{:S(2)}, u32[]{:S(2)}) collective-permute-start(s32[32]{0:T(128)S(1)} %reshape.31.wanted_ref), channel_id=1, source_target_pairs={{0,4},{2,6},{4,0},{6,2},{8,12},{10,14},{12,8},{14,10},{16,20},{18,... | collective-permute-start | bytes 392 | tf_op jit(solution)/shard_map/ppermute | solution.py:18
  21.6 4.4 %collective-permute-start.4 = (s32[32]{0:T(128)S(1)}, s32[32]{0:T(128)S(1)}, u32[]{:S(2)}, u32[]{:S(2)}) collective-permute-start(s32[32]{0:T(128)S(1)} %reshape.31.wanted_ref), channel_id=1, source_target_pairs={{0,6},{2,4},{4,2},{6,0},{8,14},{10,12},{12,10},{14,8},{16,22},{18,... | collective-permute-start | bytes 392 | tf_op jit(solution)/shard_map/ppermute | solution.py:18
  26.1 1.0 %copy-start.2 = (bf16[1024,128]{1,0:T(8,128)(2,1)S(1)}, bf16[1024,128]{1,0:T(8,128)(2,1)}, u32[]{:S(2)}) copy-start(bf16[1024,128]{1,0:T(8,128)(2,1)} %param.10) | copy-start | bytes 786436
  27.0 16.1 %copy-start.1 = (bf16[1,16,2,128,128]{4,3,2,1,0:T(8,128)(2,1)S(1)}, bf16[1,16,2,128,128]{4,3,2,1,0:T(8,128)(2,1)}, u32[]{:S(2)}) copy-start(bf16[1,16,2,128,128]{4,3,2,1,0:T(8,128)(2,1)} %param.12) | copy-start | bytes 3145732
  27.6 7.9 %collective-permute-start.5 = (bf16[6,128,128]{2,1,0:T(8,128)(2,1)S(1)}, bf16[6,128,128]{2,1,0:T(8,128)(2,1)S(1)}, u32[]{:S(2)}, u32[]{:S(2)}) collective-permute-start(bf16[6,128,128]{2,1,0:T(8,128)(2,1)S(1)} %get-tuple-element.11), channel_id=1, source_target_pairs={{0,2},{2,0},{4,6},{6,4},{8,10},{10,8},{12,14},{14,12},{16,18},{18,... | collective-permute-start | bytes 589832 | tf_op jit(solution)/shard_map/ppermute | solution.py:18
  28.2 14.9 %collective-permute-start.6 = (bf16[6,128,128]{2,1,0:T(8,128)(2,1)S(1)}, bf16[6,128,128]{2,1,0:T(8,128)(2,1)S(1)}, u32[]{:S(2)}, u32[]{:S(2)}) collective-permute-start(bf16[6,128,128]{2,1,0:T(8,128)(2,1)S(1)} %get-tuple-element.12), channel_id=1, source_target_pairs={{0,4},{2,6},{4,0},{6,2},{8,12},{10,14},{12,8},{14,10},{16,20},{18,... | collective-permute-start | bytes 589832 | tf_op jit(solution)/shard_map/ppermute | solution.py:18
  28.7 14.4 %collective-permute-start.7 = (bf16[6,128,128]{2,1,0:T(8,128)(2,1)S(1)}, bf16[6,128,128]{2,1,0:T(8,128)(2,1)S(1)}, u32[]{:S(2)}, u32[]{:S(2)}) collective-permute-start(bf16[6,128,128]{2,1,0:T(8,128)(2,1)S(1)} %get-tuple-element.13), channel_id=1, source_target_pairs={{0,6},{2,4},{4,2},{6,0},{8,14},{10,12},{12,10},{14,8},{16,22},{18,... | collective-permute-start | bytes 589832 | tf_op jit(solution)/shard_map/ppermute | solution.py:18
  31.8 12.5 %collective-permute-start.10 = (bf16[2,128,128]{2,1,0:T(8,128)(2,1)S(1)}, bf16[2,128,128]{2,1,0:T(8,128)(2,1)S(1)}, u32[]{:S(2)}, u32[]{:S(2)}) collective-permute-start(bf16[2,128,128]{2,1,0:T(8,128)(2,1)S(1)} %get-tuple-element.15), channel_id=1, source_target_pairs={{0,4},{2,6},{4,0},{6,2},{8,12},{10,14},{12,8},{14,10},{16,20},{18,... | collective-permute-start | bytes 196616 | tf_op jit(solution)/shard_map/ppermute | solution.py:18
  32.3 11.9 %collective-permute-start.11 = (bf16[2,128,128]{2,1,0:T(8,128)(2,1)S(1)}, bf16[2,128,128]{2,1,0:T(8,128)(2,1)S(1)}, u32[]{:S(2)}, u32[]{:S(2)}) collective-permute-start(bf16[2,128,128]{2,1,0:T(8,128)(2,1)S(1)} %get-tuple-element.16), channel_id=1, source_target_pairs={{0,6},{2,4},{4,2},{6,0},{8,14},{10,12},{12,10},{14,8},{16,22},{18,... | collective-permute-start | bytes 196616 | tf_op jit(solution)/shard_map/ppermute | solution.py:18
  35.5 8.7 %collective-permute-start.9 = (bf16[2,128,128]{2,1,0:T(8,128)(2,1)S(1)}, bf16[2,128,128]{2,1,0:T(8,128)(2,1)S(1)}, u32[]{:S(2)}, u32[]{:S(2)}) collective-permute-start(bf16[2,128,128]{2,1,0:T(8,128)(2,1)S(1)} %get-tuple-element.14), channel_id=1, source_target_pairs={{0,2},{2,0},{4,6},{6,4},{8,10},{10,8},{12,14},{14,12},{16,18},{18,... | collective-permute-start | bytes 196616 | tf_op jit(solution)/shard_map/ppermute | solution.py:18
  36.8 1.0 %copy-start.3 = (bf16[1024,128]{1,0:T(8,128)(2,1)S(1)}, bf16[1024,128]{1,0:T(8,128)(2,1)}, u32[]{:S(2)}) copy-start(bf16[1024,128]{1,0:T(8,128)(2,1)} %param.10) | copy-start | bytes 786436
  37.7 1.6 %copy-start.4 = (bf16[64,128,128]{2,1,0:T(8,128)(2,1)S(1)}, bf16[64,128,128]{2,1,0:T(8,128)(2,1)}, u32[]{:S(2)}) copy-start(bf16[64,128,128]{2,1,0:T(8,128)(2,1)} %tiles_ref.1) | copy-start | bytes 6291460
  44.2 13.2 %copy-start.7 = (bf16[1024,128]{1,0:T(8,128)(2,1)S(1)}, bf16[1024,128]{1,0:T(8,128)(2,1)}, u32[]{:S(2)}) copy-start(bf16[1024,128]{1,0:T(8,128)(2,1)} %param.19) | copy-start | bytes 786436
  44.2 13.2 %copy-start.8 = (f32[128]{0:T(128)S(1)}, f32[128]{0:T(128)}, u32[]{:S(2)}) copy-start(f32[128]{0:T(128)} %param.18) | copy-start | bytes 1540
  45.1 10.0 %collective-permute-start.12 = (bf16[8,128,128]{2,1,0:T(8,128)(2,1)S(1)}, bf16[8,128,128]{2,1,0:T(8,128)(2,1)S(1)}, u32[]{:S(2)}, u32[]{:S(2)}) collective-permute-start(bf16[8,128,128]{2,1,0:T(8,128)(2,1)S(1)} %get-tuple-element.18), channel_id=1, source_target_pairs={{30,0},{0,2},{2,4},{4,6},{6,8},{8,10},{10,12},{12,14},{14,16},{16,... | collective-permute-start | bytes 786440 | tf_op jit(solution)/shard_map/ppermute | solution.py:23
  59.1 5.7 %collective-permute-start.13 = (f32[264,128]{1,0:T(8,128)S(1)}, f32[264,128]{1,0:T(8,128)S(1)}, u32[]{:S(2)}, u32[]{:S(2)}) collective-permute-start(f32[264,128]{1,0:T(8,128)S(1)} %pad_maximum_fusion), channel_id=1, source_target_pairs={{0,2},{2,0},{4,6},{6,4},{8,10},{10,8},{12,14},{14,12},{16,18},{18,... | collective-permute-start | bytes 405512 | tf_op jit(solution)/shard_map/ppermute | solution.py:18
  64.8 5.1 %collective-permute-start.14 = (f32[264,128]{1,0:T(8,128)S(1)}, f32[264,128]{1,0:T(8,128)S(1)}, u32[]{:S(2)}, u32[]{:S(2)}) collective-permute-start(f32[264,128]{1,0:T(8,128)S(1)} %fusion.10), channel_id=1, source_target_pairs={{0,4},{2,6},{4,0},{6,2},{8,12},{10,14},{12,8},{14,10},{16,20},{18,... | collective-permute-start | bytes 405512 | tf_op jit(solution)/shard_map/ppermute | solution.py:18
  69.9 5.1 %collective-permute-start.15 = (f32[264,128]{1,0:T(8,128)S(1)}, f32[264,128]{1,0:T(8,128)S(1)}, u32[]{:S(2)}, u32[]{:S(2)}) collective-permute-start(f32[264,128]{1,0:T(8,128)S(1)} %add.36), channel_id=1, source_target_pairs={{0,8},{2,10},{4,12},{6,14},{8,0},{10,2},{12,4},{14,6},{16,24},{18,... | collective-permute-start | bytes 405512 | tf_op jit(solution)/shard_map/ppermute | solution.py:18
  75.0 6.9 %collective-permute-start.16 = (f32[264,128]{1,0:T(8,128)S(1)}, f32[264,128]{1,0:T(8,128)S(1)}, u32[]{:S(2)}, u32[]{:S(2)}) collective-permute-start(f32[264,128]{1,0:T(8,128)S(1)} %add.37), channel_id=1, source_target_pairs={{0,16},{2,18},{4,20},{6,22},{8,24},{10,26},{12,28},{14,30},{16,0},... | collective-permute-start | bytes 405512 | tf_op jit(solution)/shard_map/ppermute | solution.py:18
  (2 other events, 1.3 us)

commit v2 on v1

v2 whole, which is shorter than its diff:
```python
import functools

import jax
import jax.numpy as jnp
from jax import lax
from jax.experimental import pallas as pl
from jax.experimental.pallas import tpu as pltpu
from jax.sharding import PartitionSpec as P

PEERS = 4
VMEM = pl.BlockSpec(memory_space=pltpu.VMEM)
SMEM = pl.BlockSpec(memory_space=pltpu.SMEM)
PARAMS = pltpu.CompilerParams(vmem_limit_bytes=48 * 1024 * 1024)


def partner(block, bits):
    count = lax.axis_size("dom")
    return lax.ppermute(block, "dom", [(i, i ^ bits) for i in range(count)])


def passed_along(block, axis, distance):
    count = lax.axis_size(axis)
    return lax.ppermute(block, axis, [((i - distance) % count, i) for i in range(count)])


def select_kernel(members, cap, me_ref, *refs):
    asked, held, out = refs[: PEERS - 1], refs[PEERS - 1 : -(PEERS - 1)], refs[-(PEERS - 1) :]
    for at, member in enumerate(members):
        owner = me_ref[0] ^ (member * PEERS)
        for j in range(PEERS - 1):
            for c in range(cap):
                wanted = jnp.maximum(asked[j][c, owner], 0)
                out[j][at * cap + c] = held[at][wanted]


def select_blocks(me, asked, members, held, cap):
    size = held[0].shape[1:]
    shape = jax.ShapeDtypeStruct((len(members) * cap, *size), held[0].dtype)
    return pl.pallas_call(
        functools.partial(select_kernel, members, cap),
        out_shape=[shape] * (PEERS - 1),
        in_specs=[SMEM] * PEERS + [VMEM] * len(members),
        out_specs=[VMEM] * (PEERS - 1),
        compiler_params=PARAMS,
    )(me, *asked, *held)


def begin_kernel(count, src_ref, dst_ref, tiles_ref, blocks_ref, acc):
    acc[...] = jnp.zeros_like(acc)

    def body(k, carry):
        product = jnp.dot(
            tiles_ref[k], blocks_ref[src_ref[0, k]], preferred_element_type=jnp.float32
        )
        dst = dst_ref[0, k]
        acc[dst] = acc[dst] + product
        return carry

    lax.fori_loop(0, count, body, 0, unroll=8)


def begin_sum(src, dst, tiles, blocks, row_count):
    count, size, _ = tiles.shape
    return pl.pallas_call(
        functools.partial(begin_kernel, count),
        out_shape=[jax.ShapeDtypeStruct((row_count, size, blocks.shape[-1]), jnp.float32)],
        in_specs=[SMEM, SMEM, VMEM, VMEM],
        out_specs=[VMEM],
        compiler_params=PARAMS,
    )(src, dst, tiles, blocks)


def sum_kernel(members, cap, last, *refs):
    refs = list(refs)
    me_ref, wanted_ref, dst_ref, tiles_ref = refs[:4]
    del refs[:4]
    held = [refs.pop(0) for _ in members]
    pulled = [refs.pop(0) for _ in range(PEERS - 1)]
    acc = refs[-1]
    acc[...] = refs[0][...]
    for at, member in enumerate(members):
        for j in range(PEERS):
            owner = me_ref[0] ^ (member * PEERS + j)
            for c in range(cap):
                wanted = wanted_ref[c, owner]
                if j == 0:
                    block = held[at][jnp.maximum(wanted, 0)]
                else:
                    block = pulled[j - 1][at * cap + c]
                block = jnp.where(wanted >= 0, block, jnp.zeros_like(block))
                product = jnp.dot(
                    tiles_ref[owner * cap + c], block, preferred_element_type=jnp.float32
                )
                dst = dst_ref[c, owner]
                acc[dst] = acc[dst] + product
    if last:
        own_ref, next_ref = refs[1:3]
        half = own_ref.shape[0]
        own_ref[...] = acc[:half]
        next_ref[...] = acc[half:].astype(next_ref.dtype)


def tile_sum(shared, members, held, pulled, cap, row_count, acc, last=False):
    size, width = held[0].shape[1:]
    full = (row_count, size, width)
    half = (row_count // 2, size, width)
    scratch = []
    out_shape = [jax.ShapeDtypeStruct(full, jnp.float32)]
    if last:
        out_shape = [
            jax.ShapeDtypeStruct(half, jnp.float32),
            jax.ShapeDtypeStruct(half, jnp.bfloat16),
        ]
        scratch = [pltpu.VMEM(full, jnp.float32)]
    return pl.pallas_call(
        functools.partial(sum_kernel, members, cap, last),
        out_shape=out_shape,
        in_specs=[SMEM] * 3 + [VMEM] * (2 + len(held) + len(pulled)),
        out_specs=[VMEM] * len(out_shape),
        scratch_shapes=scratch,
        compiler_params=PARAMS,
    )(*shared, *held, *pulled, acc)


def activate(value):
    return jax.nn.gelu(value, approximate=True)


def rounded(value):
    return lax.reduce_precision(value, 8, 7)


def finish_kernel(weight_refs, bias_ref, weight_out, bias_out):
    at = 0
    for mine, got in weight_refs:
        depth = mine.shape[0]
        weight_out[at : at + depth] = mine[...] + got[:depth].astype(jnp.float32)
        at += depth
    got = weight_refs[0][1]
    depth = weight_refs[0][0].shape[0]
    rows = got[depth:].astype(jnp.float32)
    bias_out[...] = bias_ref[...] + (rows[:1] + rows[8:9])


def finish(parts, bias_term):
    depth = sum(mine.shape[0] for mine, _ in parts)
    width = bias_term.shape[1]
    count = len(parts)

    def kernel(*refs):
        pairs = [(refs[2 * i], refs[2 * i + 1]) for i in range(count)]
        finish_kernel(pairs, refs[2 * count], refs[2 * count + 1], refs[2 * count + 2])

    return pl.pallas_call(
        kernel,
        out_shape=[
            jax.ShapeDtypeStruct((depth, width), jnp.float32),
            jax.ShapeDtypeStruct((1, width), jnp.float32),
        ],
        in_specs=[VMEM] * (2 * count + 1),
        out_specs=[VMEM] * 2,
        compiler_params=PARAMS,
    )(*[array for pair in parts for array in pair], bias_term)


def summed(weight_term, bias_term, count):
    depth, width = weight_term.shape
    bias_term = bias_term[None]
    got, bits = None, 1
    while bits < count:
        if got is not None:
            bias_term = bias_term + (got[depth : depth + 1] + got[depth + 8 : depth + 9])
            weight_term = weight_term + got[:depth]
        weight_term = rounded(weight_term)
        high = rounded(bias_term)
        low = rounded(bias_term - high)
        bias_term = high + low
        rows = [jnp.broadcast_to(row, (8, width)) for row in (high, low)]
        raw = partner(jnp.concatenate([weight_term, *rows]).astype(jnp.bfloat16), bits)
        got = raw.astype(jnp.float32)
        bits *= 2
    grad_weight, grad_bias = finish([(weight_term, raw)], bias_term)
    return grad_weight, grad_bias[0]


def per_device(
    history,
    pull_list,
    remote_tiles,
    remote_dst,
    local_tiles,
    local_src,
    local_dst,
    weight,
    bias,
    cotangent,
):
    count = lax.axis_size("dom")
    columns = count // PEERS
    cap = pull_list.shape[2]
    half_width = history.shape[1]
    block_size = local_tiles.shape[1]
    own_blocks = history.shape[0] // block_size
    row_count = 2 * own_blocks
    blocks = history.reshape(own_blocks, block_size, half_width)
    me = lax.axis_index("dom").astype(jnp.int32).reshape(1)
    wanted = pull_list[0].T
    tiles = remote_tiles.reshape(-1, block_size, block_size)
    shared = (me, wanted, remote_dst[0].T, tiles)

    def exchange(members, held):
        picked = select_blocks(me, asked, members, held, cap)
        return picked, [partner(picked[j - 1], j) for j in range(1, PEERS)]

    held = {0: blocks}
    for member in range(columns // 2, 0, -1):
        if member & (member - 1) == 0:
            held[member] = partner(blocks, member * PEERS)
    asked = [partner(wanted, j) for j in range(1, PEERS)]
    (acc,) = begin_sum(local_src, local_dst, local_tiles, blocks, row_count)
    for member in range(1, columns):
        if member not in held:
            low = member & -member
            source, acc, *asked = lax.optimization_barrier((held[member ^ low], acc, *asked))
            held[member] = partner(source, low * PEERS)

    first, last = list(range(columns - 1)), columns - 1
    held_first = [held[k] for k in first]
    picked, pulled_first = exchange(first, held_first)
    picked, pulled_last = exchange([last], [held[last]])
    (acc,) = tile_sum(shared, first, held_first, pulled_first, cap, row_count, acc=acc)
    outs = tile_sum(
        shared, [last], [held[last]], pulled_last, cap, row_count, acc=acc, last=True
    )
    own, following = outs

    incoming = passed_along(following, "dom", 1)
    aggregate = (
        (own + incoming.astype(jnp.float32))
        .reshape(own_blocks * block_size, half_width)
        .astype(jnp.bfloat16)
    )
    aggregate_full = lax.all_gather(aggregate, "feat", axis=1, tiled=True)
    preact = jnp.dot(aggregate_full, weight, preferred_element_type=jnp.float32) + bias
    new_rows, backward_fn = jax.vjp(activate, preact)
    grad_pre = backward_fn(cotangent.astype(jnp.float32))[0].astype(jnp.bfloat16)
    weight_term = lax.dot_general(
        aggregate_full, grad_pre, (((0,), (0,)), ((), ())), preferred_element_type=jnp.float32
    )
    bias_term = jnp.sum(grad_pre.astype(jnp.float32), axis=0)
    grad_weight, grad_bias = summed(weight_term, bias_term, count)
    return (new_rows.astype(jnp.bfloat16), grad_weight, grad_bias)


def solution(mesh):
    placed = (
        P("dom", "feat"),
        P("dom", None, None),
        P("dom", None, None, None, None),
        P("dom", None, None),
        P("dom", None, None),
        P("dom", None),
        P("dom", None),
        P(None, "feat"),
        P("feat"),
        P("dom", "feat"),
    )
    return jax.shard_map(
        per_device,
        mesh=mesh,
        in_specs=placed,
        out_specs=(P("dom", "feat"), P(None, "feat"), P("feat")),
        check_vma=False,
    )
```

time: 83.3 us -> 69.8 us (0.84)
  waiting for transfers between devices: 44.9 us -> 31.4 us
  local copies, waits for them, and re-layouts: 7.68 us -> 3.92 us
  starting transfers between devices: 20.1 us -> 22.7 us
  Pallas kernels: 5.52 us -> 6.36 us
    ppermute x16, waiting for transfers between devices: 36.6 us -> 23 us  [partner(): return lax.ppermute(block, 'dom', [(i, i ^ bits) for i in range(count)])]
    ppermute x16, starting transfers between devices: 18.4 us -> 21.2 us  [partner(): return lax.ppermute(block, 'dom', [(i, i ^ bits) for i in range(count)])]
    unnamed x20 -> x22, local copies, waits for them, and re-layouts: 6.33 us -> 3.89 us
    pallas_call x3 -> x4, Pallas kernels: 4.35 us -> 5.14 us  [the longest x1 2.55 us: begin_sum(): pl.pallas_call(functools.partial(begin_kernel, count), out_shape=[jax.Sha...]
  transfers between devices with their start and end apart: 17 -> 17, of which waited for: 10 -> 9; matrix products, arithmetic and copies ran while one was open for 2% -> 0% of each run, Pallas kernels for 6% -> 7%
where the time goes in v2:
time: 69.8 us; the launch traced here: 69.6 us
  waiting for transfers between devices  31.4 us (45%)
  starting transfers between devices  22.7 us (33%)
  Pallas kernels  6.36 us (9%)
  local copies, waits for them, and re-layouts  3.92 us (6%)
  blocking collectives  2.18 us (3%)
  matrix products  1.68 us (2%)
  between operations  0.96 us (1%)
    ppermute x16, waiting for transfers between devices, partner(): return lax.ppermute(block, 'dom', [(i, i ^ bits) for i in range(count)])  23 us
    ppermute x16, starting transfers between devices, partner(): return lax.ppermute(block, 'dom', [(i, i ^ bits) for i in range(count)])  21.2 us
    ppermute x1, waiting for transfers between devices, passed_along(): lax.ppermute(block, axis, [((i - distance) % count, i) for i in range(cou...  8.48 us
    unnamed x22, local copies, waits for them, and re-layouts  3.89 us
    pallas_call x1, Pallas kernels, begin_sum(): pl.pallas_call(functools.partial(begin_kernel, count), out_shape=[jax.Sha...  2.55 us
    all_gather x1, blocking collectives, per_device(): aggregate_full = lax.all_gather(aggregate, 'feat', axis=1, tiled=True)  2.18 us
    pallas_call x2, Pallas kernels, tile_sum(): pl.pallas_call(functools.partial(sum_kernel, members, cap, last), out_sha...  1.92 us
    ppermute x1, starting transfers between devices, passed_along(): lax.ppermute(block, axis, [((i - distance) % count, i) for i in range(cou...  1.54 us
  transfers between devices with their start and end apart: 17, of which 9 were waited for; matrix products, arithmetic and copies ran while one was open for 0% of the time, Pallas kernels for 7%

profile of v2, /device:TPU:0, one launch (start us, length us, event | category | flops | bytes accessed | tf_op | source)
XLA Modules:
  0.0 69.6 jit_solution(7201815588802448840)
XLA Ops:
  0.6 4.1 %collective-permute-start = (bf16[8,128,128]{2,1,0:T(8,128)(2,1)}, bf16[8,128,128]{2,1,0:T(8,128)(2,1)S(1)}, u32[]{:S(2)}, u32[]{:S(2)}) collective-permute-start(bf16[8,128,128]{2,1,0:T(8,128)(2,1)} %bitcast.32), channel_id=1, source_target_pairs={{0,16},{2,18},{4,20},{6,22},{8,24},{10,26},{12,28},{14,30},{16,0},... | collective-permute-start | bytes 786440 | tf_op jit(solution)/shard_map/ppermute | solution.py:18
  4.8 1.6 %collective-permute-start.8 = (bf16[8,128,128]{2,1,0:T(8,128)(2,1)}, bf16[8,128,128]{2,1,0:T(8,128)(2,1)S(1)}, u32[]{:S(2)}, u32[]{:S(2)}) collective-permute-start(bf16[8,128,128]{2,1,0:T(8,128)(2,1)} %bitcast.33), channel_id=1, source_target_pairs={{0,8},{2,10},{4,12},{6,14},{8,0},{10,2},{12,4},{14,6},{16,24},{18,... | collective-permute-start | bytes 786440 | tf_op jit(solution)/shard_map/ppermute | solution.py:18
  6.3 1.5 %collective-permute-start.1 = (s32[2,16]{1,0:T(2,128)}, s32[2,16]{1,0:T(2,128)S(1)}, u32[]{:S(2)}, u32[]{:S(2)}) collective-permute-start(s32[2,16]{1,0:T(2,128)} %bitcast.37), channel_id=1, source_target_pairs={{0,2},{2,0},{4,6},{6,4},{8,10},{10,8},{12,14},{14,12},{16,18},{18,... | collective-permute-start | bytes 392 | tf_op jit(solution)/shard_map/ppermute | solution.py:18
  7.8 1.5 %collective-permute-start.2 = (s32[2,16]{1,0:T(2,128)}, s32[2,16]{1,0:T(2,128)S(1)}, u32[]{:S(2)}, u32[]{:S(2)}) collective-permute-start(s32[2,16]{1,0:T(2,128)} %bitcast.38), channel_id=1, source_target_pairs={{0,4},{2,6},{4,0},{6,2},{8,12},{10,14},{12,8},{14,10},{16,20},{18,... | collective-permute-start | bytes 392 | tf_op jit(solution)/shard_map/ppermute | solution.py:18
  10.8 1.6 %copy-done.4 = bf16[64,128,128]{2,1,0:T(8,128)(2,1)S(1)} copy-done((bf16[64,128,128]{2,1,0:T(8,128)(2,1)S(1)}, bf16[64,128,128]{2,1,0:T(8,128)(2,1)}, u32[]{:S(2)}) %copy-start.4) | copy-done | bytes 2097176
  13.7 2.5 %shard_map.121.refs_10_ = f32[16,128,128]{2,1,0:T(8,128)S(1)} custom-call(s32[1,64]{1,0:T(1,128)S(1)} %copy-done.7, s32[1,64]{1,0:T(1,128)S(1)} %copy-done.8, bf16[64,128,128]{2,1,0:T(8,128)(2,1)S(1)} %copy-done.4, bf16[8,128,128]{2,1,0:T(8,128)(2,1)S(1)} %bitcast.34), custom_call_target="tpu_custom_call" | custom-call | tf_op jit(solution)/shard_map/pallas_call | solution.py:64
  18.3 1.6 %collective-permute-start.10 = (bf16[6,128,128]{2,1,0:T(8,128)(2,1)S(1)}, bf16[6,128,128]{2,1,0:T(8,128)(2,1)S(1)}, u32[]{:S(2)}, u32[]{:S(2)}) collective-permute-start(bf16[6,128,128]{2,1,0:T(8,128)(2,1)S(1)} %get-tuple-element.26), channel_id=1, source_target_pairs={{0,4},{2,6},{4,0},{6,2},{8,12},{10,14},{12,8},{14,10},{16,20},{18,... | collective-permute-start | bytes 589832 | tf_op jit(solution)/shard_map/ppermute | solution.py:18
  19.9 1.4 %collective-permute-start.11 = (bf16[6,128,128]{2,1,0:T(8,128)(2,1)S(1)}, bf16[6,128,128]{2,1,0:T(8,128)(2,1)S(1)}, u32[]{:S(2)}, u32[]{:S(2)}) collective-permute-start(bf16[6,128,128]{2,1,0:T(8,128)(2,1)S(1)} %get-tuple-element.27), channel_id=1, source_target_pairs={{0,6},{2,4},{4,2},{6,0},{8,14},{10,12},{12,10},{14,8},{16,22},{18,... | collective-permute-start | bytes 589832 | tf_op jit(solution)/shard_map/ppermute | solution.py:18
  21.9 2.5 %collective-permute-done.4.refs_3_.refs_4_ = bf16[8,128,128]{2,1,0:T(8,128)(2,1)S(1)} collective-permute-done((bf16[8,128,128]{2,1,0:T(8,128)(2,1)S(1)}, bf16[8,128,128]{2,1,0:T(8,128)(2,1)S(1)}, u32[]{:S(2)}, u32[]{:S(2)}) %collective-permute-start.4) | collective-permute-done | bytes 262176 | tf_op jit(solution)/shard_map/ppermute | solution.py:18
  25.0 1.3 %collective-permute-start.5 = (bf16[2,128,128]{2,1,0:T(8,128)(2,1)S(1)}, bf16[2,128,128]{2,1,0:T(8,128)(2,1)S(1)}, u32[]{:S(2)}, u32[]{:S(2)}) collective-permute-start(bf16[2,128,128]{2,1,0:T(8,128)(2,1)S(1)} %get-tuple-element.22), channel_id=1, source_target_pairs={{0,2},{2,0},{4,6},{6,4},{8,10},{10,8},{12,14},{14,12},{16,18},{18,... | collective-permute-start | bytes 196616 | tf_op jit(solution)/shard_map/ppermute | solution.py:18
  26.4 1.5 %collective-permute-start.6 = (bf16[2,128,128]{2,1,0:T(8,128)(2,1)S(1)}, bf16[2,128,128]{2,1,0:T(8,128)(2,1)S(1)}, u32[]{:S(2)}, u32[]{:S(2)}) collective-permute-start(bf16[2,128,128]{2,1,0:T(8,128)(2,1)S(1)} %get-tuple-element.23), channel_id=1, source_target_pairs={{0,4},{2,6},{4,0},{6,2},{8,12},{10,14},{12,8},{14,10},{16,20},{18,... | collective-permute-start | bytes 196616 | tf_op jit(solution)/shard_map/ppermute | solution.py:18
  27.9 2.0 %collective-permute-done.10.refs_8_ = bf16[6,128,128]{2,1,0:T(8,128)(2,1)S(1)} collective-permute-done((bf16[6,128,128]{2,1,0:T(8,128)(2,1)S(1)}, bf16[6,128,128]{2,1,0:T(8,128)(2,1)S(1)}, u32[]{:S(2)}, u32[]{:S(2)}) %collective-permute-start.10) | collective-permute-done | bytes 196640 | tf_op jit(solution)/shard_map/ppermute | solution.py:18
  29.9 2.4 %collective-permute-start.7 = (bf16[2,128,128]{2,1,0:T(8,128)(2,1)S(1)}, bf16[2,128,128]{2,1,0:T(8,128)(2,1)S(1)}, u32[]{:S(2)}, u32[]{:S(2)}) collective-permute-start(bf16[2,128,128]{2,1,0:T(8,128)(2,1)S(1)} %get-tuple-element.24), channel_id=1, source_target_pairs={{0,6},{2,4},{4,2},{6,0},{8,14},{10,12},{12,10},{14,8},{16,22},{18,... | collective-permute-start | bytes 196616 | tf_op jit(solution)/shard_map/ppermute | solution.py:18
  32.4 1.1 %shard_map.124.refs_8_ = f32[16,128,128]{2,1,0:T(8,128)S(1)} custom-call(s32[1]{0:T(128)} %bitcast.me_ref.refs_0_, s32[2,16]{1,0:T(2,128)S(1)} %bitcast.40, s32[2,16]{1,0:T(2,128)S(1)} %bitcast.42, bf16[32,128,128]{2,1,0:T(8,128)(2,1)S(1)} %bitcast.30, bf16[8,128,128]{2,1,0:T(8,128)(2,1)S(1)} %bitcast.36, ...), custom_call_target="tpu_custom_call" | custom-call | tf_op jit(solution)/shard_map/pallas_call | solution.py:115
  33.5 1.6 %collective-permute-done.7.refs_7_ = bf16[2,128,128]{2,1,0:T(8,128)(2,1)S(1)} collective-permute-done((bf16[2,128,128]{2,1,0:T(8,128)(2,1)S(1)}, bf16[2,128,128]{2,1,0:T(8,128)(2,1)S(1)}, u32[]{:S(2)}, u32[]{:S(2)}) %collective-permute-start.7) | collective-permute-done | bytes 65568 | tf_op jit(solution)/shard_map/ppermute | solution.py:18
  35.9 1.5 %collective-permute-start.12 = (bf16[8,128,128]{2,1,0:T(8,128)(2,1)S(1)}, bf16[8,128,128]{2,1,0:T(8,128)(2,1)S(1)}, u32[]{:S(2)}, u32[]{:S(2)}) collective-permute-start(bf16[8,128,128]{2,1,0:T(8,128)(2,1)S(1)} %get-tuple-element.30), channel_id=1, source_target_pairs={{30,0},{0,2},{2,4},{4,6},{6,8},{8,10},{10,12},{12,14},{14,16},{16,... | collective-permute-start | bytes 786440 | tf_op jit(solution)/shard_map/ppermute | solution.py:23
  37.4 8.5 %collective-permute-done.12 = bf16[8,128,128]{2,1,0:T(8,128)(2,1)S(1)} collective-permute-done((bf16[8,128,128]{2,1,0:T(8,128)(2,1)S(1)}, bf16[8,128,128]{2,1,0:T(8,128)(2,1)S(1)}, u32[]{:S(2)}, u32[]{:S(2)}) %collective-permute-start.12) | collective-permute-done | bytes 262176 | tf_op jit(solution)/shard_map/ppermute | solution.py:23
  46.0 2.2 %all_gather.3 = bf16[1024,256]{1,0:T(8,128)(2,1)S(1)} all-gather(bf16[1024,128]{1,0:T(8,128)(2,1)S(1)} %bitcast.44), channel_id=1, replica_groups=mesh['dom'=16,'feat'=2] {'feat'}, dimensions={1}, use_global_device_ids=true | all-gather | bytes 786432 | tf_op jit(solution)/shard_map/all_gather | solution.py:243
  48.2 1.3 %convert_reduce_fusion = (f32[128]{0:T(128)S(1)}, bf16[1024,128]{1,0:T(8,128)(2,1)S(1)}, bf16[1024,128]{1,0:T(8,128)(2,1)}) fusion(bf16[1024,128]{1,0:T(8,128)(2,1)S(1)} %copy-done.9, f32[128]{0:T(128)S(1)} %copy-done.10, bf16[1024,256]{1,0:T(8,128)(2,1)S(1)} %all_gather.3, bf16[256,128]{1,0:T(8,128)(2,1)S(1)} %copy-done), kind=kOutput, calls=%fused_computation.16 | convolution fusion | flops 70516608 | bytes 1377280 | tf_op jit(solution)/shard_map/dot_general | solution.py:244
  50.0 4.3 %collective-permute-done.13 = bf16[272,128]{1,0:T(8,128)(2,1)S(1)} collective-permute-done((bf16[272,128]{1,0:T(8,128)(2,1)S(1)}, bf16[272,128]{1,0:T(8,128)(2,1)S(1)}, u32[]{:S(2)}, u32[]{:S(2)}) %collective-permute-start.13) | collective-permute-done | bytes 69664 | tf_op jit(solution)/shard_map/ppermute | solution.py:18
  54.5 4.3 %collective-permute-done.14 = bf16[272,128]{1,0:T(8,128)(2,1)S(1)} collective-permute-done((bf16[272,128]{1,0:T(8,128)(2,1)S(1)}, bf16[272,128]{1,0:T(8,128)(2,1)S(1)}, u32[]{:S(2)}, u32[]{:S(2)}) %collective-permute-start.14) | collective-permute-done | bytes 69664 | tf_op jit(solution)/shard_map/ppermute | solution.py:18
  59.0 4.3 %collective-permute-done.15 = bf16[272,128]{1,0:T(8,128)(2,1)S(1)} collective-permute-done((bf16[272,128]{1,0:T(8,128)(2,1)S(1)}, bf16[272,128]{1,0:T(8,128)(2,1)S(1)}, u32[]{:S(2)}, u32[]{:S(2)}) %collective-permute-start.15) | collective-permute-done | bytes 69664 | tf_op jit(solution)/shard_map/ppermute | solution.py:18
  63.4 2.2 %collective-permute-start.16 = (bf16[272,128]{1,0:T(8,128)(2,1)S(1)}, bf16[272,128]{1,0:T(8,128)(2,1)S(1)}, u32[]{:S(2)}, u32[]{:S(2)}) collective-permute-start(bf16[272,128]{1,0:T(8,128)(2,1)S(1)} %pad_maximum_fusion.3), channel_id=1, source_target_pairs={{0,16},{2,18},{4,20},{6,22},{8,24},{10,26},{12,28},{14,30},{16,0},... | collective-permute-start | bytes 208904 | tf_op jit(solution)/shard_map/ppermute | solution.py:18
  65.6 3.2 %collective-permute-done.16.refs_1_ = bf16[272,128]{1,0:T(8,128)(2,1)S(1)} collective-permute-done((bf16[272,128]{1,0:T(8,128)(2,1)S(1)}, bf16[272,128]{1,0:T(8,128)(2,1)S(1)}, u32[]{:S(2)}, u32[]{:S(2)}) %collective-permute-start.16) | collective-permute-done | bytes 69664 | tf_op jit(solution)/shard_map/ppermute | solution.py:18
  (67 shorter events, 8.4 us)
Async XLA Ops:
  0.6 47.6 %copy-start = (bf16[256,128]{1,0:T(8,128)(2,1)S(1)}, bf16[256,128]{1,0:T(8,128)(2,1)}, u32[]{:S(2)}) copy-start(bf16[256,128]{1,0:T(8,128)(2,1)} %param.17) | copy-start | bytes 196612
  0.6 16.3 %collective-permute-start = (bf16[8,128,128]{2,1,0:T(8,128)(2,1)}, bf16[8,128,128]{2,1,0:T(8,128)(2,1)S(1)}, u32[]{:S(2)}, u32[]{:S(2)}) collective-permute-start(bf16[8,128,128]{2,1,0:T(8,128)(2,1)} %bitcast.32), channel_id=1, source_target_pairs={{0,16},{2,18},{4,20},{6,22},{8,24},{10,26},{12,28},{14,30},{16,0},... | collective-permute-start | bytes 786440 | tf_op jit(solution)/shard_map/ppermute | solution.py:18
  4.8 13.0 %collective-permute-start.8 = (bf16[8,128,128]{2,1,0:T(8,128)(2,1)}, bf16[8,128,128]{2,1,0:T(8,128)(2,1)S(1)}, u32[]{:S(2)}, u32[]{:S(2)}) collective-permute-start(bf16[8,128,128]{2,1,0:T(8,128)(2,1)} %bitcast.33), channel_id=1, source_target_pairs={{0,8},{2,10},{4,12},{6,14},{8,0},{10,2},{12,4},{14,6},{16,24},{18,... | collective-permute-start | bytes 786440 | tf_op jit(solution)/shard_map/ppermute | solution.py:18
  6.3 26.0 %copy-start.5 = (s32[1,16,2]{1,2,0:T(2,128)S(1)}, s32[1,16,2]{1,2,0:T(2,128)}, u32[]{:S(2)}) copy-start(s32[1,16,2]{1,2,0:T(2,128)} %param.11) | copy-start | bytes 388
  6.3 26.0 %copy-start.1 = (bf16[1,16,2,128,128]{4,3,2,1,0:T(8,128)(2,1)S(1)}, bf16[1,16,2,128,128]{4,3,2,1,0:T(8,128)(2,1)}, u32[]{:S(2)}) copy-start(bf16[1,16,2,128,128]{4,3,2,1,0:T(8,128)(2,1)} %param.12) | copy-start | bytes 3145732
  6.3 9.9 %collective-permute-start.1 = (s32[2,16]{1,0:T(2,128)}, s32[2,16]{1,0:T(2,128)S(1)}, u32[]{:S(2)}, u32[]{:S(2)}) collective-permute-start(s32[2,16]{1,0:T(2,128)} %bitcast.37), channel_id=1, source_target_pairs={{0,2},{2,0},{4,6},{6,4},{8,10},{10,8},{12,14},{14,12},{16,18},{18,... | collective-permute-start | bytes 392 | tf_op jit(solution)/shard_map/ppermute | solution.py:18
  7.8 8.4 %collective-permute-start.2 = (s32[2,16]{1,0:T(2,128)}, s32[2,16]{1,0:T(2,128)S(1)}, u32[]{:S(2)}, u32[]{:S(2)}) collective-permute-start(s32[2,16]{1,0:T(2,128)} %bitcast.38), channel_id=1, source_target_pairs={{0,4},{2,6},{4,0},{6,2},{8,12},{10,14},{12,8},{14,10},{16,20},{18,... | collective-permute-start | bytes 392 | tf_op jit(solution)/shard_map/ppermute | solution.py:18
  9.3 6.9 %collective-permute-start.3 = (s32[2,16]{1,0:T(2,128)}, s32[2,16]{1,0:T(2,128)S(1)}, u32[]{:S(2)}, u32[]{:S(2)}) collective-permute-start(s32[2,16]{1,0:T(2,128)} %bitcast.39), channel_id=1, source_target_pairs={{0,6},{2,4},{4,2},{6,0},{8,14},{10,12},{12,10},{14,8},{16,22},{18,... | collective-permute-start | bytes 392 | tf_op jit(solution)/shard_map/ppermute | solution.py:18
  13.7 4.0 %copy-start.3 = (bf16[1024,128]{1,0:T(8,128)(2,1)S(1)}, bf16[1024,128]{1,0:T(8,128)(2,1)}, u32[]{:S(2)}) copy-start(bf16[1024,128]{1,0:T(8,128)(2,1)} %param.10) | copy-start | bytes 786436
  13.7 18.7 %copy-start.6 = (s32[1,16,2]{1,2,0:T(2,128)S(1)}, s32[1,16,2]{1,2,0:T(2,128)}, u32[]{:S(2)}) copy-start(s32[1,16,2]{1,2,0:T(2,128)} %param.13) | copy-start | bytes 388
  17.0 7.4 %collective-permute-start.4 = (bf16[8,128,128]{2,1,0:T(8,128)(2,1)S(1)}, bf16[8,128,128]{2,1,0:T(8,128)(2,1)S(1)}, u32[]{:S(2)}, u32[]{:S(2)}) collective-permute-start(bf16[8,128,128]{2,1,0:T(8,128)(2,1)S(1)} %collective-permute-done.refs_5_.refs_6_), channel_id=1, source_target_pairs={{0,8},{2,10},{4,12},{6,14},{8,0},{10,2},{12,4},{14,6},{16,24},{18,... | collective-permute-start | bytes 786440 | tf_op jit(solution)/shard_map/ppermute | solution.py:18
  18.3 11.5 %collective-permute-start.10 = (bf16[6,128,128]{2,1,0:T(8,128)(2,1)S(1)}, bf16[6,128,128]{2,1,0:T(8,128)(2,1)S(1)}, u32[]{:S(2)}, u32[]{:S(2)}) collective-permute-start(bf16[6,128,128]{2,1,0:T(8,128)(2,1)S(1)} %get-tuple-element.26), channel_id=1, source_target_pairs={{0,4},{2,6},{4,0},{6,2},{8,12},{10,14},{12,8},{14,10},{16,20},{18,... | collective-permute-start | bytes 589832 | tf_op jit(solution)/shard_map/ppermute | solution.py:18
  19.9 12.4 %collective-permute-start.11 = (bf16[6,128,128]{2,1,0:T(8,128)(2,1)S(1)}, bf16[6,128,128]{2,1,0:T(8,128)(2,1)S(1)}, u32[]{:S(2)}, u32[]{:S(2)}) collective-permute-start(bf16[6,128,128]{2,1,0:T(8,128)(2,1)S(1)} %get-tuple-element.27), channel_id=1, source_target_pairs={{0,6},{2,4},{4,2},{6,0},{8,14},{10,12},{12,10},{14,8},{16,22},{18,... | collective-permute-start | bytes 589832 | tf_op jit(solution)/shard_map/ppermute | solution.py:18
  21.4 11.0 %collective-permute-start.9 = (bf16[6,128,128]{2,1,0:T(8,128)(2,1)S(1)}, bf16[6,128,128]{2,1,0:T(8,128)(2,1)S(1)}, u32[]{:S(2)}, u32[]{:S(2)}) collective-permute-start(bf16[6,128,128]{2,1,0:T(8,128)(2,1)S(1)} %get-tuple-element.25), channel_id=1, source_target_pairs={{0,2},{2,0},{4,6},{6,4},{8,10},{10,8},{12,14},{14,12},{16,18},{18,... | collective-permute-start | bytes 589832 | tf_op jit(solution)/shard_map/ppermute | solution.py:18
  25.0 8.4 %collective-permute-start.5 = (bf16[2,128,128]{2,1,0:T(8,128)(2,1)S(1)}, bf16[2,128,128]{2,1,0:T(8,128)(2,1)S(1)}, u32[]{:S(2)}, u32[]{:S(2)}) collective-permute-start(bf16[2,128,128]{2,1,0:T(8,128)(2,1)S(1)} %get-tuple-element.22), channel_id=1, source_target_pairs={{0,2},{2,0},{4,6},{6,4},{8,10},{10,8},{12,14},{14,12},{16,18},{18,... | collective-permute-start | bytes 196616 | tf_op jit(solution)/shard_map/ppermute | solution.py:18
  26.4 7.1 %collective-permute-start.6 = (bf16[2,128,128]{2,1,0:T(8,128)(2,1)S(1)}, bf16[2,128,128]{2,1,0:T(8,128)(2,1)S(1)}, u32[]{:S(2)}, u32[]{:S(2)}) collective-permute-start(bf16[2,128,128]{2,1,0:T(8,128)(2,1)S(1)} %get-tuple-element.23), channel_id=1, source_target_pairs={{0,4},{2,6},{4,0},{6,2},{8,12},{10,14},{12,8},{14,10},{16,20},{18,... | collective-permute-start | bytes 196616 | tf_op jit(solution)/shard_map/ppermute | solution.py:18
  29.9 5.2 %collective-permute-start.7 = (bf16[2,128,128]{2,1,0:T(8,128)(2,1)S(1)}, bf16[2,128,128]{2,1,0:T(8,128)(2,1)S(1)}, u32[]{:S(2)}, u32[]{:S(2)}) collective-permute-start(bf16[2,128,128]{2,1,0:T(8,128)(2,1)S(1)} %get-tuple-element.24), channel_id=1, source_target_pairs={{0,6},{2,4},{4,2},{6,0},{8,14},{10,12},{12,10},{14,8},{16,22},{18,... | collective-permute-start | bytes 196616 | tf_op jit(solution)/shard_map/ppermute | solution.py:18
  33.4 14.8 %copy-start.9 = (bf16[1024,128]{1,0:T(8,128)(2,1)S(1)}, bf16[1024,128]{1,0:T(8,128)(2,1)}, u32[]{:S(2)}) copy-start(bf16[1024,128]{1,0:T(8,128)(2,1)} %param.19) | copy-start | bytes 786436
  33.4 14.8 %copy-start.10 = (f32[128]{0:T(128)S(1)}, f32[128]{0:T(128)}, u32[]{:S(2)}) copy-start(f32[128]{0:T(128)} %param.18) | copy-start | bytes 1540
  35.9 10.0 %collective-permute-start.12 = (bf16[8,128,128]{2,1,0:T(8,128)(2,1)S(1)}, bf16[8,128,128]{2,1,0:T(8,128)(2,1)S(1)}, u32[]{:S(2)}, u32[]{:S(2)}) collective-permute-start(bf16[8,128,128]{2,1,0:T(8,128)(2,1)S(1)} %get-tuple-element.30), channel_id=1, source_target_pairs={{30,0},{0,2},{2,4},{4,6},{6,8},{8,10},{10,12},{12,14},{14,16},{16,... | collective-permute-start | bytes 786440 | tf_op jit(solution)/shard_map/ppermute | solution.py:23
  49.9 4.4 %collective-permute-start.13 = (bf16[272,128]{1,0:T(8,128)(2,1)S(1)}, bf16[272,128]{1,0:T(8,128)(2,1)S(1)}, u32[]{:S(2)}, u32[]{:S(2)}) collective-permute-start(bf16[272,128]{1,0:T(8,128)(2,1)S(1)} %pad_maximum_fusion), channel_id=1, source_target_pairs={{0,2},{2,0},{4,6},{6,4},{8,10},{10,8},{12,14},{14,12},{16,18},{18,... | collective-permute-start | bytes 208904 | tf_op jit(solution)/shard_map/ppermute | solution.py:18
  54.4 4.4 %collective-permute-start.14 = (bf16[272,128]{1,0:T(8,128)(2,1)S(1)}, bf16[272,128]{1,0:T(8,128)(2,1)S(1)}, u32[]{:S(2)}, u32[]{:S(2)}) collective-permute-start(bf16[272,128]{1,0:T(8,128)(2,1)S(1)} %pad_maximum_fusion.1), channel_id=1, source_target_pairs={{0,4},{2,6},{4,0},{6,2},{8,12},{10,14},{12,8},{14,10},{16,20},{18,... | collective-permute-start | bytes 208904 | tf_op jit(solution)/shard_map/ppermute | solution.py:18
  58.9 4.4 %collective-permute-start.15 = (bf16[272,128]{1,0:T(8,128)(2,1)S(1)}, bf16[272,128]{1,0:T(8,128)(2,1)S(1)}, u32[]{:S(2)}, u32[]{:S(2)}) collective-permute-start(bf16[272,128]{1,0:T(8,128)(2,1)S(1)} %pad_maximum_fusion.2), channel_id=1, source_target_pairs={{0,8},{2,10},{4,12},{6,14},{8,0},{10,2},{12,4},{14,6},{16,24},{18,... | collective-permute-start | bytes 208904 | tf_op jit(solution)/shard_map/ppermute | solution.py:18
  63.4 5.5 %collective-permute-start.16 = (bf16[272,128]{1,0:T(8,128)(2,1)S(1)}, bf16[272,128]{1,0:T(8,128)(2,1)S(1)}, u32[]{:S(2)}, u32[]{:S(2)}) collective-permute-start(bf16[272,128]{1,0:T(8,128)(2,1)S(1)} %pad_maximum_fusion.3), channel_id=1, source_target_pairs={{0,16},{2,18},{4,20},{6,22},{8,24},{10,26},{12,28},{14,30},{16,0},... | collective-permute-start | bytes 208904 | tf_op jit(solution)/shard_map/ppermute | solution.py:18
  (4 other events, 3.9 us)

commit v3 on v2

v3 whole, which is shorter than its diff:
```python
import functools

import jax
import jax.numpy as jnp
from jax import lax
from jax.experimental import pallas as pl
from jax.experimental.pallas import tpu as pltpu
from jax.sharding import PartitionSpec as P

PEERS = 4
VMEM = pl.BlockSpec(memory_space=pltpu.VMEM)
HBM = pl.BlockSpec(memory_space=pltpu.HBM)
SMEM = pl.BlockSpec(memory_space=pltpu.SMEM)
SLABS = 2
PARAMS = pltpu.CompilerParams(vmem_limit_bytes=48 * 1024 * 1024)


def partner(block, bits):
    count = lax.axis_size("dom")
    return lax.ppermute(block, "dom", [(i, i ^ bits) for i in range(count)])


def passed_along(block, axis, distance):
    count = lax.axis_size(axis)
    return lax.ppermute(block, axis, [((i - distance) % count, i) for i in range(count)])


def select_kernel(members, cap, me_ref, *refs):
    asked, held, out = refs[: PEERS - 1], refs[PEERS - 1 : -(PEERS - 1)], refs[-(PEERS - 1) :]
    for at, member in enumerate(members):
        owner = me_ref[0] ^ (member * PEERS)
        for j in range(PEERS - 1):
            for c in range(cap):
                wanted = jnp.maximum(asked[j][c, owner], 0)
                out[j][at * cap + c] = held[at][wanted]


def select_blocks(me, asked, members, held, cap):
    size = held[0].shape[1:]
    shape = jax.ShapeDtypeStruct((len(members) * cap, *size), held[0].dtype)
    return pl.pallas_call(
        functools.partial(select_kernel, members, cap),
        out_shape=[shape] * (PEERS - 1),
        in_specs=[SMEM] * PEERS + [VMEM] * len(members),
        out_specs=[VMEM] * (PEERS - 1),
        compiler_params=PARAMS,
    )(me, *asked, *held)


def begin_kernel(chunks, *refs):
    arrays, acc, held, sems = refs[:4], refs[4], refs[5:9], refs[9]
    src_ref, dst_ref, blocks_ref, tiles_ref = held
    per_chunk = tiles_ref.shape[0] // chunks
    whole = [pltpu.make_async_copy(arrays[i], held[i], sems.at[i]) for i in range(3)]
    parts = []
    for i in range(chunks):
        rows = pl.ds(i * per_chunk, per_chunk)
        parts.append(
            pltpu.make_async_copy(arrays[3].at[rows], tiles_ref.at[rows], sems.at[3 + i])
        )
    for copy in whole + parts:
        copy.start()
    acc[...] = jnp.zeros_like(acc)
    for copy in whole:
        copy.wait()
    for i in range(chunks):
        parts[i].wait()
        for k in range(i * per_chunk, (i + 1) * per_chunk):
            product = jnp.dot(
                tiles_ref[k], blocks_ref[src_ref[0, k]], preferred_element_type=jnp.float32
            )
            dst = dst_ref[0, k]
            acc[dst] = acc[dst] + product


def begin_sum(src, dst, tiles, blocks, row_count):
    count, size, _ = tiles.shape
    chunks = 8
    return pl.pallas_call(
        functools.partial(begin_kernel, chunks),
        out_shape=[jax.ShapeDtypeStruct((row_count, size, blocks.shape[-1]), jnp.float32)],
        in_specs=[HBM] * 4,
        out_specs=[VMEM],
        scratch_shapes=[
            pltpu.SMEM(src.shape, src.dtype),
            pltpu.SMEM(dst.shape, dst.dtype),
            pltpu.VMEM(blocks.shape, blocks.dtype),
            pltpu.VMEM(tiles.shape, tiles.dtype),
            pltpu.SemaphoreType.DMA((3 + chunks,)),
        ],
        compiler_params=PARAMS,
    )(*[pltpu.with_memory_space_constraint(x, pltpu.HBM) for x in (src, dst, blocks, tiles)])


def sum_kernel(sources, cap, last, me_ref, wanted_ref, dst_ref, tiles_ref, acc_in, *refs):
    acc = refs[-1]
    acc[...] = acc_in[...]
    for bits, at, start in sources:
        owner = me_ref[0] ^ bits
        for c in range(cap):
            wanted = wanted_ref[c, owner]
            block = refs[at][jnp.maximum(wanted, 0) if start is None else start + c]
            block = jnp.where(wanted >= 0, block, jnp.zeros_like(block))
            product = jnp.dot(
                tiles_ref[owner * cap + c], block, preferred_element_type=jnp.float32
            )
            dst = dst_ref[c, owner]
            acc[dst] = acc[dst] + product
    if last:
        own_ref, *next_refs = refs[-2 - SLABS : -1]
        at = own_ref.shape[0]
        own_ref[...] = acc[:at]
        for next_ref in next_refs:
            depth = next_ref.shape[0]
            next_ref[...] = acc[at : at + depth].astype(next_ref.dtype)
            at += depth


def tile_sum(shared, acc, sources, cap, last=False):
    row_count, size, width = acc.shape
    half = (row_count // 2, size, width)
    part = (row_count // 2 // SLABS, size, width)
    arrays, places = [], []
    for bits, array, start in sources:
        known = [i for i, other in enumerate(arrays) if other is array]
        if not known:
            known = [len(arrays)]
            arrays.append(array)
        places.append((bits, known[0], start))
    scratch = []
    out_shape = [jax.ShapeDtypeStruct(acc.shape, jnp.float32)]
    if last:
        out_shape = [jax.ShapeDtypeStruct(half, jnp.float32)]
        out_shape += [jax.ShapeDtypeStruct(part, jnp.bfloat16)] * SLABS
        scratch = [pltpu.VMEM(acc.shape, jnp.float32)]
    return pl.pallas_call(
        functools.partial(sum_kernel, places, cap, last),
        out_shape=out_shape,
        in_specs=[SMEM] * 3 + [VMEM] * (2 + len(arrays)),
        out_specs=[VMEM] * len(out_shape),
        scratch_shapes=scratch,
        compiler_params=PARAMS,
    )(*shared, acc, *arrays)


def dense_kernel(start, first, last, *refs):
    mine_ref, other_ref, weight_mine, weight_other, bias_ref, cot_ref = refs[:6]
    before = [] if first else refs[6:8]
    rows_ref, weight_out, bias_out = refs[6 + len(before) : 9 + len(before)]
    depth, width = mine_ref.shape
    step = min(depth, 256)
    terms = [jnp.zeros(weight_mine.shape, jnp.float32)] * 2 if first else [
        before[0][: weight_mine.shape[0]], before[0][weight_mine.shape[0] :]
    ]
    bias_sum = jnp.zeros((1, width), jnp.float32) if first else before[1][...]
    scale = 0.7978845608028654
    cubic = 0.044715
    for at in range(0, depth, step):
        mine, other = mine_ref[at : at + step], other_ref[at : at + step]
        v = (
            jnp.dot(mine, weight_mine[...], preferred_element_type=jnp.float32)
            + jnp.dot(other, weight_other[...], preferred_element_type=jnp.float32)
            + bias_ref[...]
        )
        square = v * v
        bent = jnp.tanh(scale * v * (1.0 + cubic * square))
        half = 0.5 * (1.0 + bent)
        rows_ref[at : at + step] = (v * half).astype(rows_ref.dtype)
        slope = half + 0.5 * v * (1.0 - bent * bent) * scale * (1.0 + 3.0 * cubic * square)
        cot = cot_ref[start + at : start + at + step].astype(jnp.float32)
        grad = (cot * slope).astype(jnp.bfloat16)
        bias_sum = bias_sum + jnp.sum(grad.astype(jnp.float32), axis=0, keepdims=True)
        for i, part in enumerate((mine, other)):
            terms[i] = terms[i] + lax.dot_general(
                part, grad, (((0,), (0,)), ((), ())), preferred_element_type=jnp.float32
            )
    if last:
        sent = refs[9 + len(before)]
        at = 0
        for term in terms:
            sent[at : at + width] = term.astype(sent.dtype)
            weight_out[at : at + width] = term.astype(sent.dtype).astype(jnp.float32)
            at += width
        high = bias_sum.astype(sent.dtype).astype(jnp.float32)
        low = (bias_sum - high).astype(sent.dtype).astype(jnp.float32)
        bias_out[...] = high + low
        for row in (high, low):
            sent[at : at + 8] = jnp.broadcast_to(row, (8, width)).astype(sent.dtype)
            at += 8
    else:
        weight_out[: weight_mine.shape[0]] = terms[0]
        weight_out[weight_mine.shape[0] :] = terms[1]
        bias_out[...] = bias_sum


def dense(mine, other, weights, bias, cotangent, start, before, last):
    depth, width = mine.shape
    rows = 2 * width
    out_shape = [
        jax.ShapeDtypeStruct((depth, width), jnp.bfloat16),
        jax.ShapeDtypeStruct((rows, width), jnp.float32),
        jax.ShapeDtypeStruct((1, width), jnp.float32),
    ]
    if last:
        out_shape.append(jax.ShapeDtypeStruct((rows + 16, width), jnp.bfloat16))
    return pl.pallas_call(
        functools.partial(dense_kernel, start, not before, last),
        out_shape=out_shape,
        in_specs=[VMEM] * (6 + len(before)),
        out_specs=[VMEM] * len(out_shape),
        compiler_params=PARAMS,
    )(mine, other, *weights, bias, cotangent, *before)


def rounded(value):
    return lax.reduce_precision(value, 8, 7)


def finish_kernel(feat_ref, weight_ref, bias_ref, got_ref, weight_out, bias_out):
    depth = weight_ref.shape[0]
    half = depth // 2
    feat = feat_ref[0]
    for at, place in ((0, feat), (half, 1 - feat)):
        weight_out[pl.ds(pl.multiple_of(place * half, half), half)] = weight_ref[
            at : at + half
        ] + got_ref[at : at + half].astype(jnp.float32)
    rows = got_ref[depth:].astype(jnp.float32)
    bias_out[...] = bias_ref[...] + (rows[:1] + rows[8:9])


def summed(weight_term, bias_term, sent, count, feat):
    depth, width = weight_term.shape
    bits = 1
    while True:
        raw = partner(sent, bits)
        bits *= 2
        if bits >= count:
            break
        got = raw.astype(jnp.float32)
        weight_term = rounded(weight_term + got[:depth])
        bias_term = bias_term + (got[depth : depth + 1] + got[depth + 8 : depth + 9])
        high = rounded(bias_term)
        low = rounded(bias_term - high)
        bias_term = high + low
        rows = [jnp.broadcast_to(row, (8, width)) for row in (high, low)]
        sent = jnp.concatenate([weight_term, *rows]).astype(jnp.bfloat16)
    return pl.pallas_call(
        finish_kernel,
        out_shape=[
            jax.ShapeDtypeStruct((depth, width), jnp.float32),
            jax.ShapeDtypeStruct((1, width), jnp.float32),
        ],
        in_specs=[SMEM] + [VMEM] * 3,
        out_specs=[VMEM] * 2,
        compiler_params=PARAMS,
    )(feat, weight_term, bias_term, raw)


def per_device(
    history,
    pull_list,
    remote_tiles,
    remote_dst,
    local_tiles,
    local_src,
    local_dst,
    weight,
    bias,
    cotangent,
):
    count = lax.axis_size("dom")
    columns = count // PEERS
    cap = pull_list.shape[2]
    half_width = history.shape[1]
    block_size = local_tiles.shape[1]
    own_blocks = history.shape[0] // block_size
    row_count = 2 * own_blocks
    blocks = history.reshape(own_blocks, block_size, half_width)
    me = lax.axis_index("dom").astype(jnp.int32).reshape(1)
    wanted = pull_list[0].T
    tiles = remote_tiles.reshape(-1, block_size, block_size)
    shared = (me, wanted, remote_dst[0].T, tiles)

    def exchange(members, after, hold=None):
        arrays = [held[k] for k in members]
        if after:
            arrays[0], *_ = lax.optimization_barrier((arrays[0], *after))
        picked = list(select_blocks(me, asked, members, arrays, cap))
        for j in [3]:
            if len(members) == 1:
                picked[j - 1], _ = lax.optimization_barrier((picked[j - 1], hold))
        pulled = [partner(picked[j - 1], j) for j in range(1, PEERS)]
        sources = []
        for at, member in enumerate(members):
            sources.append((member * PEERS, held[member], None))
            for j in range(1, PEERS):
                sources.append((member * PEERS + j, pulled[j - 1], at * cap))
        return sources, pulled, picked

    held = {0: blocks}
    for member in range(columns // 2, 0, -1):
        if member & (member - 1) == 0:
            held[member] = partner(blocks, member * PEERS)
    asked = [partner(wanted, j) for j in range(1, PEERS)]
    (acc,) = begin_sum(local_src, local_dst, local_tiles, blocks, row_count)
    for member in range(1, columns):
        if member not in held:
            low = member & -member
            source, acc, *asked = lax.optimization_barrier((held[member ^ low], acc, *asked))
            held[member] = partner(source, low * PEERS)

    first, arrived, _ = exchange(list(range(columns - 1)), [])
    rest, *_ = exchange([columns - 1], [], arrived[1])
    (acc,) = tile_sum(shared, acc, first, cap)
    outs = tile_sum(shared, acc, rest, cap, last=True)
    own, *following = outs
    incoming = [passed_along(part, "dom", 1) for part in following]

    feat = lax.axis_index("feat").astype(jnp.int32).reshape(1)
    weights = [
        lax.dynamic_slice_in_dim(weight, place * half_width, half_width)
        for place in (feat[0], 1 - feat[0])
    ]
    depth = own_blocks // SLABS
    before, new_rows = [], []
    for at, part in enumerate(incoming):
        mine = (own[at * depth : (at + 1) * depth] + part.astype(jnp.float32)).astype(jnp.bfloat16)
        mine = mine.reshape(depth * block_size, half_width)
        other = passed_along(mine, "feat", 1)
        rows, *before = dense(
            mine,
            other,
            weights,
            bias[None],
            cotangent,
            at * depth * block_size,
            before,
            at == SLABS - 1,
        )
        new_rows.append(rows)
    grad_weight, grad_bias = summed(*before, count, feat)
    return (jnp.concatenate(new_rows), grad_weight, grad_bias[0])


def solution(mesh):
    placed = (
        P("dom", "feat"),
        P("dom", None, None),
        P("dom", None, None, None, None),
        P("dom", None, None),
        P("dom", None, None),
        P("dom", None),
        P("dom", None),
        P(None, "feat"),
        P("feat"),
        P("dom", "feat"),
    )
    return jax.shard_map(
        per_device,
        mesh=mesh,
        in_specs=placed,
        out_specs=(P("dom", "feat"), P(None, "feat"), P("feat")),
        check_vma=False,
    )
```

time: 69.8 us -> 66.9 us (0.958)
  local copies, waits for them, and re-layouts: 3.92 us -> 0.06 us
  waiting for transfers between devices: 31.4 us -> 33.7 us
  blocking collectives: 2.18 us -> 0 us
  matrix products: 1.68 us -> 0 us
  Pallas kernels: 6.36 us -> 7.95 us
  other arithmetic: 0.3 us -> 1.02 us
    unnamed x22 -> x14, local copies, waits for them, and re-layouts: 3.89 us -> 0.03 us
    ppermute x16, waiting for transfers between devices: 23 us -> 25.5 us  [partner(): return lax.ppermute(block, 'dom', [(i, i ^ bits) for i in range(count)])]
    all_gather x1 -> x0, blocking collectives: 2.18 us -> none  [per_device(): aggregate_full = lax.all_gather(aggregate, 'feat', axis=1, tiled=True)]
    ppermute x1 -> x4, starting transfers between devices: 1.54 us -> 3.6 us  [passed_along(): lax.ppermute(block, axis, [((i - distance) % count, i) for i in range(cou...]
    ppermute x16, starting transfers between devices: 21.2 us -> 19.5 us  [partner(): return lax.ppermute(block, 'dom', [(i, i ^ bits) for i in range(count)])]
    dot_general x2 -> x0, matrix products: 1.68 us -> none  [the longest x1 1.34 us: per_device(): jnp.dot(aggregate_full, weight, preferred_element_type=jnp.float32) + bias]
    pallas_call x4 -> x6, Pallas kernels: 5.14 us -> 6.74 us  [the longest x1 3.01 us: begin_sum(): pl.pallas_call(functools.partial(begin_kernel, chunks), out_shape=[jax.Sh...]
    concatenate x4, other arithmetic: 0.03 us -> 0.74 us  [the longest x1 0.72 us: per_device(): return (jnp.concatenate(new_rows), grad_weight, grad_bias[0])]
  transfers between devices with their start and end apart: 17 -> 20, of which waited for: 9 -> 12; matrix products, arithmetic and copies ran while one was open for 0% -> 1% of each run, Pallas kernels for 7% -> 9%
where the time goes in v3:
time: 66.9 us; the launch traced here: 66.7 us
  waiting for transfers between devices  33.7 us (50%)
  starting transfers between devices  23.1 us (35%)
  Pallas kernels  7.95 us (12%)
  other arithmetic  1.02 us (2%)
  between operations  0.94 us (1%)
    ppermute x16, waiting for transfers between devices, partner(): return lax.ppermute(block, 'dom', [(i, i ^ bits) for i in range(count)])  25.5 us
    ppermute x16, starting transfers between devices, partner(): return lax.ppermute(block, 'dom', [(i, i ^ bits) for i in range(count)])  19.5 us
    ppermute x4, waiting for transfers between devices, passed_along(): lax.ppermute(block, axis, [((i - distance) % count, i) for i in range(cou...  8.19 us
    ppermute x4, starting transfers between devices, passed_along(): lax.ppermute(block, axis, [((i - distance) % count, i) for i in range(cou...  3.6 us
    pallas_call x1, Pallas kernels, begin_sum(): pl.pallas_call(functools.partial(begin_kernel, chunks), out_shape=[jax.Sh...  3.01 us
    pallas_call x2, Pallas kernels, tile_sum(): pl.pallas_call(functools.partial(sum_kernel, places, cap, last), out_shap...  1.91 us
  transfers between devices with their start and end apart: 20, of which 12 were waited for; matrix products, arithmetic and copies ran while one was open for 1% of the time, Pallas kernels for 9%

profile of v3, /device:TPU:0, one launch (start us, length us, event | category | flops | bytes accessed | tf_op | source)
XLA Modules:
  0.0 66.7 jit_solution(5728253144521432334)
XLA Ops:
  0.6 4.1 %collective-permute-start = (bf16[8,128,128]{2,1,0:T(8,128)(2,1)}, bf16[8,128,128]{2,1,0:T(8,128)(2,1)S(1)}, u32[]{:S(2)}, u32[]{:S(2)}) collective-permute-start(bf16[8,128,128]{2,1,0:T(8,128)(2,1)} %bitcast.28), channel_id=1, source_target_pairs={{0,16},{2,18},{4,20},{6,22},{8,24},{10,26},{12,28},{14,30},{16,0},... | collective-permute-start | bytes 786440 | tf_op jit(solution)/shard_map/ppermute | solution.py:20
  4.7 1.6 %collective-permute-start.4 = (bf16[8,128,128]{2,1,0:T(8,128)(2,1)}, bf16[8,128,128]{2,1,0:T(8,128)(2,1)S(1)}, u32[]{:S(2)}, u32[]{:S(2)}) collective-permute-start(bf16[8,128,128]{2,1,0:T(8,128)(2,1)} %bitcast.29), channel_id=1, source_target_pairs={{0,8},{2,10},{4,12},{6,14},{8,0},{10,2},{12,4},{14,6},{16,24},{18,... | collective-permute-start | bytes 786440 | tf_op jit(solution)/shard_map/ppermute | solution.py:20
  6.3 1.5 %collective-permute-start.1 = (s32[2,16]{1,0:T(2,128)}, s32[2,16]{1,0:T(2,128)S(1)}, u32[]{:S(2)}, u32[]{:S(2)}) collective-permute-start(s32[2,16]{1,0:T(2,128)} %bitcast.37), channel_id=1, source_target_pairs={{0,2},{2,0},{4,6},{6,4},{8,10},{10,8},{12,14},{14,12},{16,18},{18,... | collective-permute-start | bytes 392 | tf_op jit(solution)/shard_map/ppermute | solution.py:20
  7.8 1.5 %collective-permute-start.2 = (s32[2,16]{1,0:T(2,128)}, s32[2,16]{1,0:T(2,128)S(1)}, u32[]{:S(2)}, u32[]{:S(2)}) collective-permute-start(s32[2,16]{1,0:T(2,128)} %bitcast.38), channel_id=1, source_target_pairs={{0,4},{2,6},{4,0},{6,2},{8,12},{10,14},{12,8},{14,10},{16,20},{18,... | collective-permute-start | bytes 392 | tf_op jit(solution)/shard_map/ppermute | solution.py:20
  9.8 3.0 %shard_map.121.acc_in = f32[16,128,128]{2,1,0:T(8,128)S(1)} custom-call(s32[1,64]{1,0:T(1,128)} %refs_0_.1, s32[1,64]{1,0:T(1,128)} %refs_1_.1, bf16[8,128,128]{2,1,0:T(8,128)(2,1)} %bitcast.30, bf16[64,128,128]{2,1,0:T(8,128)(2,1)} %refs_3_.1), custom_call_target="tpu_custom_call" | custom-call | tf_op jit(solution)/shard_map/pallas_call | solution.py:79
  12.9 1.2 %collective-permute-done.3.refs_2_ = s32[2,16]{1,0:T(2,128)S(1)} collective-permute-done((s32[2,16]{1,0:T(2,128)}, s32[2,16]{1,0:T(2,128)S(1)}, u32[]{:S(2)}, u32[]{:S(2)}) %collective-permute-start.3) | collective-permute-done | bytes 160 | tf_op jit(solution)/shard_map/ppermute | solution.py:20
  14.0 3.0 %collective-permute-done.refs_5_ = bf16[8,128,128]{2,1,0:T(8,128)(2,1)S(1)} collective-permute-done((bf16[8,128,128]{2,1,0:T(8,128)(2,1)}, bf16[8,128,128]{2,1,0:T(8,128)(2,1)S(1)}, u32[]{:S(2)}, u32[]{:S(2)}) %collective-permute-start) | collective-permute-done | bytes 262176 | tf_op jit(solution)/shard_map/ppermute | solution.py:20
  18.3 1.6 %collective-permute-start.6 = (bf16[6,128,128]{2,1,0:T(8,128)(2,1)S(1)}, bf16[6,128,128]{2,1,0:T(8,128)(2,1)S(1)}, u32[]{:S(2)}, u32[]{:S(2)}) collective-permute-start(bf16[6,128,128]{2,1,0:T(8,128)(2,1)S(1)} %get-tuple-element.32), channel_id=1, source_target_pairs={{0,4},{2,6},{4,0},{6,2},{8,12},{10,14},{12,8},{14,10},{16,20},{18,... | collective-permute-start | bytes 589832 | tf_op jit(solution)/shard_map/ppermute | solution.py:20
  19.9 1.5 %collective-permute-start.5 = (bf16[6,128,128]{2,1,0:T(8,128)(2,1)S(1)}, bf16[6,128,128]{2,1,0:T(8,128)(2,1)S(1)}, u32[]{:S(2)}, u32[]{:S(2)}) collective-permute-start(bf16[6,128,128]{2,1,0:T(8,128)(2,1)S(1)} %get-tuple-element.31), channel_id=1, source_target_pairs={{0,2},{2,0},{4,6},{6,4},{8,10},{10,8},{12,14},{14,12},{16,18},{18,... | collective-permute-start | bytes 589832 | tf_op jit(solution)/shard_map/ppermute | solution.py:20
  21.9 2.5 %collective-permute-done.8.refs_3_.refs_0_ = bf16[8,128,128]{2,1,0:T(8,128)(2,1)S(1)} collective-permute-done((bf16[8,128,128]{2,1,0:T(8,128)(2,1)S(1)}, bf16[8,128,128]{2,1,0:T(8,128)(2,1)S(1)}, u32[]{:S(2)}, u32[]{:S(2)}) %collective-permute-start.8) | collective-permute-done | bytes 262176 | tf_op jit(solution)/shard_map/ppermute | solution.py:20
  25.0 1.3 %collective-permute-start.9 = (bf16[2,128,128]{2,1,0:T(8,128)(2,1)S(1)}, bf16[2,128,128]{2,1,0:T(8,128)(2,1)S(1)}, u32[]{:S(2)}, u32[]{:S(2)}) collective-permute-start(bf16[2,128,128]{2,1,0:T(8,128)(2,1)S(1)} %get-tuple-element.35), channel_id=1, source_target_pairs={{0,2},{2,0},{4,6},{6,4},{8,10},{10,8},{12,14},{14,12},{16,18},{18,... | collective-permute-start | bytes 196616 | tf_op jit(solution)/shard_map/ppermute | solution.py:20
  26.4 1.5 %collective-permute-start.10 = (bf16[2,128,128]{2,1,0:T(8,128)(2,1)S(1)}, bf16[2,128,128]{2,1,0:T(8,128)(2,1)S(1)}, u32[]{:S(2)}, u32[]{:S(2)}) collective-permute-start(bf16[2,128,128]{2,1,0:T(8,128)(2,1)S(1)} %get-tuple-element.36), channel_id=1, source_target_pairs={{0,4},{2,6},{4,0},{6,2},{8,12},{10,14},{12,8},{14,10},{16,20},{18,... | collective-permute-start | bytes 196616 | tf_op jit(solution)/shard_map/ppermute | solution.py:20
  28.6 3.3 %collective-permute-done.7.refs_3_ = bf16[6,128,128]{2,1,0:T(8,128)(2,1)S(1)} collective-permute-done((bf16[6,128,128]{2,1,0:T(8,128)(2,1)S(1)}, bf16[6,128,128]{2,1,0:T(8,128)(2,1)S(1)}, u32[]{:S(2)}, u32[]{:S(2)}) %collective-permute-start.7) | collective-permute-done | bytes 196640 | tf_op jit(solution)/shard_map/ppermute | solution.py:20
  31.9 1.0 %shard_map.123.acc_in = f32[16,128,128]{2,1,0:T(8,128)S(1)} custom-call(s32[1]{0:T(128)} %bitcast.me_ref, s32[2,16]{1,0:T(2,128)S(1)} %bitcast.40, s32[2,16]{1,0:T(2,128)S(1)} %bitcast.42, bf16[32,128,128]{2,1,0:T(8,128)(2,1)S(1)} %bitcast.26, f32[16,128,128]{2,1,0:T(8,128)S(1)} %shard_map.121.acc_in, bf16[8,128,128]{2,1,0:T(8,128)(2,1)S(1)} %bitcast.32, ...), custom_call_target="tpu_custom_call" | custom-call | tf_op jit(solution)/shard_map/pallas_call | solution.py:136
  33.2 0.9 %shard_map.125 = (f32[8,128,128]{2,1,0:T(8,128)S(1)}, bf16[4,128,128]{2,1,0:T(8,128)(2,1)S(1)}, bf16[4,128,128]{2,1,0:T(8,128)(2,1)S(1)}) custom-call(s32[1]{0:T(128)} %bitcast.me_ref, s32[2,16]{1,0:T(2,128)S(1)} %bitcast.41, s32[2,16]{1,0:T(2,128)S(1)} %bitcast.43, bf16[32,128,128]{2,1,0:T(8,128)(2,1)S(1)} %bitcast.27, ...), custom_call_target="tpu_custom_call" | custom-call | tf_op jit(solution)/shard_map/pallas_call | solution.py:136
  34.1 1.6 %collective-permute-start.12 = (bf16[4,128,128]{2,1,0:T(8,128)(2,1)S(1)}, bf16[4,128,128]{2,1,0:T(8,128)(2,1)S(1)}, u32[]{:S(2)}, u32[]{:S(2)}) collective-permute-start(bf16[4,128,128]{2,1,0:T(8,128)(2,1)S(1)} %get-tuple-element.40), channel_id=1, source_target_pairs={{30,0},{0,2},{2,4},{4,6},{6,8},{8,10},{10,12},{12,14},{14,16},{16,... | collective-permute-start | bytes 393224 | tf_op jit(solution)/shard_map/ppermute | solution.py:25
  35.6 1.5 %collective-permute-start.14 = (bf16[4,128,128]{2,1,0:T(8,128)(2,1)S(1)}, bf16[4,128,128]{2,1,0:T(8,128)(2,1)S(1)}, u32[]{:S(2)}, u32[]{:S(2)}) collective-permute-start(bf16[4,128,128]{2,1,0:T(8,128)(2,1)S(1)} %get-tuple-element.42), channel_id=1, source_target_pairs={{30,0},{0,2},{2,4},{4,6},{6,8},{8,10},{10,12},{12,14},{14,16},{16,... | collective-permute-start | bytes 393224 | tf_op jit(solution)/shard_map/ppermute | solution.py:25
  37.1 6.0 %collective-permute-done.12 = bf16[4,128,128]{2,1,0:T(8,128)(2,1)S(1)} collective-permute-done((bf16[4,128,128]{2,1,0:T(8,128)(2,1)S(1)}, bf16[4,128,128]{2,1,0:T(8,128)(2,1)S(1)}, u32[]{:S(2)}, u32[]{:S(2)}) %collective-permute-start.12) | collective-permute-done | bytes 131104 | tf_op jit(solution)/shard_map/ppermute | solution.py:25
  43.1 1.4 %collective-permute-done.14 = bf16[4,128,128]{2,1,0:T(8,128)(2,1)S(1)} collective-permute-done((bf16[4,128,128]{2,1,0:T(8,128)(2,1)S(1)}, bf16[4,128,128]{2,1,0:T(8,128)(2,1)S(1)}, u32[]{:S(2)}, u32[]{:S(2)}) %collective-permute-start.14) | collective-permute-done | bytes 131104 | tf_op jit(solution)/shard_map/ppermute | solution.py:25
  47.2 4.3 %collective-permute-done.16 = bf16[272,128]{1,0:T(8,128)(2,1)S(1)} collective-permute-done((bf16[272,128]{1,0:T(8,128)(2,1)S(1)}, bf16[272,128]{1,0:T(8,128)(2,1)S(1)}, u32[]{:S(2)}, u32[]{:S(2)}) %collective-permute-start.16) | collective-permute-done | bytes 69664 | tf_op jit(solution)/shard_map/ppermute | solution.py:20
  51.7 4.3 %collective-permute-done.17 = bf16[272,128]{1,0:T(8,128)(2,1)S(1)} collective-permute-done((bf16[272,128]{1,0:T(8,128)(2,1)S(1)}, bf16[272,128]{1,0:T(8,128)(2,1)S(1)}, u32[]{:S(2)}, u32[]{:S(2)}) %collective-permute-start.17) | collective-permute-done | bytes 69664 | tf_op jit(solution)/shard_map/ppermute | solution.py:20
  56.2 4.3 %collective-permute-done.18 = bf16[272,128]{1,0:T(8,128)(2,1)S(1)} collective-permute-done((bf16[272,128]{1,0:T(8,128)(2,1)S(1)}, bf16[272,128]{1,0:T(8,128)(2,1)S(1)}, u32[]{:S(2)}, u32[]{:S(2)}) %collective-permute-start.18) | collective-permute-done | bytes 69664 | tf_op jit(solution)/shard_map/ppermute | solution.py:20
  60.6 2.2 %collective-permute-start.19 = (bf16[272,128]{1,0:T(8,128)(2,1)S(1)}, bf16[272,128]{1,0:T(8,128)(2,1)S(1)}, u32[]{:S(2)}, u32[]{:S(2)}) collective-permute-start(bf16[272,128]{1,0:T(8,128)(2,1)S(1)} %pad_maximum_fusion.3), channel_id=1, source_target_pairs={{0,16},{2,18},{4,20},{6,22},{8,24},{10,26},{12,28},{14,30},{16,0},... | collective-permute-start | bytes 208904 | tf_op jit(solution)/shard_map/ppermute | solution.py:20
  63.6 2.5 %collective-permute-done.19.got_ref = bf16[272,128]{1,0:T(8,128)(2,1)S(1)} collective-permute-done((bf16[272,128]{1,0:T(8,128)(2,1)S(1)}, bf16[272,128]{1,0:T(8,128)(2,1)S(1)}, u32[]{:S(2)}, u32[]{:S(2)}) %collective-permute-start.19) | collective-permute-done | bytes 69664 | tf_op jit(solution)/shard_map/ppermute | solution.py:20
  (62 shorter events, 8.3 us)
Async XLA Ops:
  0.6 17.1 %copy-start.1 = (bf16[1024,128]{1,0:T(8,128)(2,1)S(1)}, bf16[1024,128]{1,0:T(8,128)(2,1)}, u32[]{:S(2)}) copy-start(bf16[1024,128]{1,0:T(8,128)(2,1)} %param.10) | copy-start | bytes 786436
  0.6 16.3 %collective-permute-start = (bf16[8,128,128]{2,1,0:T(8,128)(2,1)}, bf16[8,128,128]{2,1,0:T(8,128)(2,1)S(1)}, u32[]{:S(2)}, u32[]{:S(2)}) collective-permute-start(bf16[8,128,128]{2,1,0:T(8,128)(2,1)} %bitcast.28), channel_id=1, source_target_pairs={{0,16},{2,18},{4,20},{6,22},{8,24},{10,26},{12,28},{14,30},{16,0},... | collective-permute-start | bytes 786440 | tf_op jit(solution)/shard_map/ppermute | solution.py:20
  4.7 13.0 %collective-permute-start.4 = (bf16[8,128,128]{2,1,0:T(8,128)(2,1)}, bf16[8,128,128]{2,1,0:T(8,128)(2,1)S(1)}, u32[]{:S(2)}, u32[]{:S(2)}) collective-permute-start(bf16[8,128,128]{2,1,0:T(8,128)(2,1)} %bitcast.29), channel_id=1, source_target_pairs={{0,8},{2,10},{4,12},{6,14},{8,0},{10,2},{12,4},{14,6},{16,24},{18,... | collective-permute-start | bytes 786440 | tf_op jit(solution)/shard_map/ppermute | solution.py:20
  6.3 25.5 %copy-start = (bf16[1,16,2,128,128]{4,3,2,1,0:T(8,128)(2,1)S(1)}, bf16[1,16,2,128,128]{4,3,2,1,0:T(8,128)(2,1)}, u32[]{:S(2)}) copy-start(bf16[1,16,2,128,128]{4,3,2,1,0:T(8,128)(2,1)} %param.12) | copy-start | bytes 3145732
  6.3 25.5 %copy-start.3 = (s32[1,16,2]{1,2,0:T(2,128)S(1)}, s32[1,16,2]{1,2,0:T(2,128)}, u32[]{:S(2)}) copy-start(s32[1,16,2]{1,2,0:T(2,128)} %param.11) | copy-start | bytes 388
  6.3 25.5 %copy-start.4 = (s32[1,16,2]{1,2,0:T(2,128)S(1)}, s32[1,16,2]{1,2,0:T(2,128)}, u32[]{:S(2)}) copy-start(s32[1,16,2]{1,2,0:T(2,128)} %param.13) | copy-start | bytes 388
  6.3 6.5 %collective-permute-start.1 = (s32[2,16]{1,0:T(2,128)}, s32[2,16]{1,0:T(2,128)S(1)}, u32[]{:S(2)}, u32[]{:S(2)}) collective-permute-start(s32[2,16]{1,0:T(2,128)} %bitcast.37), channel_id=1, source_target_pairs={{0,2},{2,0},{4,6},{6,4},{8,10},{10,8},{12,14},{14,12},{16,18},{18,... | collective-permute-start | bytes 392 | tf_op jit(solution)/shard_map/ppermute | solution.py:20
  7.8 5.0 %collective-permute-start.2 = (s32[2,16]{1,0:T(2,128)}, s32[2,16]{1,0:T(2,128)S(1)}, u32[]{:S(2)}, u32[]{:S(2)}) collective-permute-start(s32[2,16]{1,0:T(2,128)} %bitcast.38), channel_id=1, source_target_pairs={{0,4},{2,6},{4,0},{6,2},{8,12},{10,14},{12,8},{14,10},{16,20},{18,... | collective-permute-start | bytes 392 | tf_op jit(solution)/shard_map/ppermute | solution.py:20
  9.3 4.7 %collective-permute-start.3 = (s32[2,16]{1,0:T(2,128)}, s32[2,16]{1,0:T(2,128)S(1)}, u32[]{:S(2)}, u32[]{:S(2)}) collective-permute-start(s32[2,16]{1,0:T(2,128)} %bitcast.39), channel_id=1, source_target_pairs={{0,6},{2,4},{4,2},{6,0},{8,14},{10,12},{12,10},{14,8},{16,22},{18,... | collective-permute-start | bytes 392 | tf_op jit(solution)/shard_map/ppermute | solution.py:20
  17.0 7.4 %collective-permute-start.8 = (bf16[8,128,128]{2,1,0:T(8,128)(2,1)S(1)}, bf16[8,128,128]{2,1,0:T(8,128)(2,1)S(1)}, u32[]{:S(2)}, u32[]{:S(2)}) collective-permute-start(bf16[8,128,128]{2,1,0:T(8,128)(2,1)S(1)} %collective-permute-done.refs_5_), channel_id=1, source_target_pairs={{0,8},{2,10},{4,12},{6,14},{8,0},{10,2},{12,4},{14,6},{16,24},{18,... | collective-permute-start | bytes 786440 | tf_op jit(solution)/shard_map/ppermute | solution.py:20
  18.3 9.5 %collective-permute-start.6 = (bf16[6,128,128]{2,1,0:T(8,128)(2,1)S(1)}, bf16[6,128,128]{2,1,0:T(8,128)(2,1)S(1)}, u32[]{:S(2)}, u32[]{:S(2)}) collective-permute-start(bf16[6,128,128]{2,1,0:T(8,128)(2,1)S(1)} %get-tuple-element.32), channel_id=1, source_target_pairs={{0,4},{2,6},{4,0},{6,2},{8,12},{10,14},{12,8},{14,10},{16,20},{18,... | collective-permute-start | bytes 589832 | tf_op jit(solution)/shard_map/ppermute | solution.py:20
  19.9 8.7 %collective-permute-start.5 = (bf16[6,128,128]{2,1,0:T(8,128)(2,1)S(1)}, bf16[6,128,128]{2,1,0:T(8,128)(2,1)S(1)}, u32[]{:S(2)}, u32[]{:S(2)}) collective-permute-start(bf16[6,128,128]{2,1,0:T(8,128)(2,1)S(1)} %get-tuple-element.31), channel_id=1, source_target_pairs={{0,2},{2,0},{4,6},{6,4},{8,10},{10,8},{12,14},{14,12},{16,18},{18,... | collective-permute-start | bytes 589832 | tf_op jit(solution)/shard_map/ppermute | solution.py:20
  21.4 10.4 %collective-permute-start.7 = (bf16[6,128,128]{2,1,0:T(8,128)(2,1)S(1)}, bf16[6,128,128]{2,1,0:T(8,128)(2,1)S(1)}, u32[]{:S(2)}, u32[]{:S(2)}) collective-permute-start(bf16[6,128,128]{2,1,0:T(8,128)(2,1)S(1)} %get-tuple-element.33), channel_id=1, source_target_pairs={{0,6},{2,4},{4,2},{6,0},{8,14},{10,12},{12,10},{14,8},{16,22},{18,... | collective-permute-start | bytes 589832 | tf_op jit(solution)/shard_map/ppermute | solution.py:20
  25.0 7.9 %collective-permute-start.9 = (bf16[2,128,128]{2,1,0:T(8,128)(2,1)S(1)}, bf16[2,128,128]{2,1,0:T(8,128)(2,1)S(1)}, u32[]{:S(2)}, u32[]{:S(2)}) collective-permute-start(bf16[2,128,128]{2,1,0:T(8,128)(2,1)S(1)} %get-tuple-element.35), channel_id=1, source_target_pairs={{0,2},{2,0},{4,6},{6,4},{8,10},{10,8},{12,14},{14,12},{16,18},{18,... | collective-permute-start | bytes 196616 | tf_op jit(solution)/shard_map/ppermute | solution.py:20
  26.4 6.6 %collective-permute-start.10 = (bf16[2,128,128]{2,1,0:T(8,128)(2,1)S(1)}, bf16[2,128,128]{2,1,0:T(8,128)(2,1)S(1)}, u32[]{:S(2)}, u32[]{:S(2)}) collective-permute-start(bf16[2,128,128]{2,1,0:T(8,128)(2,1)S(1)} %get-tuple-element.36), channel_id=1, source_target_pairs={{0,4},{2,6},{4,0},{6,2},{8,12},{10,14},{12,8},{14,10},{16,20},{18,... | collective-permute-start | bytes 196616 | tf_op jit(solution)/shard_map/ppermute | solution.py:20
  27.9 5.3 %collective-permute-start.11 = (bf16[2,128,128]{2,1,0:T(8,128)(2,1)S(1)}, bf16[2,128,128]{2,1,0:T(8,128)(2,1)S(1)}, u32[]{:S(2)}, u32[]{:S(2)}) collective-permute-start(bf16[2,128,128]{2,1,0:T(8,128)(2,1)S(1)} %get-tuple-element.38), channel_id=1, source_target_pairs={{0,6},{2,4},{4,2},{6,0},{8,14},{10,12},{12,10},{14,8},{16,22},{18,... | collective-permute-start | bytes 196616 | tf_op jit(solution)/shard_map/ppermute | solution.py:20
  34.1 9.0 %collective-permute-start.12 = (bf16[4,128,128]{2,1,0:T(8,128)(2,1)S(1)}, bf16[4,128,128]{2,1,0:T(8,128)(2,1)S(1)}, u32[]{:S(2)}, u32[]{:S(2)}) collective-permute-start(bf16[4,128,128]{2,1,0:T(8,128)(2,1)S(1)} %get-tuple-element.40), channel_id=1, source_target_pairs={{30,0},{0,2},{2,4},{4,6},{6,8},{8,10},{10,12},{12,14},{14,16},{16,... | collective-permute-start | bytes 393224 | tf_op jit(solution)/shard_map/ppermute | solution.py:25
  35.6 8.8 %collective-permute-start.14 = (bf16[4,128,128]{2,1,0:T(8,128)(2,1)S(1)}, bf16[4,128,128]{2,1,0:T(8,128)(2,1)S(1)}, u32[]{:S(2)}, u32[]{:S(2)}) collective-permute-start(bf16[4,128,128]{2,1,0:T(8,128)(2,1)S(1)} %get-tuple-element.42), channel_id=1, source_target_pairs={{30,0},{0,2},{2,4},{4,6},{6,8},{8,10},{10,12},{12,14},{14,16},{16,... | collective-permute-start | bytes 393224 | tf_op jit(solution)/shard_map/ppermute | solution.py:25
  44.5 1.4 %collective-permute-start.13 = (bf16[512,128]{1,0:T(8,128)(2,1)S(1)}, bf16[512,128]{1,0:T(8,128)(2,1)S(1)}, u32[]{:S(2)}, u32[]{:S(2)}) collective-permute-start(bf16[512,128]{1,0:T(8,128)(2,1)S(1)} %bitcast.35), channel_id=1, source_target_pairs={{1,0},{0,1},{3,2},{2,3},{5,4},{4,5},{7,6},{6,7},{9,8},{8,9},{11,10... | collective-permute-start | bytes 393224 | tf_op jit(solution)/shard_map/ppermute | solution.py:25
  44.6 1.9 %collective-permute-start.15 = (bf16[512,128]{1,0:T(8,128)(2,1)S(1)}, bf16[512,128]{1,0:T(8,128)(2,1)S(1)}, u32[]{:S(2)}, u32[]{:S(2)}) collective-permute-start(bf16[512,128]{1,0:T(8,128)(2,1)S(1)} %bitcast.33), channel_id=1, source_target_pairs={{1,0},{0,1},{3,2},{2,3},{5,4},{4,5},{7,6},{6,7},{9,8},{8,9},{11,10... | collective-permute-start | bytes 393224 | tf_op jit(solution)/shard_map/ppermute | solution.py:25
  47.1 4.4 %collective-permute-start.16 = (bf16[272,128]{1,0:T(8,128)(2,1)S(1)}, bf16[272,128]{1,0:T(8,128)(2,1)S(1)}, u32[]{:S(2)}, u32[]{:S(2)}) collective-permute-start(bf16[272,128]{1,0:T(8,128)(2,1)S(1)} %get-tuple-element.47), channel_id=1, source_target_pairs={{0,2},{2,0},{4,6},{6,4},{8,10},{10,8},{12,14},{14,12},{16,18},{18,... | collective-permute-start | bytes 208904 | tf_op jit(solution)/shard_map/ppermute | solution.py:20
  51.6 4.4 %collective-permute-start.17 = (bf16[272,128]{1,0:T(8,128)(2,1)S(1)}, bf16[272,128]{1,0:T(8,128)(2,1)S(1)}, u32[]{:S(2)}, u32[]{:S(2)}) collective-permute-start(bf16[272,128]{1,0:T(8,128)(2,1)S(1)} %pad_maximum_fusion.1), channel_id=1, source_target_pairs={{0,4},{2,6},{4,0},{6,2},{8,12},{10,14},{12,8},{14,10},{16,20},{18,... | collective-permute-start | bytes 208904 | tf_op jit(solution)/shard_map/ppermute | solution.py:20
  56.1 4.4 %collective-permute-start.18 = (bf16[272,128]{1,0:T(8,128)(2,1)S(1)}, bf16[272,128]{1,0:T(8,128)(2,1)S(1)}, u32[]{:S(2)}, u32[]{:S(2)}) collective-permute-start(bf16[272,128]{1,0:T(8,128)(2,1)S(1)} %pad_maximum_fusion.2), channel_id=1, source_target_pairs={{0,8},{2,10},{4,12},{6,14},{8,0},{10,2},{12,4},{14,6},{16,24},{18,... | collective-permute-start | bytes 208904 | tf_op jit(solution)/shard_map/ppermute | solution.py:20
  60.6 5.5 %collective-permute-start.19 = (bf16[272,128]{1,0:T(8,128)(2,1)S(1)}, bf16[272,128]{1,0:T(8,128)(2,1)S(1)}, u32[]{:S(2)}, u32[]{:S(2)}) collective-permute-start(bf16[272,128]{1,0:T(8,128)(2,1)S(1)} %pad_maximum_fusion.3), channel_id=1, source_target_pairs={{0,16},{2,18},{4,20},{6,22},{8,24},{10,26},{12,28},{14,30},{16,0},... | collective-permute-start | bytes 208904 | tf_op jit(solution)/shard_map/ppermute | solution.py:20
  (3 other events, 38.2 us)

commit v4 on v3

--- a/solution.py
+++ b/solution.py
@@ -216,29 +216,48 @@
     return lax.reduce_precision(value, 8, 7)
 
 
-def finish_kernel(feat_ref, weight_ref, bias_ref, got_ref, weight_out, bias_out):
+def finish_kernel(feat_ref, weight_ref, bias_ref, *refs):
+    *got_refs, weight_out, bias_out = refs
     depth = weight_ref.shape[0]
     half = depth // 2
     feat = feat_ref[0]
+
+    def total(mine, start, rows):
+        got = [ref[start : start + rows].astype(jnp.float32) for ref in got_refs]
+        mine = mine + got[0]
+        return mine + (got[1] + got[2]) if len(got) > 1 else mine
+
     for at, place in ((0, feat), (half, 1 - feat)):
-        weight_out[pl.ds(pl.multiple_of(place * half, half), half)] = weight_ref[
-            at : at + half
-        ] + got_ref[at : at + half].astype(jnp.float32)
-    rows = got_ref[depth:].astype(jnp.float32)
-    bias_out[...] = bias_ref[...] + (rows[:1] + rows[8:9])
+        weight_out[pl.ds(pl.multiple_of(place * half, half), half)] = total(
+            weight_ref[at : at + half], at, half
+        )
+    rows = [ref[depth:].astype(jnp.float32) for ref in got_refs]
+    rows = [part[:1] + part[8:9] for part in rows]
+    bias = bias_ref[...] + rows[0]
+    bias_out[...] = bias + (rows[1] + rows[2]) if len(rows) > 1 else bias
 
 
 def summed(weight_term, bias_term, sent, count, feat):
     depth, width = weight_term.shape
-    bits = 1
-    while True:
-        raw = partner(sent, bits)
-        bits *= 2
-        if bits >= count:
+
+    def taken(raw):
+        got = raw.astype(jnp.float32)
+        return got[:depth], got[depth : depth + 1] + got[depth + 8 : depth + 9]
+
+    plan, bits = [], 1
+    while bits < count:
+        plan.append([bits * j for j in range(1, min(PEERS, count // bits))])
+        bits *= PEERS
+    for at, bits in enumerate(plan):
+        raw = [partner(sent, k) for k in bits]
+        if at == len(plan) - 1:
             break
-        got = raw.astype(jnp.float32)
-        weight_term = rounded(weight_term + got[:depth])
-        bias_term = bias_term + (got[depth : depth + 1] + got[depth + 8 : depth + 9])
+        got = [taken(part) for part in raw]
+        weight_term, bias_term = weight_term + got[0][0], bias_term + got[0][1]
+        if len(got) > 1:
+            weight_term = weight_term + (got[1][0] + got[2][0])
+            bias_term = bias_term + (got[1][1] + got[2][1])
+        weight_term = rounded(weight_term)
         high = rounded(bias_term)
         low = rounded(bias_term - high)
         bias_term = high + low
@@ -250,10 +269,10 @@
             jax.ShapeDtypeStruct((depth, width), jnp.float32),
             jax.ShapeDtypeStruct((1, width), jnp.float32),
         ],
-        in_specs=[SMEM] + [VMEM] * 3,
+        in_specs=[SMEM] + [VMEM] * (2 + len(raw)),
         out_specs=[VMEM] * 2,
         compiler_params=PARAMS,
-    )(feat, weight_term, bias_term, raw)
+    )(feat, weight_term, bias_term, *raw)
 
 
 def per_device(

time: 66.9 us -> 63.1 us (0.943)
  waiting for transfers between devices: 33.7 us -> 24.5 us
  starting transfers between devices: 23.1 us -> 28.6 us
    ppermute x16 -> x18, waiting for transfers between devices: 25.5 us -> 16.3 us  [partner(): return lax.ppermute(block, 'dom', [(i, i ^ bits) for i in range(count)])]
    ppermute x16 -> x18, starting transfers between devices: 19.5 us -> 25 us  [partner(): return lax.ppermute(block, 'dom', [(i, i ^ bits) for i in range(count)])]
  transfers between devices with their start and end apart: 20 -> 22, of which waited for: 12 -> 11; matrix products, arithmetic and copies ran while one was open for 1% -> 1% of each run, Pallas kernels for 9% -> 9%
where the time goes in v4:
time: 63.1 us; the launch traced here: 62.9 us
  starting transfers between devices  28.6 us (45%)
  waiting for transfers between devices  24.5 us (39%)
  Pallas kernels  7.98 us (13%)
  other arithmetic  0.89 us (1%)
  between operations  0.88 us (1%)
    ppermute x18, starting transfers between devices, partner(): return lax.ppermute(block, 'dom', [(i, i ^ bits) for i in range(count)])  25 us
    ppermute x18, waiting for transfers between devices, partner(): return lax.ppermute(block, 'dom', [(i, i ^ bits) for i in range(count)])  16.3 us
    ppermute x4, waiting for transfers between devices, passed_along(): lax.ppermute(block, axis, [((i - distance) % count, i) for i in range(cou...  8.19 us
    ppermute x4, starting transfers between devices, passed_along(): lax.ppermute(block, axis, [((i - distance) % count, i) for i in range(cou...  3.6 us
    pallas_call x1, Pallas kernels, begin_sum(): pl.pallas_call(functools.partial(begin_kernel, chunks), out_shape=[jax.Sh...  3.01 us
    pallas_call x2, Pallas kernels, tile_sum(): pl.pallas_call(functools.partial(sum_kernel, places, cap, last), out_shap...  1.91 us
  transfers between devices with their start and end apart: 22, of which 11 were waited for; matrix products, arithmetic and copies ran while one was open for 1% of the time, Pallas kernels for 9%

profile of v4, /device:TPU:0, one launch (start us, length us, event | category | flops | bytes accessed | tf_op | source)
XLA Modules:
  0.0 62.9 jit_solution(9713662517007238601)
XLA Ops:
  0.6 4.1 %collective-permute-start = (bf16[8,128,128]{2,1,0:T(8,128)(2,1)}, bf16[8,128,128]{2,1,0:T(8,128)(2,1)S(1)}, u32[]{:S(2)}, u32[]{:S(2)}) collective-permute-start(bf16[8,128,128]{2,1,0:T(8,128)(2,1)} %bitcast.20), channel_id=1, source_target_pairs={{0,16},{2,18},{4,20},{6,22},{8,24},{10,26},{12,28},{14,30},{16,0},... | collective-permute-start | bytes 786440 | tf_op jit(solution)/shard_map/ppermute | solution.py:20
  4.7 1.6 %collective-permute-start.4 = (bf16[8,128,128]{2,1,0:T(8,128)(2,1)}, bf16[8,128,128]{2,1,0:T(8,128)(2,1)S(1)}, u32[]{:S(2)}, u32[]{:S(2)}) collective-permute-start(bf16[8,128,128]{2,1,0:T(8,128)(2,1)} %bitcast.21), channel_id=1, source_target_pairs={{0,8},{2,10},{4,12},{6,14},{8,0},{10,2},{12,4},{14,6},{16,24},{18,... | collective-permute-start | bytes 786440 | tf_op jit(solution)/shard_map/ppermute | solution.py:20
  6.3 1.5 %collective-permute-start.1 = (s32[2,16]{1,0:T(2,128)}, s32[2,16]{1,0:T(2,128)S(1)}, u32[]{:S(2)}, u32[]{:S(2)}) collective-permute-start(s32[2,16]{1,0:T(2,128)} %bitcast.29), channel_id=1, source_target_pairs={{0,2},{2,0},{4,6},{6,4},{8,10},{10,8},{12,14},{14,12},{16,18},{18,... | collective-permute-start | bytes 392 | tf_op jit(solution)/shard_map/ppermute | solution.py:20
  7.8 1.5 %collective-permute-start.2 = (s32[2,16]{1,0:T(2,128)}, s32[2,16]{1,0:T(2,128)S(1)}, u32[]{:S(2)}, u32[]{:S(2)}) collective-permute-start(s32[2,16]{1,0:T(2,128)} %bitcast.30), channel_id=1, source_target_pairs={{0,4},{2,6},{4,0},{6,2},{8,12},{10,14},{12,8},{14,10},{16,20},{18,... | collective-permute-start | bytes 392 | tf_op jit(solution)/shard_map/ppermute | solution.py:20
  9.8 3.0 %shard_map.121.acc_in = f32[16,128,128]{2,1,0:T(8,128)S(1)} custom-call(s32[1,64]{1,0:T(1,128)} %refs_0_.1, s32[1,64]{1,0:T(1,128)} %refs_1_.1, bf16[8,128,128]{2,1,0:T(8,128)(2,1)} %bitcast.22, bf16[64,128,128]{2,1,0:T(8,128)(2,1)} %refs_3_.1), custom_call_target="tpu_custom_call" | custom-call | tf_op jit(solution)/shard_map/pallas_call | solution.py:79
  12.9 1.2 %collective-permute-done.3.refs_2_ = s32[2,16]{1,0:T(2,128)S(1)} collective-permute-done((s32[2,16]{1,0:T(2,128)}, s32[2,16]{1,0:T(2,128)S(1)}, u32[]{:S(2)}, u32[]{:S(2)}) %collective-permute-start.3) | collective-permute-done | bytes 160 | tf_op jit(solution)/shard_map/ppermute | solution.py:20
  14.0 3.0 %collective-permute-done.refs_5_ = bf16[8,128,128]{2,1,0:T(8,128)(2,1)S(1)} collective-permute-done((bf16[8,128,128]{2,1,0:T(8,128)(2,1)}, bf16[8,128,128]{2,1,0:T(8,128)(2,1)S(1)}, u32[]{:S(2)}, u32[]{:S(2)}) %collective-permute-start) | collective-permute-done | bytes 262176 | tf_op jit(solution)/shard_map/ppermute | solution.py:20
  18.3 1.6 %collective-permute-start.6 = (bf16[6,128,128]{2,1,0:T(8,128)(2,1)S(1)}, bf16[6,128,128]{2,1,0:T(8,128)(2,1)S(1)}, u32[]{:S(2)}, u32[]{:S(2)}) collective-permute-start(bf16[6,128,128]{2,1,0:T(8,128)(2,1)S(1)} %get-tuple-element.32), channel_id=1, source_target_pairs={{0,4},{2,6},{4,0},{6,2},{8,12},{10,14},{12,8},{14,10},{16,20},{18,... | collective-permute-start | bytes 589832 | tf_op jit(solution)/shard_map/ppermute | solution.py:20
  19.9 1.5 %collective-permute-start.5 = (bf16[6,128,128]{2,1,0:T(8,128)(2,1)S(1)}, bf16[6,128,128]{2,1,0:T(8,128)(2,1)S(1)}, u32[]{:S(2)}, u32[]{:S(2)}) collective-permute-start(bf16[6,128,128]{2,1,0:T(8,128)(2,1)S(1)} %get-tuple-element.31), channel_id=1, source_target_pairs={{0,2},{2,0},{4,6},{6,4},{8,10},{10,8},{12,14},{14,12},{16,18},{18,... | collective-permute-start | bytes 589832 | tf_op jit(solution)/shard_map/ppermute | solution.py:20
  21.9 2.5 %collective-permute-done.8.refs_3_.refs_0_ = bf16[8,128,128]{2,1,0:T(8,128)(2,1)S(1)} collective-permute-done((bf16[8,128,128]{2,1,0:T(8,128)(2,1)S(1)}, bf16[8,128,128]{2,1,0:T(8,128)(2,1)S(1)}, u32[]{:S(2)}, u32[]{:S(2)}) %collective-permute-start.8) | collective-permute-done | bytes 262176 | tf_op jit(solution)/shard_map/ppermute | solution.py:20
  25.0 1.3 %collective-permute-start.9 = (bf16[2,128,128]{2,1,0:T(8,128)(2,1)S(1)}, bf16[2,128,128]{2,1,0:T(8,128)(2,1)S(1)}, u32[]{:S(2)}, u32[]{:S(2)}) collective-permute-start(bf16[2,128,128]{2,1,0:T(8,128)(2,1)S(1)} %get-tuple-element.35), channel_id=1, source_target_pairs={{0,2},{2,0},{4,6},{6,4},{8,10},{10,8},{12,14},{14,12},{16,18},{18,... | collective-permute-start | bytes 196616 | tf_op jit(solution)/shard_map/ppermute | solution.py:20
  26.4 1.5 %collective-permute-start.10 = (bf16[2,128,128]{2,1,0:T(8,128)(2,1)S(1)}, bf16[2,128,128]{2,1,0:T(8,128)(2,1)S(1)}, u32[]{:S(2)}, u32[]{:S(2)}) collective-permute-start(bf16[2,128,128]{2,1,0:T(8,128)(2,1)S(1)} %get-tuple-element.36), channel_id=1, source_target_pairs={{0,4},{2,6},{4,0},{6,2},{8,12},{10,14},{12,8},{14,10},{16,20},{18,... | collective-permute-start | bytes 196616 | tf_op jit(solution)/shard_map/ppermute | solution.py:20
  28.6 3.3 %collective-permute-done.7.refs_3_ = bf16[6,128,128]{2,1,0:T(8,128)(2,1)S(1)} collective-permute-done((bf16[6,128,128]{2,1,0:T(8,128)(2,1)S(1)}, bf16[6,128,128]{2,1,0:T(8,128)(2,1)S(1)}, u32[]{:S(2)}, u32[]{:S(2)}) %collective-permute-start.7) | collective-permute-done | bytes 196640 | tf_op jit(solution)/shard_map/ppermute | solution.py:20
  31.9 1.0 %shard_map.123.acc_in = f32[16,128,128]{2,1,0:T(8,128)S(1)} custom-call(s32[1]{0:T(128)} %bitcast.me_ref, s32[2,16]{1,0:T(2,128)S(1)} %bitcast.32, s32[2,16]{1,0:T(2,128)S(1)} %bitcast.34, bf16[32,128,128]{2,1,0:T(8,128)(2,1)S(1)} %bitcast.18, f32[16,128,128]{2,1,0:T(8,128)S(1)} %shard_map.121.acc_in, bf16[8,128,128]{2,1,0:T(8,128)(2,1)S(1)} %bitcast.24, ...), custom_call_target="tpu_custom_call" | custom-call | tf_op jit(solution)/shard_map/pallas_call | solution.py:136
  34.1 1.6 %collective-permute-start.12 = (bf16[4,128,128]{2,1,0:T(8,128)(2,1)S(1)}, bf16[4,128,128]{2,1,0:T(8,128)(2,1)S(1)}, u32[]{:S(2)}, u32[]{:S(2)}) collective-permute-start(bf16[4,128,128]{2,1,0:T(8,128)(2,1)S(1)} %get-tuple-element.40), channel_id=1, source_target_pairs={{30,0},{0,2},{2,4},{4,6},{6,8},{8,10},{10,12},{12,14},{14,16},{16,... | collective-permute-start | bytes 393224 | tf_op jit(solution)/shard_map/ppermute | solution.py:25
  35.6 1.5 %collective-permute-start.14 = (bf16[4,128,128]{2,1,0:T(8,128)(2,1)S(1)}, bf16[4,128,128]{2,1,0:T(8,128)(2,1)S(1)}, u32[]{:S(2)}, u32[]{:S(2)}) collective-permute-start(bf16[4,128,128]{2,1,0:T(8,128)(2,1)S(1)} %get-tuple-element.42), channel_id=1, source_target_pairs={{30,0},{0,2},{2,4},{4,6},{6,8},{8,10},{10,12},{12,14},{14,16},{16,... | collective-permute-start | bytes 393224 | tf_op jit(solution)/shard_map/ppermute | solution.py:25
  37.1 6.0 %collective-permute-done.12 = bf16[4,128,128]{2,1,0:T(8,128)(2,1)S(1)} collective-permute-done((bf16[4,128,128]{2,1,0:T(8,128)(2,1)S(1)}, bf16[4,128,128]{2,1,0:T(8,128)(2,1)S(1)}, u32[]{:S(2)}, u32[]{:S(2)}) %collective-permute-start.12) | collective-permute-done | bytes 131104 | tf_op jit(solution)/shard_map/ppermute | solution.py:25
  43.1 1.4 %collective-permute-done.14 = bf16[4,128,128]{2,1,0:T(8,128)(2,1)S(1)} collective-permute-done((bf16[4,128,128]{2,1,0:T(8,128)(2,1)S(1)}, bf16[4,128,128]{2,1,0:T(8,128)(2,1)S(1)}, u32[]{:S(2)}, u32[]{:S(2)}) %collective-permute-start.14) | collective-permute-done | bytes 131104 | tf_op jit(solution)/shard_map/ppermute | solution.py:25
  47.3 3.4 %collective-permute-start.16 = (bf16[272,128]{1,0:T(8,128)(2,1)S(1)}, bf16[272,128]{1,0:T(8,128)(2,1)S(1)}, u32[]{:S(2)}, u32[]{:S(2)}) collective-permute-start(bf16[272,128]{1,0:T(8,128)(2,1)S(1)} %get-tuple-element.47), channel_id=1, source_target_pairs={{0,2},{2,0},{4,6},{6,4},{8,10},{10,8},{12,14},{14,12},{16,18},{18,... | collective-permute-start | bytes 208904 | tf_op jit(solution)/shard_map/ppermute | solution.py:20
  50.7 2.4 %collective-permute-done.18 = bf16[272,128]{1,0:T(8,128)(2,1)S(1)} collective-permute-done((bf16[272,128]{1,0:T(8,128)(2,1)S(1)}, bf16[272,128]{1,0:T(8,128)(2,1)S(1)}, u32[]{:S(2)}, u32[]{:S(2)}) %collective-permute-start.18) | collective-permute-done | bytes 69664 | tf_op jit(solution)/shard_map/ppermute | solution.py:20
  53.4 2.6 %collective-permute-start.20 = (bf16[272,128]{1,0:T(8,128)(2,1)S(1)}, bf16[272,128]{1,0:T(8,128)(2,1)S(1)}, u32[]{:S(2)}, u32[]{:S(2)}) collective-permute-start(bf16[272,128]{1,0:T(8,128)(2,1)S(1)} %pad_maximum_fusion.1), channel_id=1, source_target_pairs={{0,16},{2,18},{4,20},{6,22},{8,24},{10,26},{12,28},{14,30},{16,0},... | collective-permute-start | bytes 208904 | tf_op jit(solution)/shard_map/ppermute | solution.py:20
  56.0 1.7 %collective-permute-start.21 = (bf16[272,128]{1,0:T(8,128)(2,1)S(1)}, bf16[272,128]{1,0:T(8,128)(2,1)S(1)}, u32[]{:S(2)}, u32[]{:S(2)}) collective-permute-start(bf16[272,128]{1,0:T(8,128)(2,1)S(1)} %pad_maximum_fusion.1), channel_id=1, source_target_pairs={{0,24},{2,26},{4,28},{6,30},{8,16},{10,18},{12,20},{14,22},{16,8},... | collective-permute-start | bytes 208904 | tf_op jit(solution)/shard_map/ppermute | solution.py:20
  58.4 2.6 %collective-permute-done.20.refs_1_ = bf16[272,128]{1,0:T(8,128)(2,1)S(1)} collective-permute-done((bf16[272,128]{1,0:T(8,128)(2,1)S(1)}, bf16[272,128]{1,0:T(8,128)(2,1)S(1)}, u32[]{:S(2)}, u32[]{:S(2)}) %collective-permute-start.20) | collective-permute-done | bytes 69664 | tf_op jit(solution)/shard_map/ppermute | solution.py:20
  61.0 1.2 %collective-permute-done.21.refs_2_ = bf16[272,128]{1,0:T(8,128)(2,1)S(1)} collective-permute-done((bf16[272,128]{1,0:T(8,128)(2,1)S(1)}, bf16[272,128]{1,0:T(8,128)(2,1)S(1)}, u32[]{:S(2)}, u32[]{:S(2)}) %collective-permute-start.21) | collective-permute-done | bytes 69664 | tf_op jit(solution)/shard_map/ppermute | solution.py:20
  (54 shorter events, 9.2 us)
Async XLA Ops:
  0.6 16.3 %collective-permute-start = (bf16[8,128,128]{2,1,0:T(8,128)(2,1)}, bf16[8,128,128]{2,1,0:T(8,128)(2,1)S(1)}, u32[]{:S(2)}, u32[]{:S(2)}) collective-permute-start(bf16[8,128,128]{2,1,0:T(8,128)(2,1)} %bitcast.20), channel_id=1, source_target_pairs={{0,16},{2,18},{4,20},{6,22},{8,24},{10,26},{12,28},{14,30},{16,0},... | collective-permute-start | bytes 786440 | tf_op jit(solution)/shard_map/ppermute | solution.py:20
  4.7 13.0 %collective-permute-start.4 = (bf16[8,128,128]{2,1,0:T(8,128)(2,1)}, bf16[8,128,128]{2,1,0:T(8,128)(2,1)S(1)}, u32[]{:S(2)}, u32[]{:S(2)}) collective-permute-start(bf16[8,128,128]{2,1,0:T(8,128)(2,1)} %bitcast.21), channel_id=1, source_target_pairs={{0,8},{2,10},{4,12},{6,14},{8,0},{10,2},{12,4},{14,6},{16,24},{18,... | collective-permute-start | bytes 786440 | tf_op jit(solution)/shard_map/ppermute | solution.py:20
  6.3 25.5 %copy-start.3 = (s32[1,16,2]{1,2,0:T(2,128)S(1)}, s32[1,16,2]{1,2,0:T(2,128)}, u32[]{:S(2)}) copy-start(s32[1,16,2]{1,2,0:T(2,128)} %param.11) | copy-start | bytes 388
  6.3 25.5 %copy-start.4 = (s32[1,16,2]{1,2,0:T(2,128)S(1)}, s32[1,16,2]{1,2,0:T(2,128)}, u32[]{:S(2)}) copy-start(s32[1,16,2]{1,2,0:T(2,128)} %param.13) | copy-start | bytes 388
  6.3 6.5 %collective-permute-start.1 = (s32[2,16]{1,0:T(2,128)}, s32[2,16]{1,0:T(2,128)S(1)}, u32[]{:S(2)}, u32[]{:S(2)}) collective-permute-start(s32[2,16]{1,0:T(2,128)} %bitcast.29), channel_id=1, source_target_pairs={{0,2},{2,0},{4,6},{6,4},{8,10},{10,8},{12,14},{14,12},{16,18},{18,... | collective-permute-start | bytes 392 | tf_op jit(solution)/shard_map/ppermute | solution.py:20
  7.8 5.0 %collective-permute-start.2 = (s32[2,16]{1,0:T(2,128)}, s32[2,16]{1,0:T(2,128)S(1)}, u32[]{:S(2)}, u32[]{:S(2)}) collective-permute-start(s32[2,16]{1,0:T(2,128)} %bitcast.30), channel_id=1, source_target_pairs={{0,4},{2,6},{4,0},{6,2},{8,12},{10,14},{12,8},{14,10},{16,20},{18,... | collective-permute-start | bytes 392 | tf_op jit(solution)/shard_map/ppermute | solution.py:20
  9.3 4.7 %collective-permute-start.3 = (s32[2,16]{1,0:T(2,128)}, s32[2,16]{1,0:T(2,128)S(1)}, u32[]{:S(2)}, u32[]{:S(2)}) collective-permute-start(s32[2,16]{1,0:T(2,128)} %bitcast.31), channel_id=1, source_target_pairs={{0,6},{2,4},{4,2},{6,0},{8,14},{10,12},{12,10},{14,8},{16,22},{18,... | collective-permute-start | bytes 392 | tf_op jit(solution)/shard_map/ppermute | solution.py:20
  17.0 7.4 %collective-permute-start.8 = (bf16[8,128,128]{2,1,0:T(8,128)(2,1)S(1)}, bf16[8,128,128]{2,1,0:T(8,128)(2,1)S(1)}, u32[]{:S(2)}, u32[]{:S(2)}) collective-permute-start(bf16[8,128,128]{2,1,0:T(8,128)(2,1)S(1)} %collective-permute-done.refs_5_), channel_id=1, source_target_pairs={{0,8},{2,10},{4,12},{6,14},{8,0},{10,2},{12,4},{14,6},{16,24},{18,... | collective-permute-start | bytes 786440 | tf_op jit(solution)/shard_map/ppermute | solution.py:20
  18.3 9.5 %collective-permute-start.6 = (bf16[6,128,128]{2,1,0:T(8,128)(2,1)S(1)}, bf16[6,128,128]{2,1,0:T(8,128)(2,1)S(1)}, u32[]{:S(2)}, u32[]{:S(2)}) collective-permute-start(bf16[6,128,128]{2,1,0:T(8,128)(2,1)S(1)} %get-tuple-element.32), channel_id=1, source_target_pairs={{0,4},{2,6},{4,0},{6,2},{8,12},{10,14},{12,8},{14,10},{16,20},{18,... | collective-permute-start | bytes 589832 | tf_op jit(solution)/shard_map/ppermute | solution.py:20
  19.9 8.7 %collective-permute-start.5 = (bf16[6,128,128]{2,1,0:T(8,128)(2,1)S(1)}, bf16[6,128,128]{2,1,0:T(8,128)(2,1)S(1)}, u32[]{:S(2)}, u32[]{:S(2)}) collective-permute-start(bf16[6,128,128]{2,1,0:T(8,128)(2,1)S(1)} %get-tuple-element.31), channel_id=1, source_target_pairs={{0,2},{2,0},{4,6},{6,4},{8,10},{10,8},{12,14},{14,12},{16,18},{18,... | collective-permute-start | bytes 589832 | tf_op jit(solution)/shard_map/ppermute | solution.py:20
  21.4 10.4 %collective-permute-start.7 = (bf16[6,128,128]{2,1,0:T(8,128)(2,1)S(1)}, bf16[6,128,128]{2,1,0:T(8,128)(2,1)S(1)}, u32[]{:S(2)}, u32[]{:S(2)}) collective-permute-start(bf16[6,128,128]{2,1,0:T(8,128)(2,1)S(1)} %get-tuple-element.33), channel_id=1, source_target_pairs={{0,6},{2,4},{4,2},{6,0},{8,14},{10,12},{12,10},{14,8},{16,22},{18,... | collective-permute-start | bytes 589832 | tf_op jit(solution)/shard_map/ppermute | solution.py:20
  25.0 7.9 %collective-permute-start.9 = (bf16[2,128,128]{2,1,0:T(8,128)(2,1)S(1)}, bf16[2,128,128]{2,1,0:T(8,128)(2,1)S(1)}, u32[]{:S(2)}, u32[]{:S(2)}) collective-permute-start(bf16[2,128,128]{2,1,0:T(8,128)(2,1)S(1)} %get-tuple-element.35), channel_id=1, source_target_pairs={{0,2},{2,0},{4,6},{6,4},{8,10},{10,8},{12,14},{14,12},{16,18},{18,... | collective-permute-start | bytes 196616 | tf_op jit(solution)/shard_map/ppermute | solution.py:20
  26.4 6.6 %collective-permute-start.10 = (bf16[2,128,128]{2,1,0:T(8,128)(2,1)S(1)}, bf16[2,128,128]{2,1,0:T(8,128)(2,1)S(1)}, u32[]{:S(2)}, u32[]{:S(2)}) collective-permute-start(bf16[2,128,128]{2,1,0:T(8,128)(2,1)S(1)} %get-tuple-element.36), channel_id=1, source_target_pairs={{0,4},{2,6},{4,0},{6,2},{8,12},{10,14},{12,8},{14,10},{16,20},{18,... | collective-permute-start | bytes 196616 | tf_op jit(solution)/shard_map/ppermute | solution.py:20
  27.9 5.3 %collective-permute-start.11 = (bf16[2,128,128]{2,1,0:T(8,128)(2,1)S(1)}, bf16[2,128,128]{2,1,0:T(8,128)(2,1)S(1)}, u32[]{:S(2)}, u32[]{:S(2)}) collective-permute-start(bf16[2,128,128]{2,1,0:T(8,128)(2,1)S(1)} %get-tuple-element.38), channel_id=1, source_target_pairs={{0,6},{2,4},{4,2},{6,0},{8,14},{10,12},{12,10},{14,8},{16,22},{18,... | collective-permute-start | bytes 196616 | tf_op jit(solution)/shard_map/ppermute | solution.py:20
  34.1 9.0 %collective-permute-start.12 = (bf16[4,128,128]{2,1,0:T(8,128)(2,1)S(1)}, bf16[4,128,128]{2,1,0:T(8,128)(2,1)S(1)}, u32[]{:S(2)}, u32[]{:S(2)}) collective-permute-start(bf16[4,128,128]{2,1,0:T(8,128)(2,1)S(1)} %get-tuple-element.40), channel_id=1, source_target_pairs={{30,0},{0,2},{2,4},{4,6},{6,8},{8,10},{10,12},{12,14},{14,16},{16,... | collective-permute-start | bytes 393224 | tf_op jit(solution)/shard_map/ppermute | solution.py:25
  35.6 8.8 %collective-permute-start.14 = (bf16[4,128,128]{2,1,0:T(8,128)(2,1)S(1)}, bf16[4,128,128]{2,1,0:T(8,128)(2,1)S(1)}, u32[]{:S(2)}, u32[]{:S(2)}) collective-permute-start(bf16[4,128,128]{2,1,0:T(8,128)(2,1)S(1)} %get-tuple-element.42), channel_id=1, source_target_pairs={{30,0},{0,2},{2,4},{4,6},{6,8},{8,10},{10,12},{12,14},{14,16},{16,... | collective-permute-start | bytes 393224 | tf_op jit(solution)/shard_map/ppermute | solution.py:25
  44.5 1.4 %collective-permute-start.13 = (bf16[512,128]{1,0:T(8,128)(2,1)S(1)}, bf16[512,128]{1,0:T(8,128)(2,1)S(1)}, u32[]{:S(2)}, u32[]{:S(2)}) collective-permute-start(bf16[512,128]{1,0:T(8,128)(2,1)S(1)} %bitcast.27), channel_id=1, source_target_pairs={{1,0},{0,1},{3,2},{2,3},{5,4},{4,5},{7,6},{6,7},{9,8},{8,9},{11,10... | collective-permute-start | bytes 393224 | tf_op jit(solution)/shard_map/ppermute | solution.py:25
  44.6 1.9 %collective-permute-start.15 = (bf16[512,128]{1,0:T(8,128)(2,1)S(1)}, bf16[512,128]{1,0:T(8,128)(2,1)S(1)}, u32[]{:S(2)}, u32[]{:S(2)}) collective-permute-start(bf16[512,128]{1,0:T(8,128)(2,1)S(1)} %bitcast.25), channel_id=1, source_target_pairs={{1,0},{0,1},{3,2},{2,3},{5,4},{4,5},{7,6},{6,7},{9,8},{8,9},{11,10... | collective-permute-start | bytes 393224 | tf_op jit(solution)/shard_map/ppermute | solution.py:25
  47.1 5.9 %collective-permute-start.18 = (bf16[272,128]{1,0:T(8,128)(2,1)S(1)}, bf16[272,128]{1,0:T(8,128)(2,1)S(1)}, u32[]{:S(2)}, u32[]{:S(2)}) collective-permute-start(bf16[272,128]{1,0:T(8,128)(2,1)S(1)} %get-tuple-element.47), channel_id=1, source_target_pairs={{0,6},{2,4},{4,2},{6,0},{8,14},{10,12},{12,10},{14,8},{16,22},{18,... | collective-permute-start | bytes 208904 | tf_op jit(solution)/shard_map/ppermute | solution.py:20
  47.2 5.9 %collective-permute-start.17 = (bf16[272,128]{1,0:T(8,128)(2,1)S(1)}, bf16[272,128]{1,0:T(8,128)(2,1)S(1)}, u32[]{:S(2)}, u32[]{:S(2)}) collective-permute-start(bf16[272,128]{1,0:T(8,128)(2,1)S(1)} %get-tuple-element.47), channel_id=1, source_target_pairs={{0,4},{2,6},{4,0},{6,2},{8,12},{10,14},{12,8},{14,10},{16,20},{18,... | collective-permute-start | bytes 208904 | tf_op jit(solution)/shard_map/ppermute | solution.py:20
  47.3 5.8 %collective-permute-start.16 = (bf16[272,128]{1,0:T(8,128)(2,1)S(1)}, bf16[272,128]{1,0:T(8,128)(2,1)S(1)}, u32[]{:S(2)}, u32[]{:S(2)}) collective-permute-start(bf16[272,128]{1,0:T(8,128)(2,1)S(1)} %get-tuple-element.47), channel_id=1, source_target_pairs={{0,2},{2,0},{4,6},{6,4},{8,10},{10,8},{12,14},{14,12},{16,18},{18,... | collective-permute-start | bytes 208904 | tf_op jit(solution)/shard_map/ppermute | solution.py:20
  53.3 5.2 %collective-permute-start.19 = (bf16[272,128]{1,0:T(8,128)(2,1)S(1)}, bf16[272,128]{1,0:T(8,128)(2,1)S(1)}, u32[]{:S(2)}, u32[]{:S(2)}) collective-permute-start(bf16[272,128]{1,0:T(8,128)(2,1)S(1)} %pad_maximum_fusion.1), channel_id=1, source_target_pairs={{0,8},{2,10},{4,12},{6,14},{8,0},{10,2},{12,4},{14,6},{16,24},{18,... | collective-permute-start | bytes 208904 | tf_op jit(solution)/shard_map/ppermute | solution.py:20
  53.4 7.5 %collective-permute-start.20 = (bf16[272,128]{1,0:T(8,128)(2,1)S(1)}, bf16[272,128]{1,0:T(8,128)(2,1)S(1)}, u32[]{:S(2)}, u32[]{:S(2)}) collective-permute-start(bf16[272,128]{1,0:T(8,128)(2,1)S(1)} %pad_maximum_fusion.1), channel_id=1, source_target_pairs={{0,16},{2,18},{4,20},{6,22},{8,24},{10,26},{12,28},{14,30},{16,0},... | collective-permute-start | bytes 208904 | tf_op jit(solution)/shard_map/ppermute | solution.py:20
  56.0 6.2 %collective-permute-start.21 = (bf16[272,128]{1,0:T(8,128)(2,1)S(1)}, bf16[272,128]{1,0:T(8,128)(2,1)S(1)}, u32[]{:S(2)}, u32[]{:S(2)}) collective-permute-start(bf16[272,128]{1,0:T(8,128)(2,1)S(1)} %pad_maximum_fusion.1), channel_id=1, source_target_pairs={{0,24},{2,26},{4,28},{6,30},{8,16},{10,18},{12,20},{14,22},{16,8},... | collective-permute-start | bytes 208904 | tf_op jit(solution)/shard_map/ppermute | solution.py:20
  (5 other events, 80.8 us)

commit v5 on v4

--- a/solution.py
+++ b/solution.py
@@ -343,6 +343,8 @@
     depth = own_blocks // SLABS
     before, new_rows = [], []
     for at, part in enumerate(incoming):
+        if new_rows:
+            part, other = lax.optimization_barrier((part, other))
         mine = (own[at * depth : (at + 1) * depth] + part.astype(jnp.float32)).astype(jnp.bfloat16)
         mine = mine.reshape(depth * block_size, half_width)
         other = passed_along(mine, "feat", 1)

time: 63.1 us -> 62.5 us (level)
  no operation moved by 1% of the time
where the time goes in v5:
time: 62.5 us; the launch traced here: 62.3 us
  starting transfers between devices  28.3 us (45%)
  waiting for transfers between devices  24.2 us (39%)
  Pallas kernels  7.97 us (13%)
  other arithmetic  0.89 us (1%)
  between operations  0.89 us (1%)
    ppermute x18, starting transfers between devices, partner(): return lax.ppermute(block, 'dom', [(i, i ^ bits) for i in range(count)])  25 us
    ppermute x18, waiting for transfers between devices, partner(): return lax.ppermute(block, 'dom', [(i, i ^ bits) for i in range(count)])  16.3 us
    ppermute x4, waiting for transfers between devices, passed_along(): lax.ppermute(block, axis, [((i - distance) % count, i) for i in range(cou...  7.87 us
    ppermute x4, starting transfers between devices, passed_along(): lax.ppermute(block, axis, [((i - distance) % count, i) for i in range(cou...  3.32 us
    pallas_call x1, Pallas kernels, begin_sum(): pl.pallas_call(functools.partial(begin_kernel, chunks), out_shape=[jax.Sh...  3.01 us
    pallas_call x2, Pallas kernels, tile_sum(): pl.pallas_call(functools.partial(sum_kernel, places, cap, last), out_shap...  1.91 us
  transfers between devices with their start and end apart: 22, of which 11 were waited for; matrix products, arithmetic and copies ran while one was open for 1% of the time, Pallas kernels for 9%

profile of v5, /device:TPU:0, one launch (start us, length us, event | category | flops | bytes accessed | tf_op | source)
XLA Modules:
  0.0 62.3 jit_solution(3335187916256319836)
XLA Ops:
  0.6 4.1 %collective-permute-start = (bf16[8,128,128]{2,1,0:T(8,128)(2,1)}, bf16[8,128,128]{2,1,0:T(8,128)(2,1)S(1)}, u32[]{:S(2)}, u32[]{:S(2)}) collective-permute-start(bf16[8,128,128]{2,1,0:T(8,128)(2,1)} %bitcast.20), channel_id=1, source_target_pairs={{0,16},{2,18},{4,20},{6,22},{8,24},{10,26},{12,28},{14,30},{16,0},... | collective-permute-start | bytes 786440 | tf_op jit(solution)/shard_map/ppermute | solution.py:20
  4.7 1.6 %collective-permute-start.4 = (bf16[8,128,128]{2,1,0:T(8,128)(2,1)}, bf16[8,128,128]{2,1,0:T(8,128)(2,1)S(1)}, u32[]{:S(2)}, u32[]{:S(2)}) collective-permute-start(bf16[8,128,128]{2,1,0:T(8,128)(2,1)} %bitcast.21), channel_id=1, source_target_pairs={{0,8},{2,10},{4,12},{6,14},{8,0},{10,2},{12,4},{14,6},{16,24},{18,... | collective-permute-start | bytes 786440 | tf_op jit(solution)/shard_map/ppermute | solution.py:20
  6.3 1.5 %collective-permute-start.1 = (s32[2,16]{1,0:T(2,128)}, s32[2,16]{1,0:T(2,128)S(1)}, u32[]{:S(2)}, u32[]{:S(2)}) collective-permute-start(s32[2,16]{1,0:T(2,128)} %bitcast.29), channel_id=1, source_target_pairs={{0,2},{2,0},{4,6},{6,4},{8,10},{10,8},{12,14},{14,12},{16,18},{18,... | collective-permute-start | bytes 392 | tf_op jit(solution)/shard_map/ppermute | solution.py:20
  7.8 1.5 %collective-permute-start.2 = (s32[2,16]{1,0:T(2,128)}, s32[2,16]{1,0:T(2,128)S(1)}, u32[]{:S(2)}, u32[]{:S(2)}) collective-permute-start(s32[2,16]{1,0:T(2,128)} %bitcast.30), channel_id=1, source_target_pairs={{0,4},{2,6},{4,0},{6,2},{8,12},{10,14},{12,8},{14,10},{16,20},{18,... | collective-permute-start | bytes 392 | tf_op jit(solution)/shard_map/ppermute | solution.py:20
  9.8 3.0 %shard_map.121.acc_in = f32[16,128,128]{2,1,0:T(8,128)S(1)} custom-call(s32[1,64]{1,0:T(1,128)} %refs_0_.1, s32[1,64]{1,0:T(1,128)} %refs_1_.1, bf16[8,128,128]{2,1,0:T(8,128)(2,1)} %bitcast.22, bf16[64,128,128]{2,1,0:T(8,128)(2,1)} %refs_3_.1), custom_call_target="tpu_custom_call" | custom-call | tf_op jit(solution)/shard_map/pallas_call | solution.py:79
  12.9 1.2 %collective-permute-done.3.refs_2_ = s32[2,16]{1,0:T(2,128)S(1)} collective-permute-done((s32[2,16]{1,0:T(2,128)}, s32[2,16]{1,0:T(2,128)S(1)}, u32[]{:S(2)}, u32[]{:S(2)}) %collective-permute-start.3) | collective-permute-done | bytes 160 | tf_op jit(solution)/shard_map/ppermute | solution.py:20
  14.0 3.0 %collective-permute-done.refs_5_ = bf16[8,128,128]{2,1,0:T(8,128)(2,1)S(1)} collective-permute-done((bf16[8,128,128]{2,1,0:T(8,128)(2,1)}, bf16[8,128,128]{2,1,0:T(8,128)(2,1)S(1)}, u32[]{:S(2)}, u32[]{:S(2)}) %collective-permute-start) | collective-permute-done | bytes 262176 | tf_op jit(solution)/shard_map/ppermute | solution.py:20
  18.3 1.6 %collective-permute-start.6 = (bf16[6,128,128]{2,1,0:T(8,128)(2,1)S(1)}, bf16[6,128,128]{2,1,0:T(8,128)(2,1)S(1)}, u32[]{:S(2)}, u32[]{:S(2)}) collective-permute-start(bf16[6,128,128]{2,1,0:T(8,128)(2,1)S(1)} %get-tuple-element.33), channel_id=1, source_target_pairs={{0,4},{2,6},{4,0},{6,2},{8,12},{10,14},{12,8},{14,10},{16,20},{18,... | collective-permute-start | bytes 589832 | tf_op jit(solution)/shard_map/ppermute | solution.py:20
  19.9 1.5 %collective-permute-start.5 = (bf16[6,128,128]{2,1,0:T(8,128)(2,1)S(1)}, bf16[6,128,128]{2,1,0:T(8,128)(2,1)S(1)}, u32[]{:S(2)}, u32[]{:S(2)}) collective-permute-start(bf16[6,128,128]{2,1,0:T(8,128)(2,1)S(1)} %get-tuple-element.32), channel_id=1, source_target_pairs={{0,2},{2,0},{4,6},{6,4},{8,10},{10,8},{12,14},{14,12},{16,18},{18,... | collective-permute-start | bytes 589832 | tf_op jit(solution)/shard_map/ppermute | solution.py:20
  21.9 2.5 %collective-permute-done.8.refs_3_.refs_0_ = bf16[8,128,128]{2,1,0:T(8,128)(2,1)S(1)} collective-permute-done((bf16[8,128,128]{2,1,0:T(8,128)(2,1)S(1)}, bf16[8,128,128]{2,1,0:T(8,128)(2,1)S(1)}, u32[]{:S(2)}, u32[]{:S(2)}) %collective-permute-start.8) | collective-permute-done | bytes 262176 | tf_op jit(solution)/shard_map/ppermute | solution.py:20
  25.0 1.3 %collective-permute-start.9 = (bf16[2,128,128]{2,1,0:T(8,128)(2,1)S(1)}, bf16[2,128,128]{2,1,0:T(8,128)(2,1)S(1)}, u32[]{:S(2)}, u32[]{:S(2)}) collective-permute-start(bf16[2,128,128]{2,1,0:T(8,128)(2,1)S(1)} %get-tuple-element.36), channel_id=1, source_target_pairs={{0,2},{2,0},{4,6},{6,4},{8,10},{10,8},{12,14},{14,12},{16,18},{18,... | collective-permute-start | bytes 196616 | tf_op jit(solution)/shard_map/ppermute | solution.py:20
  26.4 1.5 %collective-permute-start.10 = (bf16[2,128,128]{2,1,0:T(8,128)(2,1)S(1)}, bf16[2,128,128]{2,1,0:T(8,128)(2,1)S(1)}, u32[]{:S(2)}, u32[]{:S(2)}) collective-permute-start(bf16[2,128,128]{2,1,0:T(8,128)(2,1)S(1)} %get-tuple-element.37), channel_id=1, source_target_pairs={{0,4},{2,6},{4,0},{6,2},{8,12},{10,14},{12,8},{14,10},{16,20},{18,... | collective-permute-start | bytes 196616 | tf_op jit(solution)/shard_map/ppermute | solution.py:20
  28.6 3.3 %collective-permute-done.7.refs_3_ = bf16[6,128,128]{2,1,0:T(8,128)(2,1)S(1)} collective-permute-done((bf16[6,128,128]{2,1,0:T(8,128)(2,1)S(1)}, bf16[6,128,128]{2,1,0:T(8,128)(2,1)S(1)}, u32[]{:S(2)}, u32[]{:S(2)}) %collective-permute-start.7) | collective-permute-done | bytes 196640 | tf_op jit(solution)/shard_map/ppermute | solution.py:20
  31.9 1.0 %shard_map.123.acc_in = f32[16,128,128]{2,1,0:T(8,128)S(1)} custom-call(s32[1]{0:T(128)} %bitcast.me_ref, s32[2,16]{1,0:T(2,128)S(1)} %bitcast.32, s32[2,16]{1,0:T(2,128)S(1)} %bitcast.34, bf16[32,128,128]{2,1,0:T(8,128)(2,1)S(1)} %bitcast.18, f32[16,128,128]{2,1,0:T(8,128)S(1)} %shard_map.121.acc_in, bf16[8,128,128]{2,1,0:T(8,128)(2,1)S(1)} %bitcast.24, ...), custom_call_target="tpu_custom_call" | custom-call | tf_op jit(solution)/shard_map/pallas_call | solution.py:136
  34.1 1.6 %collective-permute-start.12 = (bf16[4,128,128]{2,1,0:T(8,128)(2,1)S(1)}, bf16[4,128,128]{2,1,0:T(8,128)(2,1)S(1)}, u32[]{:S(2)}, u32[]{:S(2)}) collective-permute-start(bf16[4,128,128]{2,1,0:T(8,128)(2,1)S(1)} %get-tuple-element.41), channel_id=1, source_target_pairs={{30,0},{0,2},{2,4},{4,6},{6,8},{8,10},{10,12},{12,14},{14,16},{16,... | collective-permute-start | bytes 393224 | tf_op jit(solution)/shard_map/ppermute | solution.py:25
  35.6 1.5 %collective-permute-start.14 = (bf16[4,128,128]{2,1,0:T(8,128)(2,1)S(1)}, bf16[4,128,128]{2,1,0:T(8,128)(2,1)S(1)}, u32[]{:S(2)}, u32[]{:S(2)}) collective-permute-start(bf16[4,128,128]{2,1,0:T(8,128)(2,1)S(1)} %get-tuple-element.43), channel_id=1, source_target_pairs={{30,0},{0,2},{2,4},{4,6},{6,8},{8,10},{10,12},{12,14},{14,16},{16,... | collective-permute-start | bytes 393224 | tf_op jit(solution)/shard_map/ppermute | solution.py:25
  37.1 6.0 %collective-permute-done.12 = bf16[4,128,128]{2,1,0:T(8,128)(2,1)S(1)} collective-permute-done((bf16[4,128,128]{2,1,0:T(8,128)(2,1)S(1)}, bf16[4,128,128]{2,1,0:T(8,128)(2,1)S(1)}, u32[]{:S(2)}, u32[]{:S(2)}) %collective-permute-start.12) | collective-permute-done | bytes 131104 | tf_op jit(solution)/shard_map/ppermute | solution.py:25
  43.2 1.3 %collective-permute-done.14 = bf16[4,128,128]{2,1,0:T(8,128)(2,1)S(1)} collective-permute-done((bf16[4,128,128]{2,1,0:T(8,128)(2,1)S(1)}, bf16[4,128,128]{2,1,0:T(8,128)(2,1)S(1)}, u32[]{:S(2)}, u32[]{:S(2)}) %collective-permute-start.14) | collective-permute-done | bytes 131104 | tf_op jit(solution)/shard_map/ppermute | solution.py:25
  46.7 3.4 %collective-permute-start.16 = (bf16[272,128]{1,0:T(8,128)(2,1)S(1)}, bf16[272,128]{1,0:T(8,128)(2,1)S(1)}, u32[]{:S(2)}, u32[]{:S(2)}) collective-permute-start(bf16[272,128]{1,0:T(8,128)(2,1)S(1)} %get-tuple-element.49), channel_id=1, source_target_pairs={{0,2},{2,0},{4,6},{6,4},{8,10},{10,8},{12,14},{14,12},{16,18},{18,... | collective-permute-start | bytes 208904 | tf_op jit(solution)/shard_map/ppermute | solution.py:20
  50.1 2.4 %collective-permute-done.18 = bf16[272,128]{1,0:T(8,128)(2,1)S(1)} collective-permute-done((bf16[272,128]{1,0:T(8,128)(2,1)S(1)}, bf16[272,128]{1,0:T(8,128)(2,1)S(1)}, u32[]{:S(2)}, u32[]{:S(2)}) %collective-permute-start.18) | collective-permute-done | bytes 69664 | tf_op jit(solution)/shard_map/ppermute | solution.py:20
  52.8 2.6 %collective-permute-start.20 = (bf16[272,128]{1,0:T(8,128)(2,1)S(1)}, bf16[272,128]{1,0:T(8,128)(2,1)S(1)}, u32[]{:S(2)}, u32[]{:S(2)}) collective-permute-start(bf16[272,128]{1,0:T(8,128)(2,1)S(1)} %pad_maximum_fusion.1), channel_id=1, source_target_pairs={{0,16},{2,18},{4,20},{6,22},{8,24},{10,26},{12,28},{14,30},{16,0},... | collective-permute-start | bytes 208904 | tf_op jit(solution)/shard_map/ppermute | solution.py:20
  55.4 1.7 %collective-permute-start.21 = (bf16[272,128]{1,0:T(8,128)(2,1)S(1)}, bf16[272,128]{1,0:T(8,128)(2,1)S(1)}, u32[]{:S(2)}, u32[]{:S(2)}) collective-permute-start(bf16[272,128]{1,0:T(8,128)(2,1)S(1)} %pad_maximum_fusion.1), channel_id=1, source_target_pairs={{0,24},{2,26},{4,28},{6,30},{8,16},{10,18},{12,20},{14,22},{16,8},... | collective-permute-start | bytes 208904 | tf_op jit(solution)/shard_map/ppermute | solution.py:20
  57.8 2.6 %collective-permute-done.20.refs_1_ = bf16[272,128]{1,0:T(8,128)(2,1)S(1)} collective-permute-done((bf16[272,128]{1,0:T(8,128)(2,1)S(1)}, bf16[272,128]{1,0:T(8,128)(2,1)S(1)}, u32[]{:S(2)}, u32[]{:S(2)}) %collective-permute-start.20) | collective-permute-done | bytes 69664 | tf_op jit(solution)/shard_map/ppermute | solution.py:20
  60.4 1.2 %collective-permute-done.21.refs_2_ = bf16[272,128]{1,0:T(8,128)(2,1)S(1)} collective-permute-done((bf16[272,128]{1,0:T(8,128)(2,1)S(1)}, bf16[272,128]{1,0:T(8,128)(2,1)S(1)}, u32[]{:S(2)}, u32[]{:S(2)}) %collective-permute-start.21) | collective-permute-done | bytes 69664 | tf_op jit(solution)/shard_map/ppermute | solution.py:20
  (55 shorter events, 8.7 us)
Async XLA Ops:
  0.6 16.3 %collective-permute-start = (bf16[8,128,128]{2,1,0:T(8,128)(2,1)}, bf16[8,128,128]{2,1,0:T(8,128)(2,1)S(1)}, u32[]{:S(2)}, u32[]{:S(2)}) collective-permute-start(bf16[8,128,128]{2,1,0:T(8,128)(2,1)} %bitcast.20), channel_id=1, source_target_pairs={{0,16},{2,18},{4,20},{6,22},{8,24},{10,26},{12,28},{14,30},{16,0},... | collective-permute-start | bytes 786440 | tf_op jit(solution)/shard_map/ppermute | solution.py:20
  4.7 13.0 %collective-permute-start.4 = (bf16[8,128,128]{2,1,0:T(8,128)(2,1)}, bf16[8,128,128]{2,1,0:T(8,128)(2,1)S(1)}, u32[]{:S(2)}, u32[]{:S(2)}) collective-permute-start(bf16[8,128,128]{2,1,0:T(8,128)(2,1)} %bitcast.21), channel_id=1, source_target_pairs={{0,8},{2,10},{4,12},{6,14},{8,0},{10,2},{12,4},{14,6},{16,24},{18,... | collective-permute-start | bytes 786440 | tf_op jit(solution)/shard_map/ppermute | solution.py:20
  6.3 25.5 %copy-start.3 = (s32[1,16,2]{1,2,0:T(2,128)S(1)}, s32[1,16,2]{1,2,0:T(2,128)}, u32[]{:S(2)}) copy-start(s32[1,16,2]{1,2,0:T(2,128)} %param.11) | copy-start | bytes 388
  6.3 25.5 %copy-start.4 = (s32[1,16,2]{1,2,0:T(2,128)S(1)}, s32[1,16,2]{1,2,0:T(2,128)}, u32[]{:S(2)}) copy-start(s32[1,16,2]{1,2,0:T(2,128)} %param.13) | copy-start | bytes 388
  6.3 6.5 %collective-permute-start.1 = (s32[2,16]{1,0:T(2,128)}, s32[2,16]{1,0:T(2,128)S(1)}, u32[]{:S(2)}, u32[]{:S(2)}) collective-permute-start(s32[2,16]{1,0:T(2,128)} %bitcast.29), channel_id=1, source_target_pairs={{0,2},{2,0},{4,6},{6,4},{8,10},{10,8},{12,14},{14,12},{16,18},{18,... | collective-permute-start | bytes 392 | tf_op jit(solution)/shard_map/ppermute | solution.py:20
  7.8 5.0 %collective-permute-start.2 = (s32[2,16]{1,0:T(2,128)}, s32[2,16]{1,0:T(2,128)S(1)}, u32[]{:S(2)}, u32[]{:S(2)}) collective-permute-start(s32[2,16]{1,0:T(2,128)} %bitcast.30), channel_id=1, source_target_pairs={{0,4},{2,6},{4,0},{6,2},{8,12},{10,14},{12,8},{14,10},{16,20},{18,... | collective-permute-start | bytes 392 | tf_op jit(solution)/shard_map/ppermute | solution.py:20
  9.3 4.7 %collective-permute-start.3 = (s32[2,16]{1,0:T(2,128)}, s32[2,16]{1,0:T(2,128)S(1)}, u32[]{:S(2)}, u32[]{:S(2)}) collective-permute-start(s32[2,16]{1,0:T(2,128)} %bitcast.31), channel_id=1, source_target_pairs={{0,6},{2,4},{4,2},{6,0},{8,14},{10,12},{12,10},{14,8},{16,22},{18,... | collective-permute-start | bytes 392 | tf_op jit(solution)/shard_map/ppermute | solution.py:20
  17.0 7.4 %collective-permute-start.8 = (bf16[8,128,128]{2,1,0:T(8,128)(2,1)S(1)}, bf16[8,128,128]{2,1,0:T(8,128)(2,1)S(1)}, u32[]{:S(2)}, u32[]{:S(2)}) collective-permute-start(bf16[8,128,128]{2,1,0:T(8,128)(2,1)S(1)} %collective-permute-done.refs_5_), channel_id=1, source_target_pairs={{0,8},{2,10},{4,12},{6,14},{8,0},{10,2},{12,4},{14,6},{16,24},{18,... | collective-permute-start | bytes 786440 | tf_op jit(solution)/shard_map/ppermute | solution.py:20
  18.3 9.5 %collective-permute-start.6 = (bf16[6,128,128]{2,1,0:T(8,128)(2,1)S(1)}, bf16[6,128,128]{2,1,0:T(8,128)(2,1)S(1)}, u32[]{:S(2)}, u32[]{:S(2)}) collective-permute-start(bf16[6,128,128]{2,1,0:T(8,128)(2,1)S(1)} %get-tuple-element.33), channel_id=1, source_target_pairs={{0,4},{2,6},{4,0},{6,2},{8,12},{10,14},{12,8},{14,10},{16,20},{18,... | collective-permute-start | bytes 589832 | tf_op jit(solution)/shard_map/ppermute | solution.py:20
  19.9 8.7 %collective-permute-start.5 = (bf16[6,128,128]{2,1,0:T(8,128)(2,1)S(1)}, bf16[6,128,128]{2,1,0:T(8,128)(2,1)S(1)}, u32[]{:S(2)}, u32[]{:S(2)}) collective-permute-start(bf16[6,128,128]{2,1,0:T(8,128)(2,1)S(1)} %get-tuple-element.32), channel_id=1, source_target_pairs={{0,2},{2,0},{4,6},{6,4},{8,10},{10,8},{12,14},{14,12},{16,18},{18,... | collective-permute-start | bytes 589832 | tf_op jit(solution)/shard_map/ppermute | solution.py:20
  21.4 10.4 %collective-permute-start.7 = (bf16[6,128,128]{2,1,0:T(8,128)(2,1)S(1)}, bf16[6,128,128]{2,1,0:T(8,128)(2,1)S(1)}, u32[]{:S(2)}, u32[]{:S(2)}) collective-permute-start(bf16[6,128,128]{2,1,0:T(8,128)(2,1)S(1)} %get-tuple-element.34), channel_id=1, source_target_pairs={{0,6},{2,4},{4,2},{6,0},{8,14},{10,12},{12,10},{14,8},{16,22},{18,... | collective-permute-start | bytes 589832 | tf_op jit(solution)/shard_map/ppermute | solution.py:20
  25.0 7.9 %collective-permute-start.9 = (bf16[2,128,128]{2,1,0:T(8,128)(2,1)S(1)}, bf16[2,128,128]{2,1,0:T(8,128)(2,1)S(1)}, u32[]{:S(2)}, u32[]{:S(2)}) collective-permute-start(bf16[2,128,128]{2,1,0:T(8,128)(2,1)S(1)} %get-tuple-element.36), channel_id=1, source_target_pairs={{0,2},{2,0},{4,6},{6,4},{8,10},{10,8},{12,14},{14,12},{16,18},{18,... | collective-permute-start | bytes 196616 | tf_op jit(solution)/shard_map/ppermute | solution.py:20
  26.4 6.6 %collective-permute-start.10 = (bf16[2,128,128]{2,1,0:T(8,128)(2,1)S(1)}, bf16[2,128,128]{2,1,0:T(8,128)(2,1)S(1)}, u32[]{:S(2)}, u32[]{:S(2)}) collective-permute-start(bf16[2,128,128]{2,1,0:T(8,128)(2,1)S(1)} %get-tuple-element.37), channel_id=1, source_target_pairs={{0,4},{2,6},{4,0},{6,2},{8,12},{10,14},{12,8},{14,10},{16,20},{18,... | collective-permute-start | bytes 196616 | tf_op jit(solution)/shard_map/ppermute | solution.py:20
  27.9 5.3 %collective-permute-start.11 = (bf16[2,128,128]{2,1,0:T(8,128)(2,1)S(1)}, bf16[2,128,128]{2,1,0:T(8,128)(2,1)S(1)}, u32[]{:S(2)}, u32[]{:S(2)}) collective-permute-start(bf16[2,128,128]{2,1,0:T(8,128)(2,1)S(1)} %get-tuple-element.39), channel_id=1, source_target_pairs={{0,6},{2,4},{4,2},{6,0},{8,14},{10,12},{12,10},{14,8},{16,22},{18,... | collective-permute-start | bytes 196616 | tf_op jit(solution)/shard_map/ppermute | solution.py:20
  34.1 9.0 %collective-permute-start.12 = (bf16[4,128,128]{2,1,0:T(8,128)(2,1)S(1)}, bf16[4,128,128]{2,1,0:T(8,128)(2,1)S(1)}, u32[]{:S(2)}, u32[]{:S(2)}) collective-permute-start(bf16[4,128,128]{2,1,0:T(8,128)(2,1)S(1)} %get-tuple-element.41), channel_id=1, source_target_pairs={{30,0},{0,2},{2,4},{4,6},{6,8},{8,10},{10,12},{12,14},{14,16},{16,... | collective-permute-start | bytes 393224 | tf_op jit(solution)/shard_map/ppermute | solution.py:25
  35.6 8.8 %collective-permute-start.14 = (bf16[4,128,128]{2,1,0:T(8,128)(2,1)S(1)}, bf16[4,128,128]{2,1,0:T(8,128)(2,1)S(1)}, u32[]{:S(2)}, u32[]{:S(2)}) collective-permute-start(bf16[4,128,128]{2,1,0:T(8,128)(2,1)S(1)} %get-tuple-element.43), channel_id=1, source_target_pairs={{30,0},{0,2},{2,4},{4,6},{6,8},{8,10},{10,12},{12,14},{14,16},{16,... | collective-permute-start | bytes 393224 | tf_op jit(solution)/shard_map/ppermute | solution.py:25
  43.1 1.4 %collective-permute-start.13 = (bf16[512,128]{1,0:T(8,128)(2,1)S(1)}, bf16[512,128]{1,0:T(8,128)(2,1)S(1)}, u32[]{:S(2)}, u32[]{:S(2)}) collective-permute-start(bf16[512,128]{1,0:T(8,128)(2,1)S(1)} %bitcast.25), channel_id=1, source_target_pairs={{1,0},{0,1},{3,2},{2,3},{5,4},{4,5},{7,6},{6,7},{9,8},{8,9},{11,10... | collective-permute-start | bytes 393224 | tf_op jit(solution)/shard_map/ppermute | solution.py:25
  44.5 1.4 %collective-permute-start.15 = (bf16[512,128]{1,0:T(8,128)(2,1)S(1)}, bf16[512,128]{1,0:T(8,128)(2,1)S(1)}, u32[]{:S(2)}, u32[]{:S(2)}) collective-permute-start(bf16[512,128]{1,0:T(8,128)(2,1)S(1)} %bitcast.27), channel_id=1, source_target_pairs={{1,0},{0,1},{3,2},{2,3},{5,4},{4,5},{7,6},{6,7},{9,8},{8,9},{11,10... | collective-permute-start | bytes 393224 | tf_op jit(solution)/shard_map/ppermute | solution.py:25
  46.5 5.9 %collective-permute-start.18 = (bf16[272,128]{1,0:T(8,128)(2,1)S(1)}, bf16[272,128]{1,0:T(8,128)(2,1)S(1)}, u32[]{:S(2)}, u32[]{:S(2)}) collective-permute-start(bf16[272,128]{1,0:T(8,128)(2,1)S(1)} %get-tuple-element.49), channel_id=1, source_target_pairs={{0,6},{2,4},{4,2},{6,0},{8,14},{10,12},{12,10},{14,8},{16,22},{18,... | collective-permute-start | bytes 208904 | tf_op jit(solution)/shard_map/ppermute | solution.py:20
  46.6 5.9 %collective-permute-start.17 = (bf16[272,128]{1,0:T(8,128)(2,1)S(1)}, bf16[272,128]{1,0:T(8,128)(2,1)S(1)}, u32[]{:S(2)}, u32[]{:S(2)}) collective-permute-start(bf16[272,128]{1,0:T(8,128)(2,1)S(1)} %get-tuple-element.49), channel_id=1, source_target_pairs={{0,4},{2,6},{4,0},{6,2},{8,12},{10,14},{12,8},{14,10},{16,20},{18,... | collective-permute-start | bytes 208904 | tf_op jit(solution)/shard_map/ppermute | solution.py:20
  46.7 5.8 %collective-permute-start.16 = (bf16[272,128]{1,0:T(8,128)(2,1)S(1)}, bf16[272,128]{1,0:T(8,128)(2,1)S(1)}, u32[]{:S(2)}, u32[]{:S(2)}) collective-permute-start(bf16[272,128]{1,0:T(8,128)(2,1)S(1)} %get-tuple-element.49), channel_id=1, source_target_pairs={{0,2},{2,0},{4,6},{6,4},{8,10},{10,8},{12,14},{14,12},{16,18},{18,... | collective-permute-start | bytes 208904 | tf_op jit(solution)/shard_map/ppermute | solution.py:20
  52.7 5.2 %collective-permute-start.19 = (bf16[272,128]{1,0:T(8,128)(2,1)S(1)}, bf16[272,128]{1,0:T(8,128)(2,1)S(1)}, u32[]{:S(2)}, u32[]{:S(2)}) collective-permute-start(bf16[272,128]{1,0:T(8,128)(2,1)S(1)} %pad_maximum_fusion.1), channel_id=1, source_target_pairs={{0,8},{2,10},{4,12},{6,14},{8,0},{10,2},{12,4},{14,6},{16,24},{18,... | collective-permute-start | bytes 208904 | tf_op jit(solution)/shard_map/ppermute | solution.py:20
  52.8 7.5 %collective-permute-start.20 = (bf16[272,128]{1,0:T(8,128)(2,1)S(1)}, bf16[272,128]{1,0:T(8,128)(2,1)S(1)}, u32[]{:S(2)}, u32[]{:S(2)}) collective-permute-start(bf16[272,128]{1,0:T(8,128)(2,1)S(1)} %pad_maximum_fusion.1), channel_id=1, source_target_pairs={{0,16},{2,18},{4,20},{6,22},{8,24},{10,26},{12,28},{14,30},{16,0},... | collective-permute-start | bytes 208904 | tf_op jit(solution)/shard_map/ppermute | solution.py:20
  55.4 6.2 %collective-permute-start.21 = (bf16[272,128]{1,0:T(8,128)(2,1)S(1)}, bf16[272,128]{1,0:T(8,128)(2,1)S(1)}, u32[]{:S(2)}, u32[]{:S(2)}) collective-permute-start(bf16[272,128]{1,0:T(8,128)(2,1)S(1)} %pad_maximum_fusion.1), channel_id=1, source_target_pairs={{0,24},{2,26},{4,28},{6,30},{8,16},{10,18},{12,20},{14,22},{16,8},... | collective-permute-start | bytes 208904 | tf_op jit(solution)/shard_map/ppermute | solution.py:20
  (5 other events, 78.1 us)

commit v6 on v5

--- a/solution.py
+++ b/solution.py
@@ -184,9 +184,8 @@
         high = bias_sum.astype(sent.dtype).astype(jnp.float32)
         low = (bias_sum - high).astype(sent.dtype).astype(jnp.float32)
         bias_out[...] = high + low
-        for row in (high, low):
-            sent[at : at + 8] = jnp.broadcast_to(row, (8, width)).astype(sent.dtype)
-            at += 8
+        rows = [jnp.broadcast_to(row, (8, width)) for row in (high, low)]
+        sent[at : at + 16] = jnp.concatenate(rows).astype(sent.dtype)
     else:
         weight_out[: weight_mine.shape[0]] = terms[0]
         weight_out[weight_mine.shape[0] :] = terms[1]
@@ -300,21 +299,15 @@
     tiles = remote_tiles.reshape(-1, block_size, block_size)
     shared = (me, wanted, remote_dst[0].T, tiles)
 
-    def exchange(members, after, hold=None):
-        arrays = [held[k] for k in members]
-        if after:
-            arrays[0], *_ = lax.optimization_barrier((arrays[0], *after))
-        picked = list(select_blocks(me, asked, members, arrays, cap))
-        for j in [3]:
-            if len(members) == 1:
-                picked[j - 1], _ = lax.optimization_barrier((picked[j - 1], hold))
+    def exchange(members):
+        picked = select_blocks(me, asked, members, [held[k] for k in members], cap)
         pulled = [partner(picked[j - 1], j) for j in range(1, PEERS)]
         sources = []
         for at, member in enumerate(members):
             sources.append((member * PEERS, held[member], None))
             for j in range(1, PEERS):
                 sources.append((member * PEERS + j, pulled[j - 1], at * cap))
-        return sources, pulled, picked
+        return sources
 
     held = {0: blocks}
     for member in range(columns // 2, 0, -1):
@@ -328,8 +321,8 @@
             source, acc, *asked = lax.optimization_barrier((held[member ^ low], acc, *asked))
             held[member] = partner(source, low * PEERS)
 
-    first, arrived, _ = exchange(list(range(columns - 1)), [])
-    rest, *_ = exchange([columns - 1], [], arrived[1])
+    first = exchange(list(range(columns - 1)))
+    rest = exchange([columns - 1])
     (acc,) = tile_sum(shared, acc, first, cap)
     outs = tile_sum(shared, acc, rest, cap, last=True)
     own, *following = outs

time: 62.5 us -> 62.5 us (level)
  no operation moved by 1% of the time
where the time goes in v6:
time: 62.5 us; the launch traced here: 62.3 us
  starting transfers between devices  28.3 us (45%)
  waiting for transfers between devices  24.2 us (39%)
  Pallas kernels  7.97 us (13%)
  between operations  0.9 us (1%)
  other arithmetic  0.89 us (1%)
    ppermute x18, starting transfers between devices, partner(): return lax.ppermute(block, 'dom', [(i, i ^ bits) for i in range(count)])  25 us
    ppermute x18, waiting for transfers between devices, partner(): return lax.ppermute(block, 'dom', [(i, i ^ bits) for i in range(count)])  16 us
    ppermute x4, waiting for transfers between devices, passed_along(): lax.ppermute(block, axis, [((i - distance) % count, i) for i in range(cou...  8.23 us
    ppermute x4, starting transfers between devices, passed_along(): lax.ppermute(block, axis, [((i - distance) % count, i) for i in range(cou...  3.32 us
    pallas_call x1, Pallas kernels, begin_sum(): pl.pallas_call(functools.partial(begin_kernel, chunks), out_shape=[jax.Sh...  3.01 us
    pallas_call x2, Pallas kernels, tile_sum(): pl.pallas_call(functools.partial(sum_kernel, places, cap, last), out_shap...  1.91 us
  transfers between devices with their start and end apart: 22, of which 11 were waited for; matrix products, arithmetic and copies ran while one was open for 1% of the time, Pallas kernels for 9%

profile of v6, /device:TPU:0, one launch (start us, length us, event | category | flops | bytes accessed | tf_op | source)
XLA Modules:
  0.0 62.3 jit_solution(18102256797292691126)
XLA Ops:
  0.6 4.1 %collective-permute-start = (bf16[8,128,128]{2,1,0:T(8,128)(2,1)}, bf16[8,128,128]{2,1,0:T(8,128)(2,1)S(1)}, u32[]{:S(2)}, u32[]{:S(2)}) collective-permute-start(bf16[8,128,128]{2,1,0:T(8,128)(2,1)} %bitcast.20), channel_id=1, source_target_pairs={{0,16},{2,18},{4,20},{6,22},{8,24},{10,26},{12,28},{14,30},{16,0},... | collective-permute-start | bytes 786440 | tf_op jit(solution)/shard_map/ppermute | solution.py:20
  4.7 1.6 %collective-permute-start.4 = (bf16[8,128,128]{2,1,0:T(8,128)(2,1)}, bf16[8,128,128]{2,1,0:T(8,128)(2,1)S(1)}, u32[]{:S(2)}, u32[]{:S(2)}) collective-permute-start(bf16[8,128,128]{2,1,0:T(8,128)(2,1)} %bitcast.21), channel_id=1, source_target_pairs={{0,8},{2,10},{4,12},{6,14},{8,0},{10,2},{12,4},{14,6},{16,24},{18,... | collective-permute-start | bytes 786440 | tf_op jit(solution)/shard_map/ppermute | solution.py:20
  6.3 1.5 %collective-permute-start.1 = (s32[2,16]{1,0:T(2,128)}, s32[2,16]{1,0:T(2,128)S(1)}, u32[]{:S(2)}, u32[]{:S(2)}) collective-permute-start(s32[2,16]{1,0:T(2,128)} %bitcast.29), channel_id=1, source_target_pairs={{0,2},{2,0},{4,6},{6,4},{8,10},{10,8},{12,14},{14,12},{16,18},{18,... | collective-permute-start | bytes 392 | tf_op jit(solution)/shard_map/ppermute | solution.py:20
  7.8 1.5 %collective-permute-start.2 = (s32[2,16]{1,0:T(2,128)}, s32[2,16]{1,0:T(2,128)S(1)}, u32[]{:S(2)}, u32[]{:S(2)}) collective-permute-start(s32[2,16]{1,0:T(2,128)} %bitcast.30), channel_id=1, source_target_pairs={{0,4},{2,6},{4,0},{6,2},{8,12},{10,14},{12,8},{14,10},{16,20},{18,... | collective-permute-start | bytes 392 | tf_op jit(solution)/shard_map/ppermute | solution.py:20
  9.8 3.0 %shard_map.121.acc_in = f32[16,128,128]{2,1,0:T(8,128)S(1)} custom-call(s32[1,64]{1,0:T(1,128)} %refs_0_.1, s32[1,64]{1,0:T(1,128)} %refs_1_.1, bf16[8,128,128]{2,1,0:T(8,128)(2,1)} %bitcast.22, bf16[64,128,128]{2,1,0:T(8,128)(2,1)} %refs_3_.1), custom_call_target="tpu_custom_call" | custom-call | tf_op jit(solution)/shard_map/pallas_call | solution.py:79
  12.9 1.2 %collective-permute-done.3.refs_2_ = s32[2,16]{1,0:T(2,128)S(1)} collective-permute-done((s32[2,16]{1,0:T(2,128)}, s32[2,16]{1,0:T(2,128)S(1)}, u32[]{:S(2)}, u32[]{:S(2)}) %collective-permute-start.3) | collective-permute-done | bytes 160 | tf_op jit(solution)/shard_map/ppermute | solution.py:20
  14.0 3.0 %collective-permute-done.refs_5_ = bf16[8,128,128]{2,1,0:T(8,128)(2,1)S(1)} collective-permute-done((bf16[8,128,128]{2,1,0:T(8,128)(2,1)}, bf16[8,128,128]{2,1,0:T(8,128)(2,1)S(1)}, u32[]{:S(2)}, u32[]{:S(2)}) %collective-permute-start) | collective-permute-done | bytes 262176 | tf_op jit(solution)/shard_map/ppermute | solution.py:20
  18.3 1.6 %collective-permute-start.5 = (bf16[6,128,128]{2,1,0:T(8,128)(2,1)S(1)}, bf16[6,128,128]{2,1,0:T(8,128)(2,1)S(1)}, u32[]{:S(2)}, u32[]{:S(2)}) collective-permute-start(bf16[6,128,128]{2,1,0:T(8,128)(2,1)S(1)} %get-tuple-element.31), channel_id=1, source_target_pairs={{0,2},{2,0},{4,6},{6,4},{8,10},{10,8},{12,14},{14,12},{16,18},{18,... | collective-permute-start | bytes 589832 | tf_op jit(solution)/shard_map/ppermute | solution.py:20
  19.9 1.5 %collective-permute-start.6 = (bf16[6,128,128]{2,1,0:T(8,128)(2,1)S(1)}, bf16[6,128,128]{2,1,0:T(8,128)(2,1)S(1)}, u32[]{:S(2)}, u32[]{:S(2)}) collective-permute-start(bf16[6,128,128]{2,1,0:T(8,128)(2,1)S(1)} %get-tuple-element.32), channel_id=1, source_target_pairs={{0,4},{2,6},{4,0},{6,2},{8,12},{10,14},{12,8},{14,10},{16,20},{18,... | collective-permute-start | bytes 589832 | tf_op jit(solution)/shard_map/ppermute | solution.py:20
  21.9 2.5 %collective-permute-done.8.refs_3_.refs_0_ = bf16[8,128,128]{2,1,0:T(8,128)(2,1)S(1)} collective-permute-done((bf16[8,128,128]{2,1,0:T(8,128)(2,1)S(1)}, bf16[8,128,128]{2,1,0:T(8,128)(2,1)S(1)}, u32[]{:S(2)}, u32[]{:S(2)}) %collective-permute-start.8) | collective-permute-done | bytes 262176 | tf_op jit(solution)/shard_map/ppermute | solution.py:20
  25.0 1.4 %collective-permute-start.10 = (bf16[2,128,128]{2,1,0:T(8,128)(2,1)S(1)}, bf16[2,128,128]{2,1,0:T(8,128)(2,1)S(1)}, u32[]{:S(2)}, u32[]{:S(2)}) collective-permute-start(bf16[2,128,128]{2,1,0:T(8,128)(2,1)S(1)} %get-tuple-element.36), channel_id=1, source_target_pairs={{0,4},{2,6},{4,0},{6,2},{8,12},{10,14},{12,8},{14,10},{16,20},{18,... | collective-permute-start | bytes 196616 | tf_op jit(solution)/shard_map/ppermute | solution.py:20
  26.4 1.4 %collective-permute-start.11 = (bf16[2,128,128]{2,1,0:T(8,128)(2,1)S(1)}, bf16[2,128,128]{2,1,0:T(8,128)(2,1)S(1)}, u32[]{:S(2)}, u32[]{:S(2)}) collective-permute-start(bf16[2,128,128]{2,1,0:T(8,128)(2,1)S(1)} %get-tuple-element.37), channel_id=1, source_target_pairs={{0,6},{2,4},{4,2},{6,0},{8,14},{10,12},{12,10},{14,8},{16,22},{18,... | collective-permute-start | bytes 196616 | tf_op jit(solution)/shard_map/ppermute | solution.py:20
  28.6 3.9 %collective-permute-done.6.refs_2_ = bf16[6,128,128]{2,1,0:T(8,128)(2,1)S(1)} collective-permute-done((bf16[6,128,128]{2,1,0:T(8,128)(2,1)S(1)}, bf16[6,128,128]{2,1,0:T(8,128)(2,1)S(1)}, u32[]{:S(2)}, u32[]{:S(2)}) %collective-permute-start.6) | collective-permute-done | bytes 196640 | tf_op jit(solution)/shard_map/ppermute | solution.py:20
  32.5 1.0 %shard_map.123.acc_in = f32[16,128,128]{2,1,0:T(8,128)S(1)} custom-call(s32[1]{0:T(128)} %bitcast.me_ref, s32[2,16]{1,0:T(2,128)S(1)} %bitcast.32, s32[2,16]{1,0:T(2,128)S(1)} %bitcast.34, bf16[32,128,128]{2,1,0:T(8,128)(2,1)S(1)} %bitcast.18, f32[16,128,128]{2,1,0:T(8,128)S(1)} %shard_map.121.acc_in, bf16[8,128,128]{2,1,0:T(8,128)(2,1)S(1)} %bitcast.24, ...), custom_call_target="tpu_custom_call" | custom-call | tf_op jit(solution)/shard_map/pallas_call | solution.py:136
  35.0 2.6 %collective-permute-start.14 = (bf16[4,128,128]{2,1,0:T(8,128)(2,1)S(1)}, bf16[4,128,128]{2,1,0:T(8,128)(2,1)S(1)}, u32[]{:S(2)}, u32[]{:S(2)}) collective-permute-start(bf16[4,128,128]{2,1,0:T(8,128)(2,1)S(1)} %get-tuple-element.41), channel_id=1, source_target_pairs={{30,0},{0,2},{2,4},{4,6},{6,8},{8,10},{10,12},{12,14},{14,16},{16,... | collective-permute-start | bytes 393224 | tf_op jit(solution)/shard_map/ppermute | solution.py:25
  37.5 6.3 %collective-permute-done.12 = bf16[4,128,128]{2,1,0:T(8,128)(2,1)S(1)} collective-permute-done((bf16[4,128,128]{2,1,0:T(8,128)(2,1)S(1)}, bf16[4,128,128]{2,1,0:T(8,128)(2,1)S(1)}, u32[]{:S(2)}, u32[]{:S(2)}) %collective-permute-start.12) | collective-permute-done | bytes 131104 | tf_op jit(solution)/shard_map/ppermute | solution.py:25
  44.0 1.3 %collective-permute-done.14 = bf16[4,128,128]{2,1,0:T(8,128)(2,1)S(1)} collective-permute-done((bf16[4,128,128]{2,1,0:T(8,128)(2,1)S(1)}, bf16[4,128,128]{2,1,0:T(8,128)(2,1)S(1)}, u32[]{:S(2)}, u32[]{:S(2)}) %collective-permute-start.14) | collective-permute-done | bytes 131104 | tf_op jit(solution)/shard_map/ppermute | solution.py:25
  47.5 3.4 %collective-permute-start.18 = (bf16[272,128]{1,0:T(8,128)(2,1)S(1)}, bf16[272,128]{1,0:T(8,128)(2,1)S(1)}, u32[]{:S(2)}, u32[]{:S(2)}) collective-permute-start(bf16[272,128]{1,0:T(8,128)(2,1)S(1)} %get-tuple-element.47), channel_id=1, source_target_pairs={{0,6},{2,4},{4,2},{6,0},{8,14},{10,12},{12,10},{14,8},{16,22},{18,... | collective-permute-start | bytes 208904 | tf_op jit(solution)/shard_map/ppermute | solution.py:20
  50.9 1.2 %collective-permute-done.16 = bf16[272,128]{1,0:T(8,128)(2,1)S(1)} collective-permute-done((bf16[272,128]{1,0:T(8,128)(2,1)S(1)}, bf16[272,128]{1,0:T(8,128)(2,1)S(1)}, u32[]{:S(2)}, u32[]{:S(2)}) %collective-permute-start.16) | collective-permute-done | bytes 69664 | tf_op jit(solution)/shard_map/ppermute | solution.py:20
  52.1 1.2 %collective-permute-done.17 = bf16[272,128]{1,0:T(8,128)(2,1)S(1)} collective-permute-done((bf16[272,128]{1,0:T(8,128)(2,1)S(1)}, bf16[272,128]{1,0:T(8,128)(2,1)S(1)}, u32[]{:S(2)}, u32[]{:S(2)}) %collective-permute-start.17) | collective-permute-done | bytes 69664 | tf_op jit(solution)/shard_map/ppermute | solution.py:20
  53.9 1.6 %collective-permute-start.20 = (bf16[272,128]{1,0:T(8,128)(2,1)S(1)}, bf16[272,128]{1,0:T(8,128)(2,1)S(1)}, u32[]{:S(2)}, u32[]{:S(2)}) collective-permute-start(bf16[272,128]{1,0:T(8,128)(2,1)S(1)} %pad_maximum_fusion.1), channel_id=1, source_target_pairs={{0,16},{2,18},{4,20},{6,22},{8,24},{10,26},{12,28},{14,30},{16,0},... | collective-permute-start | bytes 208904 | tf_op jit(solution)/shard_map/ppermute | solution.py:20
  55.5 2.4 %collective-permute-start.21 = (bf16[272,128]{1,0:T(8,128)(2,1)S(1)}, bf16[272,128]{1,0:T(8,128)(2,1)S(1)}, u32[]{:S(2)}, u32[]{:S(2)}) collective-permute-start(bf16[272,128]{1,0:T(8,128)(2,1)S(1)} %pad_maximum_fusion.1), channel_id=1, source_target_pairs={{0,24},{2,26},{4,28},{6,30},{8,16},{10,18},{12,20},{14,22},{16,8},... | collective-permute-start | bytes 208904 | tf_op jit(solution)/shard_map/ppermute | solution.py:20
  58.6 2.0 %collective-permute-done.20.refs_1_ = bf16[272,128]{1,0:T(8,128)(2,1)S(1)} collective-permute-done((bf16[272,128]{1,0:T(8,128)(2,1)S(1)}, bf16[272,128]{1,0:T(8,128)(2,1)S(1)}, u32[]{:S(2)}, u32[]{:S(2)}) %collective-permute-start.20) | collective-permute-done | bytes 69664 | tf_op jit(solution)/shard_map/ppermute | solution.py:20
  60.6 1.1 %collective-permute-done.21.refs_2_ = bf16[272,128]{1,0:T(8,128)(2,1)S(1)} collective-permute-done((bf16[272,128]{1,0:T(8,128)(2,1)S(1)}, bf16[272,128]{1,0:T(8,128)(2,1)S(1)}, u32[]{:S(2)}, u32[]{:S(2)}) %collective-permute-start.21) | collective-permute-done | bytes 69664 | tf_op jit(solution)/shard_map/ppermute | solution.py:20
  (55 shorter events, 9.3 us)
Async XLA Ops:
  0.6 16.3 %collective-permute-start = (bf16[8,128,128]{2,1,0:T(8,128)(2,1)}, bf16[8,128,128]{2,1,0:T(8,128)(2,1)S(1)}, u32[]{:S(2)}, u32[]{:S(2)}) collective-permute-start(bf16[8,128,128]{2,1,0:T(8,128)(2,1)} %bitcast.20), channel_id=1, source_target_pairs={{0,16},{2,18},{4,20},{6,22},{8,24},{10,26},{12,28},{14,30},{16,0},... | collective-permute-start | bytes 786440 | tf_op jit(solution)/shard_map/ppermute | solution.py:20
  4.7 13.0 %collective-permute-start.4 = (bf16[8,128,128]{2,1,0:T(8,128)(2,1)}, bf16[8,128,128]{2,1,0:T(8,128)(2,1)S(1)}, u32[]{:S(2)}, u32[]{:S(2)}) collective-permute-start(bf16[8,128,128]{2,1,0:T(8,128)(2,1)} %bitcast.21), channel_id=1, source_target_pairs={{0,8},{2,10},{4,12},{6,14},{8,0},{10,2},{12,4},{14,6},{16,24},{18,... | collective-permute-start | bytes 786440 | tf_op jit(solution)/shard_map/ppermute | solution.py:20
  6.3 26.2 %copy-start.3 = (s32[1,16,2]{1,2,0:T(2,128)S(1)}, s32[1,16,2]{1,2,0:T(2,128)}, u32[]{:S(2)}) copy-start(s32[1,16,2]{1,2,0:T(2,128)} %param.11) | copy-start | bytes 388
  6.3 26.2 %copy-start.4 = (s32[1,16,2]{1,2,0:T(2,128)S(1)}, s32[1,16,2]{1,2,0:T(2,128)}, u32[]{:S(2)}) copy-start(s32[1,16,2]{1,2,0:T(2,128)} %param.13) | copy-start | bytes 388
  6.3 6.5 %collective-permute-start.1 = (s32[2,16]{1,0:T(2,128)}, s32[2,16]{1,0:T(2,128)S(1)}, u32[]{:S(2)}, u32[]{:S(2)}) collective-permute-start(s32[2,16]{1,0:T(2,128)} %bitcast.29), channel_id=1, source_target_pairs={{0,2},{2,0},{4,6},{6,4},{8,10},{10,8},{12,14},{14,12},{16,18},{18,... | collective-permute-start | bytes 392 | tf_op jit(solution)/shard_map/ppermute | solution.py:20
  7.8 5.0 %collective-permute-start.2 = (s32[2,16]{1,0:T(2,128)}, s32[2,16]{1,0:T(2,128)S(1)}, u32[]{:S(2)}, u32[]{:S(2)}) collective-permute-start(s32[2,16]{1,0:T(2,128)} %bitcast.30), channel_id=1, source_target_pairs={{0,4},{2,6},{4,0},{6,2},{8,12},{10,14},{12,8},{14,10},{16,20},{18,... | collective-permute-start | bytes 392 | tf_op jit(solution)/shard_map/ppermute | solution.py:20
  9.3 4.7 %collective-permute-start.3 = (s32[2,16]{1,0:T(2,128)}, s32[2,16]{1,0:T(2,128)S(1)}, u32[]{:S(2)}, u32[]{:S(2)}) collective-permute-start(s32[2,16]{1,0:T(2,128)} %bitcast.31), channel_id=1, source_target_pairs={{0,6},{2,4},{4,2},{6,0},{8,14},{10,12},{12,10},{14,8},{16,22},{18,... | collective-permute-start | bytes 392 | tf_op jit(solution)/shard_map/ppermute | solution.py:20
  17.0 7.4 %collective-permute-start.8 = (bf16[8,128,128]{2,1,0:T(8,128)(2,1)S(1)}, bf16[8,128,128]{2,1,0:T(8,128)(2,1)S(1)}, u32[]{:S(2)}, u32[]{:S(2)}) collective-permute-start(bf16[8,128,128]{2,1,0:T(8,128)(2,1)S(1)} %collective-permute-done.refs_5_), channel_id=1, source_target_pairs={{0,8},{2,10},{4,12},{6,14},{8,0},{10,2},{12,4},{14,6},{16,24},{18,... | collective-permute-start | bytes 786440 | tf_op jit(solution)/shard_map/ppermute | solution.py:20
  18.3 9.5 %collective-permute-start.5 = (bf16[6,128,128]{2,1,0:T(8,128)(2,1)S(1)}, bf16[6,128,128]{2,1,0:T(8,128)(2,1)S(1)}, u32[]{:S(2)}, u32[]{:S(2)}) collective-permute-start(bf16[6,128,128]{2,1,0:T(8,128)(2,1)S(1)} %get-tuple-element.31), channel_id=1, source_target_pairs={{0,2},{2,0},{4,6},{6,4},{8,10},{10,8},{12,14},{14,12},{16,18},{18,... | collective-permute-start | bytes 589832 | tf_op jit(solution)/shard_map/ppermute | solution.py:20
  19.9 12.6 %collective-permute-start.6 = (bf16[6,128,128]{2,1,0:T(8,128)(2,1)S(1)}, bf16[6,128,128]{2,1,0:T(8,128)(2,1)S(1)}, u32[]{:S(2)}, u32[]{:S(2)}) collective-permute-start(bf16[6,128,128]{2,1,0:T(8,128)(2,1)S(1)} %get-tuple-element.32), channel_id=1, source_target_pairs={{0,4},{2,6},{4,0},{6,2},{8,12},{10,14},{12,8},{14,10},{16,20},{18,... | collective-permute-start | bytes 589832 | tf_op jit(solution)/shard_map/ppermute | solution.py:20
  21.4 11.1 %collective-permute-start.7 = (bf16[6,128,128]{2,1,0:T(8,128)(2,1)S(1)}, bf16[6,128,128]{2,1,0:T(8,128)(2,1)S(1)}, u32[]{:S(2)}, u32[]{:S(2)}) collective-permute-start(bf16[6,128,128]{2,1,0:T(8,128)(2,1)S(1)} %get-tuple-element.33), channel_id=1, source_target_pairs={{0,6},{2,4},{4,2},{6,0},{8,14},{10,12},{12,10},{14,8},{16,22},{18,... | collective-permute-start | bytes 589832 | tf_op jit(solution)/shard_map/ppermute | solution.py:20
  25.0 8.6 %collective-permute-start.10 = (bf16[2,128,128]{2,1,0:T(8,128)(2,1)S(1)}, bf16[2,128,128]{2,1,0:T(8,128)(2,1)S(1)}, u32[]{:S(2)}, u32[]{:S(2)}) collective-permute-start(bf16[2,128,128]{2,1,0:T(8,128)(2,1)S(1)} %get-tuple-element.36), channel_id=1, source_target_pairs={{0,4},{2,6},{4,0},{6,2},{8,12},{10,14},{12,8},{14,10},{16,20},{18,... | collective-permute-start | bytes 196616 | tf_op jit(solution)/shard_map/ppermute | solution.py:20
  26.4 7.2 %collective-permute-start.11 = (bf16[2,128,128]{2,1,0:T(8,128)(2,1)S(1)}, bf16[2,128,128]{2,1,0:T(8,128)(2,1)S(1)}, u32[]{:S(2)}, u32[]{:S(2)}) collective-permute-start(bf16[2,128,128]{2,1,0:T(8,128)(2,1)S(1)} %get-tuple-element.37), channel_id=1, source_target_pairs={{0,6},{2,4},{4,2},{6,0},{8,14},{10,12},{12,10},{14,8},{16,22},{18,... | collective-permute-start | bytes 196616 | tf_op jit(solution)/shard_map/ppermute | solution.py:20
  27.8 5.8 %collective-permute-start.9 = (bf16[2,128,128]{2,1,0:T(8,128)(2,1)S(1)}, bf16[2,128,128]{2,1,0:T(8,128)(2,1)S(1)}, u32[]{:S(2)}, u32[]{:S(2)}) collective-permute-start(bf16[2,128,128]{2,1,0:T(8,128)(2,1)S(1)} %get-tuple-element.35), channel_id=1, source_target_pairs={{0,2},{2,0},{4,6},{6,4},{8,10},{10,8},{12,14},{14,12},{16,18},{18,... | collective-permute-start | bytes 196616 | tf_op jit(solution)/shard_map/ppermute | solution.py:20
  34.5 9.4 %collective-permute-start.12 = (bf16[4,128,128]{2,1,0:T(8,128)(2,1)S(1)}, bf16[4,128,128]{2,1,0:T(8,128)(2,1)S(1)}, u32[]{:S(2)}, u32[]{:S(2)}) collective-permute-start(bf16[4,128,128]{2,1,0:T(8,128)(2,1)S(1)} %get-tuple-element.39), channel_id=1, source_target_pairs={{30,0},{0,2},{2,4},{4,6},{6,8},{8,10},{10,12},{12,14},{14,16},{16,... | collective-permute-start | bytes 393224 | tf_op jit(solution)/shard_map/ppermute | solution.py:25
  35.0 10.3 %collective-permute-start.14 = (bf16[4,128,128]{2,1,0:T(8,128)(2,1)S(1)}, bf16[4,128,128]{2,1,0:T(8,128)(2,1)S(1)}, u32[]{:S(2)}, u32[]{:S(2)}) collective-permute-start(bf16[4,128,128]{2,1,0:T(8,128)(2,1)S(1)} %get-tuple-element.41), channel_id=1, source_target_pairs={{30,0},{0,2},{2,4},{4,6},{6,8},{8,10},{10,12},{12,14},{14,16},{16,... | collective-permute-start | bytes 393224 | tf_op jit(solution)/shard_map/ppermute | solution.py:25
  43.9 1.4 %collective-permute-start.13 = (bf16[512,128]{1,0:T(8,128)(2,1)S(1)}, bf16[512,128]{1,0:T(8,128)(2,1)S(1)}, u32[]{:S(2)}, u32[]{:S(2)}) collective-permute-start(bf16[512,128]{1,0:T(8,128)(2,1)S(1)} %bitcast.25), channel_id=1, source_target_pairs={{1,0},{0,1},{3,2},{2,3},{5,4},{4,5},{7,6},{6,7},{9,8},{8,9},{11,10... | collective-permute-start | bytes 393224 | tf_op jit(solution)/shard_map/ppermute | solution.py:25
  45.3 1.4 %collective-permute-start.15 = (bf16[512,128]{1,0:T(8,128)(2,1)S(1)}, bf16[512,128]{1,0:T(8,128)(2,1)S(1)}, u32[]{:S(2)}, u32[]{:S(2)}) collective-permute-start(bf16[512,128]{1,0:T(8,128)(2,1)S(1)} %bitcast.27), channel_id=1, source_target_pairs={{1,0},{0,1},{3,2},{2,3},{5,4},{4,5},{7,6},{6,7},{9,8},{8,9},{11,10... | collective-permute-start | bytes 393224 | tf_op jit(solution)/shard_map/ppermute | solution.py:25
  47.3 4.8 %collective-permute-start.16 = (bf16[272,128]{1,0:T(8,128)(2,1)S(1)}, bf16[272,128]{1,0:T(8,128)(2,1)S(1)}, u32[]{:S(2)}, u32[]{:S(2)}) collective-permute-start(bf16[272,128]{1,0:T(8,128)(2,1)S(1)} %get-tuple-element.47), channel_id=1, source_target_pairs={{0,2},{2,0},{4,6},{6,4},{8,10},{10,8},{12,14},{14,12},{16,18},{18,... | collective-permute-start | bytes 208904 | tf_op jit(solution)/shard_map/ppermute | solution.py:20
  47.4 5.9 %collective-permute-start.17 = (bf16[272,128]{1,0:T(8,128)(2,1)S(1)}, bf16[272,128]{1,0:T(8,128)(2,1)S(1)}, u32[]{:S(2)}, u32[]{:S(2)}) collective-permute-start(bf16[272,128]{1,0:T(8,128)(2,1)S(1)} %get-tuple-element.47), channel_id=1, source_target_pairs={{0,4},{2,6},{4,0},{6,2},{8,12},{10,14},{12,8},{14,10},{16,20},{18,... | collective-permute-start | bytes 208904 | tf_op jit(solution)/shard_map/ppermute | solution.py:20
  47.5 5.8 %collective-permute-start.18 = (bf16[272,128]{1,0:T(8,128)(2,1)S(1)}, bf16[272,128]{1,0:T(8,128)(2,1)S(1)}, u32[]{:S(2)}, u32[]{:S(2)}) collective-permute-start(bf16[272,128]{1,0:T(8,128)(2,1)S(1)} %get-tuple-element.47), channel_id=1, source_target_pairs={{0,6},{2,4},{4,2},{6,0},{8,14},{10,12},{12,10},{14,8},{16,22},{18,... | collective-permute-start | bytes 208904 | tf_op jit(solution)/shard_map/ppermute | solution.py:20
  53.4 5.2 %collective-permute-start.19 = (bf16[272,128]{1,0:T(8,128)(2,1)S(1)}, bf16[272,128]{1,0:T(8,128)(2,1)S(1)}, u32[]{:S(2)}, u32[]{:S(2)}) collective-permute-start(bf16[272,128]{1,0:T(8,128)(2,1)S(1)} %pad_maximum_fusion.1), channel_id=1, source_target_pairs={{0,8},{2,10},{4,12},{6,14},{8,0},{10,2},{12,4},{14,6},{16,24},{18,... | collective-permute-start | bytes 208904 | tf_op jit(solution)/shard_map/ppermute | solution.py:20
  53.9 6.7 %collective-permute-start.20 = (bf16[272,128]{1,0:T(8,128)(2,1)S(1)}, bf16[272,128]{1,0:T(8,128)(2,1)S(1)}, u32[]{:S(2)}, u32[]{:S(2)}) collective-permute-start(bf16[272,128]{1,0:T(8,128)(2,1)S(1)} %pad_maximum_fusion.1), channel_id=1, source_target_pairs={{0,16},{2,18},{4,20},{6,22},{8,24},{10,26},{12,28},{14,30},{16,0},... | collective-permute-start | bytes 208904 | tf_op jit(solution)/shard_map/ppermute | solution.py:20
  55.5 6.2 %collective-permute-start.21 = (bf16[272,128]{1,0:T(8,128)(2,1)S(1)}, bf16[272,128]{1,0:T(8,128)(2,1)S(1)}, u32[]{:S(2)}, u32[]{:S(2)}) collective-permute-start(bf16[272,128]{1,0:T(8,128)(2,1)S(1)} %pad_maximum_fusion.1), channel_id=1, source_target_pairs={{0,24},{2,26},{4,28},{6,30},{8,16},{10,18},{12,20},{14,22},{16,8},... | collective-permute-start | bytes 208904 | tf_op jit(solution)/shard_map/ppermute | solution.py:20
  (5 other events, 79.2 us)

commit v7 on v6

--- a/solution.py
+++ b/solution.py
@@ -107,10 +107,8 @@
             dst = dst_ref[c, owner]
             acc[dst] = acc[dst] + product
     if last:
-        own_ref, *next_refs = refs[-2 - SLABS : -1]
-        at = own_ref.shape[0]
-        own_ref[...] = acc[:at]
-        for next_ref in next_refs:
+        at = acc.shape[0] // 2
+        for next_ref in refs[-1 - SLABS : -1]:
             depth = next_ref.shape[0]
             next_ref[...] = acc[at : at + depth].astype(next_ref.dtype)
             at += depth
@@ -118,7 +116,6 @@
 
 def tile_sum(shared, acc, sources, cap, last=False):
     row_count, size, width = acc.shape
-    half = (row_count // 2, size, width)
     part = (row_count // 2 // SLABS, size, width)
     arrays, places = [], []
     for bits, array, start in sources:
@@ -127,18 +124,14 @@
             known = [len(arrays)]
             arrays.append(array)
         places.append((bits, known[0], start))
-    scratch = []
     out_shape = [jax.ShapeDtypeStruct(acc.shape, jnp.float32)]
     if last:
-        out_shape = [jax.ShapeDtypeStruct(half, jnp.float32)]
-        out_shape += [jax.ShapeDtypeStruct(part, jnp.bfloat16)] * SLABS
-        scratch = [pltpu.VMEM(acc.shape, jnp.float32)]
+        out_shape = [jax.ShapeDtypeStruct(part, jnp.bfloat16)] * SLABS + out_shape
     return pl.pallas_call(
         functools.partial(sum_kernel, places, cap, last),
         out_shape=out_shape,
         in_specs=[SMEM] * 3 + [VMEM] * (2 + len(arrays)),
         out_specs=[VMEM] * len(out_shape),
-        scratch_shapes=scratch,
         compiler_params=PARAMS,
     )(*shared, acc, *arrays)
 
@@ -325,7 +318,7 @@
     rest = exchange([columns - 1])
     (acc,) = tile_sum(shared, acc, first, cap)
     outs = tile_sum(shared, acc, rest, cap, last=True)
-    own, *following = outs
+    *following, own = outs
     incoming = [passed_along(part, "dom", 1) for part in following]
 
     feat = lax.axis_index("feat").astype(jnp.int32).reshape(1)

time: 62.5 us -> 62.5 us (level)
  no operation moved by 1% of the time
where the time goes in v7:
time: 62.5 us; the launch traced here: 62.3 us
  starting transfers between devices  28.3 us (45%)
  waiting for transfers between devices  24.2 us (39%)
  Pallas kernels  7.94 us (13%)
  between operations  0.9 us (1%)
  other arithmetic  0.88 us (1%)
    ppermute x18, starting transfers between devices, partner(): return lax.ppermute(block, 'dom', [(i, i ^ bits) for i in range(count)])  25 us
    ppermute x18, waiting for transfers between devices, partner(): return lax.ppermute(block, 'dom', [(i, i ^ bits) for i in range(count)])  16 us
    ppermute x4, waiting for transfers between devices, passed_along(): lax.ppermute(block, axis, [((i - distance) % count, i) for i in range(cou...  8.23 us
    ppermute x4, starting transfers between devices, passed_along(): lax.ppermute(block, axis, [((i - distance) % count, i) for i in range(cou...  3.32 us
    pallas_call x1, Pallas kernels, begin_sum(): pl.pallas_call(functools.partial(begin_kernel, chunks), out_shape=[jax.Sh...  3.01 us
    pallas_call x2, Pallas kernels, tile_sum(): pl.pallas_call(functools.partial(sum_kernel, places, cap, last), out_shap...  1.88 us
  transfers between devices with their start and end apart: 22, of which 11 were waited for; matrix products, arithmetic and copies ran while one was open for 1% of the time, Pallas kernels for 9%

profile of v7, /device:TPU:0, one launch (start us, length us, event | category | flops | bytes accessed | tf_op | source)
XLA Modules:
  0.0 62.3 jit_solution(10312252245300222129)
XLA Ops:
  0.6 4.1 %collective-permute-start = (bf16[8,128,128]{2,1,0:T(8,128)(2,1)}, bf16[8,128,128]{2,1,0:T(8,128)(2,1)S(1)}, u32[]{:S(2)}, u32[]{:S(2)}) collective-permute-start(bf16[8,128,128]{2,1,0:T(8,128)(2,1)} %bitcast.20), channel_id=1, source_target_pairs={{0,16},{2,18},{4,20},{6,22},{8,24},{10,26},{12,28},{14,30},{16,0},... | collective-permute-start | bytes 786440 | tf_op jit(solution)/shard_map/ppermute | solution.py:20
  4.7 1.6 %collective-permute-start.4 = (bf16[8,128,128]{2,1,0:T(8,128)(2,1)}, bf16[8,128,128]{2,1,0:T(8,128)(2,1)S(1)}, u32[]{:S(2)}, u32[]{:S(2)}) collective-permute-start(bf16[8,128,128]{2,1,0:T(8,128)(2,1)} %bitcast.21), channel_id=1, source_target_pairs={{0,8},{2,10},{4,12},{6,14},{8,0},{10,2},{12,4},{14,6},{16,24},{18,... | collective-permute-start | bytes 786440 | tf_op jit(solution)/shard_map/ppermute | solution.py:20
  6.3 1.5 %collective-permute-start.1 = (s32[2,16]{1,0:T(2,128)}, s32[2,16]{1,0:T(2,128)S(1)}, u32[]{:S(2)}, u32[]{:S(2)}) collective-permute-start(s32[2,16]{1,0:T(2,128)} %bitcast.29), channel_id=1, source_target_pairs={{0,2},{2,0},{4,6},{6,4},{8,10},{10,8},{12,14},{14,12},{16,18},{18,... | collective-permute-start | bytes 392 | tf_op jit(solution)/shard_map/ppermute | solution.py:20
  7.8 1.5 %collective-permute-start.2 = (s32[2,16]{1,0:T(2,128)}, s32[2,16]{1,0:T(2,128)S(1)}, u32[]{:S(2)}, u32[]{:S(2)}) collective-permute-start(s32[2,16]{1,0:T(2,128)} %bitcast.30), channel_id=1, source_target_pairs={{0,4},{2,6},{4,0},{6,2},{8,12},{10,14},{12,8},{14,10},{16,20},{18,... | collective-permute-start | bytes 392 | tf_op jit(solution)/shard_map/ppermute | solution.py:20
  9.8 3.0 %shard_map.121.acc_in = f32[16,128,128]{2,1,0:T(8,128)S(1)} custom-call(s32[1,64]{1,0:T(1,128)} %refs_0_.1, s32[1,64]{1,0:T(1,128)} %refs_1_.1, bf16[8,128,128]{2,1,0:T(8,128)(2,1)} %bitcast.22, bf16[64,128,128]{2,1,0:T(8,128)(2,1)} %refs_3_.1), custom_call_target="tpu_custom_call" | custom-call | tf_op jit(solution)/shard_map/pallas_call | solution.py:79
  12.9 1.2 %collective-permute-done.3.refs_2_ = s32[2,16]{1,0:T(2,128)S(1)} collective-permute-done((s32[2,16]{1,0:T(2,128)}, s32[2,16]{1,0:T(2,128)S(1)}, u32[]{:S(2)}, u32[]{:S(2)}) %collective-permute-start.3) | collective-permute-done | bytes 160 | tf_op jit(solution)/shard_map/ppermute | solution.py:20
  14.0 3.0 %collective-permute-done.refs_5_ = bf16[8,128,128]{2,1,0:T(8,128)(2,1)S(1)} collective-permute-done((bf16[8,128,128]{2,1,0:T(8,128)(2,1)}, bf16[8,128,128]{2,1,0:T(8,128)(2,1)S(1)}, u32[]{:S(2)}, u32[]{:S(2)}) %collective-permute-start) | collective-permute-done | bytes 262176 | tf_op jit(solution)/shard_map/ppermute | solution.py:20
  18.3 1.6 %collective-permute-start.5 = (bf16[6,128,128]{2,1,0:T(8,128)(2,1)S(1)}, bf16[6,128,128]{2,1,0:T(8,128)(2,1)S(1)}, u32[]{:S(2)}, u32[]{:S(2)}) collective-permute-start(bf16[6,128,128]{2,1,0:T(8,128)(2,1)S(1)} %get-tuple-element.31), channel_id=1, source_target_pairs={{0,2},{2,0},{4,6},{6,4},{8,10},{10,8},{12,14},{14,12},{16,18},{18,... | collective-permute-start | bytes 589832 | tf_op jit(solution)/shard_map/ppermute | solution.py:20
  19.9 1.5 %collective-permute-start.6 = (bf16[6,128,128]{2,1,0:T(8,128)(2,1)S(1)}, bf16[6,128,128]{2,1,0:T(8,128)(2,1)S(1)}, u32[]{:S(2)}, u32[]{:S(2)}) collective-permute-start(bf16[6,128,128]{2,1,0:T(8,128)(2,1)S(1)} %get-tuple-element.32), channel_id=1, source_target_pairs={{0,4},{2,6},{4,0},{6,2},{8,12},{10,14},{12,8},{14,10},{16,20},{18,... | collective-permute-start | bytes 589832 | tf_op jit(solution)/shard_map/ppermute | solution.py:20
  21.9 2.5 %collective-permute-done.8.refs_3_.refs_0_ = bf16[8,128,128]{2,1,0:T(8,128)(2,1)S(1)} collective-permute-done((bf16[8,128,128]{2,1,0:T(8,128)(2,1)S(1)}, bf16[8,128,128]{2,1,0:T(8,128)(2,1)S(1)}, u32[]{:S(2)}, u32[]{:S(2)}) %collective-permute-start.8) | collective-permute-done | bytes 262176 | tf_op jit(solution)/shard_map/ppermute | solution.py:20
  25.0 1.4 %collective-permute-start.10 = (bf16[2,128,128]{2,1,0:T(8,128)(2,1)S(1)}, bf16[2,128,128]{2,1,0:T(8,128)(2,1)S(1)}, u32[]{:S(2)}, u32[]{:S(2)}) collective-permute-start(bf16[2,128,128]{2,1,0:T(8,128)(2,1)S(1)} %get-tuple-element.36), channel_id=1, source_target_pairs={{0,4},{2,6},{4,0},{6,2},{8,12},{10,14},{12,8},{14,10},{16,20},{18,... | collective-permute-start | bytes 196616 | tf_op jit(solution)/shard_map/ppermute | solution.py:20
  26.4 1.4 %collective-permute-start.11 = (bf16[2,128,128]{2,1,0:T(8,128)(2,1)S(1)}, bf16[2,128,128]{2,1,0:T(8,128)(2,1)S(1)}, u32[]{:S(2)}, u32[]{:S(2)}) collective-permute-start(bf16[2,128,128]{2,1,0:T(8,128)(2,1)S(1)} %get-tuple-element.37), channel_id=1, source_target_pairs={{0,6},{2,4},{4,2},{6,0},{8,14},{10,12},{12,10},{14,8},{16,22},{18,... | collective-permute-start | bytes 196616 | tf_op jit(solution)/shard_map/ppermute | solution.py:20
  28.6 3.9 %collective-permute-done.6.refs_2_ = bf16[6,128,128]{2,1,0:T(8,128)(2,1)S(1)} collective-permute-done((bf16[6,128,128]{2,1,0:T(8,128)(2,1)S(1)}, bf16[6,128,128]{2,1,0:T(8,128)(2,1)S(1)}, u32[]{:S(2)}, u32[]{:S(2)}) %collective-permute-start.6) | collective-permute-done | bytes 196640 | tf_op jit(solution)/shard_map/ppermute | solution.py:20
  32.5 1.0 %shard_map.123.acc_in = f32[16,128,128]{2,1,0:T(8,128)S(1)} custom-call(s32[1]{0:T(128)} %bitcast.me_ref, s32[2,16]{1,0:T(2,128)S(1)} %bitcast.32, s32[2,16]{1,0:T(2,128)S(1)} %bitcast.34, bf16[32,128,128]{2,1,0:T(8,128)(2,1)S(1)} %bitcast.18, f32[16,128,128]{2,1,0:T(8,128)S(1)} %shard_map.121.acc_in, bf16[8,128,128]{2,1,0:T(8,128)(2,1)S(1)} %bitcast.24, ...), custom_call_target="tpu_custom_call" | custom-call | tf_op jit(solution)/shard_map/pallas_call | solution.py:130
  34.9 2.6 %collective-permute-start.14 = (bf16[4,128,128]{2,1,0:T(8,128)(2,1)S(1)}, bf16[4,128,128]{2,1,0:T(8,128)(2,1)S(1)}, u32[]{:S(2)}, u32[]{:S(2)}) collective-permute-start(bf16[4,128,128]{2,1,0:T(8,128)(2,1)S(1)} %get-tuple-element.41), channel_id=1, source_target_pairs={{30,0},{0,2},{2,4},{4,6},{6,8},{8,10},{10,12},{12,14},{14,16},{16,... | collective-permute-start | bytes 393224 | tf_op jit(solution)/shard_map/ppermute | solution.py:25
  37.5 6.3 %collective-permute-done.12 = bf16[4,128,128]{2,1,0:T(8,128)(2,1)S(1)} collective-permute-done((bf16[4,128,128]{2,1,0:T(8,128)(2,1)S(1)}, bf16[4,128,128]{2,1,0:T(8,128)(2,1)S(1)}, u32[]{:S(2)}, u32[]{:S(2)}) %collective-permute-start.12) | collective-permute-done | bytes 131104 | tf_op jit(solution)/shard_map/ppermute | solution.py:25
  43.9 1.3 %collective-permute-done.14 = bf16[4,128,128]{2,1,0:T(8,128)(2,1)S(1)} collective-permute-done((bf16[4,128,128]{2,1,0:T(8,128)(2,1)S(1)}, bf16[4,128,128]{2,1,0:T(8,128)(2,1)S(1)}, u32[]{:S(2)}, u32[]{:S(2)}) %collective-permute-start.14) | collective-permute-done | bytes 131104 | tf_op jit(solution)/shard_map/ppermute | solution.py:25
  47.4 3.4 %collective-permute-start.18 = (bf16[272,128]{1,0:T(8,128)(2,1)S(1)}, bf16[272,128]{1,0:T(8,128)(2,1)S(1)}, u32[]{:S(2)}, u32[]{:S(2)}) collective-permute-start(bf16[272,128]{1,0:T(8,128)(2,1)S(1)} %get-tuple-element.47), channel_id=1, source_target_pairs={{0,6},{2,4},{4,2},{6,0},{8,14},{10,12},{12,10},{14,8},{16,22},{18,... | collective-permute-start | bytes 208904 | tf_op jit(solution)/shard_map/ppermute | solution.py:20
  50.8 1.2 %collective-permute-done.16 = bf16[272,128]{1,0:T(8,128)(2,1)S(1)} collective-permute-done((bf16[272,128]{1,0:T(8,128)(2,1)S(1)}, bf16[272,128]{1,0:T(8,128)(2,1)S(1)}, u32[]{:S(2)}, u32[]{:S(2)}) %collective-permute-start.16) | collective-permute-done | bytes 69664 | tf_op jit(solution)/shard_map/ppermute | solution.py:20
  52.0 1.2 %collective-permute-done.17 = bf16[272,128]{1,0:T(8,128)(2,1)S(1)} collective-permute-done((bf16[272,128]{1,0:T(8,128)(2,1)S(1)}, bf16[272,128]{1,0:T(8,128)(2,1)S(1)}, u32[]{:S(2)}, u32[]{:S(2)}) %collective-permute-start.17) | collective-permute-done | bytes 69664 | tf_op jit(solution)/shard_map/ppermute | solution.py:20
  53.9 1.6 %collective-permute-start.20 = (bf16[272,128]{1,0:T(8,128)(2,1)S(1)}, bf16[272,128]{1,0:T(8,128)(2,1)S(1)}, u32[]{:S(2)}, u32[]{:S(2)}) collective-permute-start(bf16[272,128]{1,0:T(8,128)(2,1)S(1)} %pad_maximum_fusion.1), channel_id=1, source_target_pairs={{0,16},{2,18},{4,20},{6,22},{8,24},{10,26},{12,28},{14,30},{16,0},... | collective-permute-start | bytes 208904 | tf_op jit(solution)/shard_map/ppermute | solution.py:20
  55.4 2.4 %collective-permute-start.21 = (bf16[272,128]{1,0:T(8,128)(2,1)S(1)}, bf16[272,128]{1,0:T(8,128)(2,1)S(1)}, u32[]{:S(2)}, u32[]{:S(2)}) collective-permute-start(bf16[272,128]{1,0:T(8,128)(2,1)S(1)} %pad_maximum_fusion.1), channel_id=1, source_target_pairs={{0,24},{2,26},{4,28},{6,30},{8,16},{10,18},{12,20},{14,22},{16,8},... | collective-permute-start | bytes 208904 | tf_op jit(solution)/shard_map/ppermute | solution.py:20
  58.5 2.0 %collective-permute-done.20.refs_1_ = bf16[272,128]{1,0:T(8,128)(2,1)S(1)} collective-permute-done((bf16[272,128]{1,0:T(8,128)(2,1)S(1)}, bf16[272,128]{1,0:T(8,128)(2,1)S(1)}, u32[]{:S(2)}, u32[]{:S(2)}) %collective-permute-start.20) | collective-permute-done | bytes 69664 | tf_op jit(solution)/shard_map/ppermute | solution.py:20
  60.5 1.1 %collective-permute-done.21.refs_2_ = bf16[272,128]{1,0:T(8,128)(2,1)S(1)} collective-permute-done((bf16[272,128]{1,0:T(8,128)(2,1)S(1)}, bf16[272,128]{1,0:T(8,128)(2,1)S(1)}, u32[]{:S(2)}, u32[]{:S(2)}) %collective-permute-start.21) | collective-permute-done | bytes 69664 | tf_op jit(solution)/shard_map/ppermute | solution.py:20
  (55 shorter events, 9.3 us)
Async XLA Ops:
  0.6 16.3 %collective-permute-start = (bf16[8,128,128]{2,1,0:T(8,128)(2,1)}, bf16[8,128,128]{2,1,0:T(8,128)(2,1)S(1)}, u32[]{:S(2)}, u32[]{:S(2)}) collective-permute-start(bf16[8,128,128]{2,1,0:T(8,128)(2,1)} %bitcast.20), channel_id=1, source_target_pairs={{0,16},{2,18},{4,20},{6,22},{8,24},{10,26},{12,28},{14,30},{16,0},... | collective-permute-start | bytes 786440 | tf_op jit(solution)/shard_map/ppermute | solution.py:20
  4.7 13.0 %collective-permute-start.4 = (bf16[8,128,128]{2,1,0:T(8,128)(2,1)}, bf16[8,128,128]{2,1,0:T(8,128)(2,1)S(1)}, u32[]{:S(2)}, u32[]{:S(2)}) collective-permute-start(bf16[8,128,128]{2,1,0:T(8,128)(2,1)} %bitcast.21), channel_id=1, source_target_pairs={{0,8},{2,10},{4,12},{6,14},{8,0},{10,2},{12,4},{14,6},{16,24},{18,... | collective-permute-start | bytes 786440 | tf_op jit(solution)/shard_map/ppermute | solution.py:20
  6.3 26.2 %copy-start.3 = (s32[1,16,2]{1,2,0:T(2,128)S(1)}, s32[1,16,2]{1,2,0:T(2,128)}, u32[]{:S(2)}) copy-start(s32[1,16,2]{1,2,0:T(2,128)} %param.11) | copy-start | bytes 388
  6.3 26.2 %copy-start.4 = (s32[1,16,2]{1,2,0:T(2,128)S(1)}, s32[1,16,2]{1,2,0:T(2,128)}, u32[]{:S(2)}) copy-start(s32[1,16,2]{1,2,0:T(2,128)} %param.13) | copy-start | bytes 388
  6.3 6.5 %collective-permute-start.1 = (s32[2,16]{1,0:T(2,128)}, s32[2,16]{1,0:T(2,128)S(1)}, u32[]{:S(2)}, u32[]{:S(2)}) collective-permute-start(s32[2,16]{1,0:T(2,128)} %bitcast.29), channel_id=1, source_target_pairs={{0,2},{2,0},{4,6},{6,4},{8,10},{10,8},{12,14},{14,12},{16,18},{18,... | collective-permute-start | bytes 392 | tf_op jit(solution)/shard_map/ppermute | solution.py:20
  7.8 5.0 %collective-permute-start.2 = (s32[2,16]{1,0:T(2,128)}, s32[2,16]{1,0:T(2,128)S(1)}, u32[]{:S(2)}, u32[]{:S(2)}) collective-permute-start(s32[2,16]{1,0:T(2,128)} %bitcast.30), channel_id=1, source_target_pairs={{0,4},{2,6},{4,0},{6,2},{8,12},{10,14},{12,8},{14,10},{16,20},{18,... | collective-permute-start | bytes 392 | tf_op jit(solution)/shard_map/ppermute | solution.py:20
  9.3 4.7 %collective-permute-start.3 = (s32[2,16]{1,0:T(2,128)}, s32[2,16]{1,0:T(2,128)S(1)}, u32[]{:S(2)}, u32[]{:S(2)}) collective-permute-start(s32[2,16]{1,0:T(2,128)} %bitcast.31), channel_id=1, source_target_pairs={{0,6},{2,4},{4,2},{6,0},{8,14},{10,12},{12,10},{14,8},{16,22},{18,... | collective-permute-start | bytes 392 | tf_op jit(solution)/shard_map/ppermute | solution.py:20
  17.0 7.4 %collective-permute-start.8 = (bf16[8,128,128]{2,1,0:T(8,128)(2,1)S(1)}, bf16[8,128,128]{2,1,0:T(8,128)(2,1)S(1)}, u32[]{:S(2)}, u32[]{:S(2)}) collective-permute-start(bf16[8,128,128]{2,1,0:T(8,128)(2,1)S(1)} %collective-permute-done.refs_5_), channel_id=1, source_target_pairs={{0,8},{2,10},{4,12},{6,14},{8,0},{10,2},{12,4},{14,6},{16,24},{18,... | collective-permute-start | bytes 786440 | tf_op jit(solution)/shard_map/ppermute | solution.py:20
  18.3 9.5 %collective-permute-start.5 = (bf16[6,128,128]{2,1,0:T(8,128)(2,1)S(1)}, bf16[6,128,128]{2,1,0:T(8,128)(2,1)S(1)}, u32[]{:S(2)}, u32[]{:S(2)}) collective-permute-start(bf16[6,128,128]{2,1,0:T(8,128)(2,1)S(1)} %get-tuple-element.31), channel_id=1, source_target_pairs={{0,2},{2,0},{4,6},{6,4},{8,10},{10,8},{12,14},{14,12},{16,18},{18,... | collective-permute-start | bytes 589832 | tf_op jit(solution)/shard_map/ppermute | solution.py:20
  19.9 12.6 %collective-permute-start.6 = (bf16[6,128,128]{2,1,0:T(8,128)(2,1)S(1)}, bf16[6,128,128]{2,1,0:T(8,128)(2,1)S(1)}, u32[]{:S(2)}, u32[]{:S(2)}) collective-permute-start(bf16[6,128,128]{2,1,0:T(8,128)(2,1)S(1)} %get-tuple-element.32), channel_id=1, source_target_pairs={{0,4},{2,6},{4,0},{6,2},{8,12},{10,14},{12,8},{14,10},{16,20},{18,... | collective-permute-start | bytes 589832 | tf_op jit(solution)/shard_map/ppermute | solution.py:20
  21.4 11.1 %collective-permute-start.7 = (bf16[6,128,128]{2,1,0:T(8,128)(2,1)S(1)}, bf16[6,128,128]{2,1,0:T(8,128)(2,1)S(1)}, u32[]{:S(2)}, u32[]{:S(2)}) collective-permute-start(bf16[6,128,128]{2,1,0:T(8,128)(2,1)S(1)} %get-tuple-element.33), channel_id=1, source_target_pairs={{0,6},{2,4},{4,2},{6,0},{8,14},{10,12},{12,10},{14,8},{16,22},{18,... | collective-permute-start | bytes 589832 | tf_op jit(solution)/shard_map/ppermute | solution.py:20
  25.0 8.6 %collective-permute-start.10 = (bf16[2,128,128]{2,1,0:T(8,128)(2,1)S(1)}, bf16[2,128,128]{2,1,0:T(8,128)(2,1)S(1)}, u32[]{:S(2)}, u32[]{:S(2)}) collective-permute-start(bf16[2,128,128]{2,1,0:T(8,128)(2,1)S(1)} %get-tuple-element.36), channel_id=1, source_target_pairs={{0,4},{2,6},{4,0},{6,2},{8,12},{10,14},{12,8},{14,10},{16,20},{18,... | collective-permute-start | bytes 196616 | tf_op jit(solution)/shard_map/ppermute | solution.py:20
  26.4 7.2 %collective-permute-start.11 = (bf16[2,128,128]{2,1,0:T(8,128)(2,1)S(1)}, bf16[2,128,128]{2,1,0:T(8,128)(2,1)S(1)}, u32[]{:S(2)}, u32[]{:S(2)}) collective-permute-start(bf16[2,128,128]{2,1,0:T(8,128)(2,1)S(1)} %get-tuple-element.37), channel_id=1, source_target_pairs={{0,6},{2,4},{4,2},{6,0},{8,14},{10,12},{12,10},{14,8},{16,22},{18,... | collective-permute-start | bytes 196616 | tf_op jit(solution)/shard_map/ppermute | solution.py:20
  27.8 5.8 %collective-permute-start.9 = (bf16[2,128,128]{2,1,0:T(8,128)(2,1)S(1)}, bf16[2,128,128]{2,1,0:T(8,128)(2,1)S(1)}, u32[]{:S(2)}, u32[]{:S(2)}) collective-permute-start(bf16[2,128,128]{2,1,0:T(8,128)(2,1)S(1)} %get-tuple-element.35), channel_id=1, source_target_pairs={{0,2},{2,0},{4,6},{6,4},{8,10},{10,8},{12,14},{14,12},{16,18},{18,... | collective-permute-start | bytes 196616 | tf_op jit(solution)/shard_map/ppermute | solution.py:20
  34.5 9.3 %collective-permute-start.12 = (bf16[4,128,128]{2,1,0:T(8,128)(2,1)S(1)}, bf16[4,128,128]{2,1,0:T(8,128)(2,1)S(1)}, u32[]{:S(2)}, u32[]{:S(2)}) collective-permute-start(bf16[4,128,128]{2,1,0:T(8,128)(2,1)S(1)} %get-tuple-element.39), channel_id=1, source_target_pairs={{30,0},{0,2},{2,4},{4,6},{6,8},{8,10},{10,12},{12,14},{14,16},{16,... | collective-permute-start | bytes 393224 | tf_op jit(solution)/shard_map/ppermute | solution.py:25
  34.9 10.3 %collective-permute-start.14 = (bf16[4,128,128]{2,1,0:T(8,128)(2,1)S(1)}, bf16[4,128,128]{2,1,0:T(8,128)(2,1)S(1)}, u32[]{:S(2)}, u32[]{:S(2)}) collective-permute-start(bf16[4,128,128]{2,1,0:T(8,128)(2,1)S(1)} %get-tuple-element.41), channel_id=1, source_target_pairs={{30,0},{0,2},{2,4},{4,6},{6,8},{8,10},{10,12},{12,14},{14,16},{16,... | collective-permute-start | bytes 393224 | tf_op jit(solution)/shard_map/ppermute | solution.py:25
  43.8 1.4 %collective-permute-start.13 = (bf16[512,128]{1,0:T(8,128)(2,1)S(1)}, bf16[512,128]{1,0:T(8,128)(2,1)S(1)}, u32[]{:S(2)}, u32[]{:S(2)}) collective-permute-start(bf16[512,128]{1,0:T(8,128)(2,1)S(1)} %bitcast.25), channel_id=1, source_target_pairs={{1,0},{0,1},{3,2},{2,3},{5,4},{4,5},{7,6},{6,7},{9,8},{8,9},{11,10... | collective-permute-start | bytes 393224 | tf_op jit(solution)/shard_map/ppermute | solution.py:25
  45.3 1.4 %collective-permute-start.15 = (bf16[512,128]{1,0:T(8,128)(2,1)S(1)}, bf16[512,128]{1,0:T(8,128)(2,1)S(1)}, u32[]{:S(2)}, u32[]{:S(2)}) collective-permute-start(bf16[512,128]{1,0:T(8,128)(2,1)S(1)} %bitcast.27), channel_id=1, source_target_pairs={{1,0},{0,1},{3,2},{2,3},{5,4},{4,5},{7,6},{6,7},{9,8},{8,9},{11,10... | collective-permute-start | bytes 393224 | tf_op jit(solution)/shard_map/ppermute | solution.py:25
  47.3 4.8 %collective-permute-start.16 = (bf16[272,128]{1,0:T(8,128)(2,1)S(1)}, bf16[272,128]{1,0:T(8,128)(2,1)S(1)}, u32[]{:S(2)}, u32[]{:S(2)}) collective-permute-start(bf16[272,128]{1,0:T(8,128)(2,1)S(1)} %get-tuple-element.47), channel_id=1, source_target_pairs={{0,2},{2,0},{4,6},{6,4},{8,10},{10,8},{12,14},{14,12},{16,18},{18,... | collective-permute-start | bytes 208904 | tf_op jit(solution)/shard_map/ppermute | solution.py:20
  47.3 5.9 %collective-permute-start.17 = (bf16[272,128]{1,0:T(8,128)(2,1)S(1)}, bf16[272,128]{1,0:T(8,128)(2,1)S(1)}, u32[]{:S(2)}, u32[]{:S(2)}) collective-permute-start(bf16[272,128]{1,0:T(8,128)(2,1)S(1)} %get-tuple-element.47), channel_id=1, source_target_pairs={{0,4},{2,6},{4,0},{6,2},{8,12},{10,14},{12,8},{14,10},{16,20},{18,... | collective-permute-start | bytes 208904 | tf_op jit(solution)/shard_map/ppermute | solution.py:20
  47.4 5.8 %collective-permute-start.18 = (bf16[272,128]{1,0:T(8,128)(2,1)S(1)}, bf16[272,128]{1,0:T(8,128)(2,1)S(1)}, u32[]{:S(2)}, u32[]{:S(2)}) collective-permute-start(bf16[272,128]{1,0:T(8,128)(2,1)S(1)} %get-tuple-element.47), channel_id=1, source_target_pairs={{0,6},{2,4},{4,2},{6,0},{8,14},{10,12},{12,10},{14,8},{16,22},{18,... | collective-permute-start | bytes 208904 | tf_op jit(solution)/shard_map/ppermute | solution.py:20
  53.4 5.2 %collective-permute-start.19 = (bf16[272,128]{1,0:T(8,128)(2,1)S(1)}, bf16[272,128]{1,0:T(8,128)(2,1)S(1)}, u32[]{:S(2)}, u32[]{:S(2)}) collective-permute-start(bf16[272,128]{1,0:T(8,128)(2,1)S(1)} %pad_maximum_fusion.1), channel_id=1, source_target_pairs={{0,8},{2,10},{4,12},{6,14},{8,0},{10,2},{12,4},{14,6},{16,24},{18,... | collective-permute-start | bytes 208904 | tf_op jit(solution)/shard_map/ppermute | solution.py:20
  53.9 6.7 %collective-permute-start.20 = (bf16[272,128]{1,0:T(8,128)(2,1)S(1)}, bf16[272,128]{1,0:T(8,128)(2,1)S(1)}, u32[]{:S(2)}, u32[]{:S(2)}) collective-permute-start(bf16[272,128]{1,0:T(8,128)(2,1)S(1)} %pad_maximum_fusion.1), channel_id=1, source_target_pairs={{0,16},{2,18},{4,20},{6,22},{8,24},{10,26},{12,28},{14,30},{16,0},... | collective-permute-start | bytes 208904 | tf_op jit(solution)/shard_map/ppermute | solution.py:20
  55.4 6.2 %collective-permute-start.21 = (bf16[272,128]{1,0:T(8,128)(2,1)S(1)}, bf16[272,128]{1,0:T(8,128)(2,1)S(1)}, u32[]{:S(2)}, u32[]{:S(2)}) collective-permute-start(bf16[272,128]{1,0:T(8,128)(2,1)S(1)} %pad_maximum_fusion.1), channel_id=1, source_target_pairs={{0,24},{2,26},{4,28},{6,30},{8,16},{10,18},{12,20},{14,22},{16,8},... | collective-permute-start | bytes 208904 | tf_op jit(solution)/shard_map/ppermute | solution.py:20
  (5 other events, 79.1 us)
